TPU v7x, 512 devices: a whole 4x4x16 slice. The times are simulated.
512 devices in a mesh: group: 16 (over z), dev: 32 (over x, y, core).
Axes of the slice: x: 4, y: 4, z: 16, core: 2. Of those that a mesh axis runs over, the one named last changes fastest.
Arguments:
- positions: float32 [3, 16384, 256], P(None, ('group', 'dev')), may hold values from -3 to 3
- velocities: float32 [3, 16384, 256], P(None, ('group', 'dev')), may hold values from -3 to 3
- masses: float32 [16384, 256], P(('group', 'dev')), may hold values from 0.005 to 0.05
- counts: int32 [16384], P(('group', 'dev')), may hold values from 64 to 256, as said below
- walls: int32 [16384, 256], P(('group', 'dev')), may hold values 0 or 1
- neighbours: int32 [16384, 3], P(('group', 'dev')), may hold values from 0 to 103, as said below
- send_cells: int32 [16, 32, 32, 2], P('group', 'dev'), may hold values from -1 to 31, as said below
- owners: int32 [16, 1024], P('group'), may hold values from 0 to 31, as said below
Outputs:
- new_state: float32 [6, 16384, 256], P(None, ('group', 'dev'))
- new_density: float32 [16384, 256], P(('group', 'dev'))
Inputs may be any that keep to these rules, and one draw needn't show every extreme that they name: `counts`: every device holds at least one cell with 256 particles. `send_cells`: A device never sends to itself; slot 0 to every other device of its group holds a cell. `neighbours`: A cell never names its own row; on each device every rim row and every filled incoming slot is named at least once, and no empty incoming slot is named. `owners`: each device of a group owns exactly 32 cells afterwards; each device keeps 32 - 8 * 2 of its cells and hands exactly 2 cells to each of 8 other devices of its group, and none to the rest.
All inputs are finite; a program needn't handle non-finite values. No bound on the sum of `walls` on one device may be relied on, other than what follows from the above.
Results may differ from a plain program's by a relative error of at most 0.0003.
Values sent between devices are 32-bit elements; how exact they have to be, the bound alone decides.
No kernel may reach another device: no remote copies, remote signals or barrier semaphores. Data moves between devices by JAX's collectives and lax.ppermute only.
A program may use at most 64 MiB of HBM per device.

v0:
```python
import jax
import jax.numpy as jnp
from jax import lax
from jax.sharding import PartitionSpec as P

RIM_CELLS = 4


SUPPORT = 4.0
STIFFNESS = 2.0
REST_DENSITY = 0.8
VISCOSITY = 0.5
COHESION = 0.3
ADHESION = 0.8
GRAVITY = 1.0
TIME_STEP = 0.5


def with_halo(cells, sides, width):
    for axis, dim in sides:
        count = lax.axis_size(axis)
        ends = count - 1
        head = lax.slice_in_dim(cells, 0, width, axis=dim)
        tail = lax.slice_in_dim(cells, cells.shape[dim] - width, cells.shape[dim], axis=dim)
        cells = jnp.concatenate(
            [
                lax.ppermute(tail, axis, [(i, (i + 1) % count) for i in range(ends)]),
                cells,
                lax.ppermute(head, axis, [((i + 1) % count, i) for i in range(ends)]),
            ],
            axis=dim,
        )
    return cells


def pair_density(own_pos, lookup, columns):
    remote = lookup[:, columns, :]
    distance = jnp.zeros(
        (own_pos.shape[1], own_pos.shape[2], columns.shape[1], lookup.shape[2]), jnp.float32
    )
    for component in range(3):
        offset = own_pos[component][:, :, None, None] - remote[component][:, None, :, :]
        distance = distance + offset * offset
    weight = jnp.maximum(1.0 - distance / SUPPORT, 0.0)
    return jnp.sum(remote[3][:, None, :, :] * weight * weight * weight, axis=(2, 3))


def pair_force(own_pos, own_vel, own_q, lookup, columns):
    remote = lookup[:, columns, :]
    distance = jnp.zeros(
        (own_pos.shape[1], own_pos.shape[2], columns.shape[1], lookup.shape[2]), jnp.float32
    )
    offsets = []
    for component in range(3):
        offset = own_pos[component][:, :, None, None] - remote[component][:, None, :, :]
        offsets.append(offset)
        distance = distance + offset * offset
    weight = jnp.maximum(1.0 - distance / SUPPORT, 0.0)
    cube = weight * weight * weight
    pushes = (
        remote[6][:, None]
        * (own_q[:, :, None, None] + remote[8][:, None])
        * (6.0 / SUPPORT)
        * weight
        * weight
        - remote[7][:, None] * weight
    )
    damping = VISCOSITY * remote[6][:, None] * cube
    total_damping = jnp.sum(damping, axis=(2, 3))
    rows = []
    for component in range(3):
        rows.append(
            jnp.sum(
                offsets[component] * pushes + damping * remote[3 + component][:, None], axis=(2, 3)
            )
            - own_vel[component] * total_damping
        )
    return jnp.stack(rows, 0)


def shards(positions, velocities, masses, counts, walls, neighbours, send_cells, owners):
    cell_count = positions.shape[1]
    block_width = positions.shape[2]
    peer_count = lax.axis_size("dev")
    particle_slot = lax.broadcasted_iota(jnp.int32, (cell_count, block_width), 1)
    active = (particle_slot < counts[:, None]).astype(jnp.float32)
    wall_mask = walls.astype(jnp.float32) * active
    fluid_mask = active - wall_mask
    mass_eff = masses * active
    bond = mass_eff * (COHESION + (ADHESION - COHESION) * wall_mask)
    send_list = send_cells[0, 0].reshape(-1)
    present = (send_list >= 0).astype(jnp.float32)
    chosen = jnp.maximum(send_list, 0)

    def outgoing(field):
        return field[:, chosen, :] * present[None, :, None]

    def joined(padded, arrived):
        return jnp.concatenate([padded, arrived], 1)

    dens_field = jnp.concatenate([positions, mass_eff[None]], 0)
    dens_table = joined(
        with_halo(dens_field, (("group", 1),), RIM_CELLS),
        lax.all_to_all(outgoing(dens_field), "dev", split_axis=1, concat_axis=1, tiled=True),
    )
    cell_blocks = jnp.arange(cell_count, dtype=jnp.int32).reshape(-1, 4)

    def density_block(cell_ids):
        columns = jnp.concatenate([RIM_CELLS + cell_ids[:, None], neighbours[cell_ids]], 1)
        return pair_density(positions[:, cell_ids, :], dens_table, columns)

    density = lax.map(density_block, cell_blocks).reshape(cell_count, block_width)
    safe_rho = active * density + (1.0 - active)
    pressure_q = active * STIFFNESS * (density - REST_DENSITY) / (safe_rho * safe_rho)
    force_field = jnp.concatenate(
        [positions, velocities, mass_eff[None], bond[None], pressure_q[None]], 0
    )
    force_table = joined(
        with_halo(force_field, (("group", 1),), RIM_CELLS),
        lax.all_to_all(outgoing(force_field), "dev", split_axis=1, concat_axis=1, tiled=True),
    )

    def force_block(cell_ids):
        columns = jnp.concatenate([RIM_CELLS + cell_ids[:, None], neighbours[cell_ids]], 1)
        return pair_force(
            positions[:, cell_ids, :],
            velocities[:, cell_ids, :],
            pressure_q[cell_ids],
            force_table,
            columns,
        )

    acceleration = lax.map(force_block, cell_blocks)
    acceleration = jnp.transpose(acceleration, (1, 0, 2, 3)).reshape(3, cell_count, block_width)
    gravity_vec = jnp.array([0.0, 0.0, GRAVITY], jnp.float32)[:, None, None]
    acceleration = acceleration - gravity_vec
    new_vel = velocities + TIME_STEP * fluid_mask[None] * acceleration
    new_pos = positions + TIME_STEP * fluid_mask[None] * new_vel
    moved = jnp.concatenate([new_pos, new_vel, density[None]], 0) * active[None]
    capacity = max(2, cell_count // (2 * peer_count))
    own_index = lax.axis_index("dev")
    group_owner = owners[0]
    own_owners = lax.dynamic_slice_in_dim(group_owner, own_index * cell_count, cell_count)
    one_hot = (own_owners[:, None] == jnp.arange(peer_count, dtype=jnp.int32)[None, :]).astype(
        jnp.int32
    )
    send_rank = jnp.sum((jnp.cumsum(one_hot, 0) - one_hot) * one_hot, 1)
    staying = own_owners == own_index
    slot_index = jnp.where(staying, peer_count * capacity, own_owners * capacity + send_rank)
    outbox = (
        jnp.zeros((7, peer_count * capacity, block_width), jnp.float32)
        .at[:, slot_index, :]
        .set(moved, mode="drop")
    )
    inbox = lax.all_to_all(outbox, "dev", split_axis=1, concat_axis=1, tiled=True)
    arrivals = jnp.sum(
        (group_owner.reshape(peer_count, cell_count) == own_index).astype(jnp.int32), 1
    )
    arrival_start = jnp.cumsum(arrivals) - arrivals
    rank_in = lax.broadcasted_iota(jnp.int32, (peer_count, capacity), 1)
    source_row = lax.broadcasted_iota(jnp.int32, (peer_count, capacity), 0)
    usable = (rank_in < arrivals[:, None]) & (source_row != own_index)
    arrival_slot = jnp.where(usable, arrival_start[:, None] + rank_in, cell_count).reshape(-1)
    keep_slot = jnp.where(staying, arrival_start[own_index] + send_rank, cell_count)
    settled = (
        jnp.zeros((7, cell_count, block_width), jnp.float32)
        .at[:, arrival_slot, :]
        .set(inbox, mode="drop")
    )
    settled = settled.at[:, keep_slot, :].set(moved, mode="drop")
    return (settled[0:6], settled[6])


def solution(mesh):
    return jax.shard_map(
        shards,
        mesh=mesh,
        in_specs=(
            P(None, ("group", "dev"), None),
            P(None, ("group", "dev"), None),
            P(("group", "dev"), None),
            P(("group", "dev")),
            P(("group", "dev"), None),
            P(("group", "dev"), None),
            P("group", "dev", None, None),
            P("group", None),
        ),
        out_specs=(P(None, ("group", "dev"), None), P(("group", "dev"), None)),
        check_vma=False,
    )
```

profile of v0, /device:TPU:225, one launch (start us, length us, event | category | flops | bytes accessed | tf_op | source)
XLA Modules:
  0.0 218.3 jit_solution(3036807145699850680)
XLA Ops:
  2.1 1.5 multiply_bitcast_fusion.2
  3.6 1.0 copy.51
  5.7 0.8 multiply_bitcast_fusion.1
  6.6 7.8 %all-to-all-start = ((f32[4,64,256]{2,0,1:T(4,128)}), f32[4,64,256]{2,0,1:T(4,128)S(1)}, u32[]{:S(2)}, u32[]{:S(2)}) async-start(f32[4,64,256]{2,0,1:T(4,128)} %multiply_bitcast_fusion.1), calls=%async_computation | async-start | bytes 524288 | tf_op jit(solution)/shard_map/all_to_all | solution.py:104
  14.4 4.8 %collective-permute-start = (f32[4,4,256]{2,0,1:T(4,128)S(1)}, f32[4,4,256]{2,0,1:T(4,128)S(1)}, u32[]{:S(2)}, u32[]{:S(2)}) collective-permute-start(f32[4,4,256]{2,0,1:T(4,128)S(1)} %get-tuple-element.204), channel_id=1, source_target_pairs={{0,32},{32,64},{64,96},{96,128},{128,160},{160,192},{192,224},{224... | collective-permute-start | bytes 49160 | tf_op jit(solution)/shard_map/ppermute | solution.py:27
  19.1 1.9 collective-permute-start.1
  23.5 1.3 collective-permute-done.1
  25.0 37.5 %while.20 = (s32[]{:T(128)}, f32[8,4,256]{2,1,0:T(4,128)S(1)}, s32[8,4]{1,0:T(8,128)S(1)}, s32[32,3]{1,0:T(8,128)S(1)}, f32[4,104,256]{2,0,1:T(4,128)S(1)}, /*index=5*/f32[3,32,256]{2,0,1:T(4,128)S(1)}, s32[]{:T(128)}) while((s32[]{:T(128)}, f32[8,4,256]{2,1,0:T(4,128)S(1)}, s32[8,4]{1,0:T(8,128)S(1)}, s32[32,3]{1,0:T(8,128)S(1)}, ...), condition=%wide.region_6.7_spmd, body=%wide.region_4.0_spmd.sunk | while | flops 15729746 | bytes 565941 | solution.py:112
  27.2 2.5 %fusion.57 = f32[4,256]{1,0:T(4,128)S(1)} fusion(f32[4,4,256]{2,1,0:T(4,128)S(1)} %get-tuple-element.339, f32[4,256]{1,0:T(4,128)S(1)} %get-tuple-element.342, f32[4,4,256]{2,1,0:T(4,128)S(1)} %get-tuple-element.343, f32[4,256]{1,0:T(4,128)S(1)} %get-tuple-element.344, f32[4,4,256]{2,1,0:T(4,128)S(1)} %get-tuple-element.347, ...), kind=kLoop, calls=%fused_computation.14.clone.1 | loop fusion | flops 15727616 | bytes 81920 | tf_op jit(solution)/shard_map/while/body/eval_jaxpr/reduce_sum | solution.py:45
  31.8 2.5 %fusion.57 = f32[4,256]{1,0:T(4,128)S(1)} fusion(f32[4,4,256]{2,1,0:T(4,128)S(1)} %get-tuple-element.339, f32[4,256]{1,0:T(4,128)S(1)} %get-tuple-element.342, f32[4,4,256]{2,1,0:T(4,128)S(1)} %get-tuple-element.343, f32[4,256]{1,0:T(4,128)S(1)} %get-tuple-element.344, f32[4,4,256]{2,1,0:T(4,128)S(1)} %get-tuple-element.347, ...), kind=kLoop, calls=%fused_computation.14.clone.1 | loop fusion | flops 15727616 | bytes 81920 | tf_op jit(solution)/shard_map/while/body/eval_jaxpr/reduce_sum | solution.py:45
  36.5 2.5 %fusion.57 = f32[4,256]{1,0:T(4,128)S(1)} fusion(f32[4,4,256]{2,1,0:T(4,128)S(1)} %get-tuple-element.339, f32[4,256]{1,0:T(4,128)S(1)} %get-tuple-element.342, f32[4,4,256]{2,1,0:T(4,128)S(1)} %get-tuple-element.343, f32[4,256]{1,0:T(4,128)S(1)} %get-tuple-element.344, f32[4,4,256]{2,1,0:T(4,128)S(1)} %get-tuple-element.347, ...), kind=kLoop, calls=%fused_computation.14.clone.1 | loop fusion | flops 15727616 | bytes 81920 | tf_op jit(solution)/shard_map/while/body/eval_jaxpr/reduce_sum | solution.py:45
  41.2 2.5 %fusion.57 = f32[4,256]{1,0:T(4,128)S(1)} fusion(f32[4,4,256]{2,1,0:T(4,128)S(1)} %get-tuple-element.339, f32[4,256]{1,0:T(4,128)S(1)} %get-tuple-element.342, f32[4,4,256]{2,1,0:T(4,128)S(1)} %get-tuple-element.343, f32[4,256]{1,0:T(4,128)S(1)} %get-tuple-element.344, f32[4,4,256]{2,1,0:T(4,128)S(1)} %get-tuple-element.347, ...), kind=kLoop, calls=%fused_computation.14.clone.1 | loop fusion | flops 15727616 | bytes 81920 | tf_op jit(solution)/shard_map/while/body/eval_jaxpr/reduce_sum | solution.py:45
  45.9 2.5 %fusion.57 = f32[4,256]{1,0:T(4,128)S(1)} fusion(f32[4,4,256]{2,1,0:T(4,128)S(1)} %get-tuple-element.339, f32[4,256]{1,0:T(4,128)S(1)} %get-tuple-element.342, f32[4,4,256]{2,1,0:T(4,128)S(1)} %get-tuple-element.343, f32[4,256]{1,0:T(4,128)S(1)} %get-tuple-element.344, f32[4,4,256]{2,1,0:T(4,128)S(1)} %get-tuple-element.347, ...), kind=kLoop, calls=%fused_computation.14.clone.1 | loop fusion | flops 15727616 | bytes 81920 | tf_op jit(solution)/shard_map/while/body/eval_jaxpr/reduce_sum | solution.py:45
  50.6 2.5 %fusion.57 = f32[4,256]{1,0:T(4,128)S(1)} fusion(f32[4,4,256]{2,1,0:T(4,128)S(1)} %get-tuple-element.339, f32[4,256]{1,0:T(4,128)S(1)} %get-tuple-element.342, f32[4,4,256]{2,1,0:T(4,128)S(1)} %get-tuple-element.343, f32[4,256]{1,0:T(4,128)S(1)} %get-tuple-element.344, f32[4,4,256]{2,1,0:T(4,128)S(1)} %get-tuple-element.347, ...), kind=kLoop, calls=%fused_computation.14.clone.1 | loop fusion | flops 15727616 | bytes 81920 | tf_op jit(solution)/shard_map/while/body/eval_jaxpr/reduce_sum | solution.py:45
  55.3 2.5 %fusion.57 = f32[4,256]{1,0:T(4,128)S(1)} fusion(f32[4,4,256]{2,1,0:T(4,128)S(1)} %get-tuple-element.339, f32[4,256]{1,0:T(4,128)S(1)} %get-tuple-element.342, f32[4,4,256]{2,1,0:T(4,128)S(1)} %get-tuple-element.343, f32[4,256]{1,0:T(4,128)S(1)} %get-tuple-element.344, f32[4,4,256]{2,1,0:T(4,128)S(1)} %get-tuple-element.347, ...), kind=kLoop, calls=%fused_computation.14.clone.1 | loop fusion | flops 15727616 | bytes 81920 | tf_op jit(solution)/shard_map/while/body/eval_jaxpr/reduce_sum | solution.py:45
  60.0 2.5 %fusion.57 = f32[4,256]{1,0:T(4,128)S(1)} fusion(f32[4,4,256]{2,1,0:T(4,128)S(1)} %get-tuple-element.339, f32[4,256]{1,0:T(4,128)S(1)} %get-tuple-element.342, f32[4,4,256]{2,1,0:T(4,128)S(1)} %get-tuple-element.343, f32[4,256]{1,0:T(4,128)S(1)} %get-tuple-element.344, f32[4,4,256]{2,1,0:T(4,128)S(1)} %get-tuple-element.347, ...), kind=kLoop, calls=%fused_computation.14.clone.1 | loop fusion | flops 15727616 | bytes 81920 | tf_op jit(solution)/shard_map/while/body/eval_jaxpr/reduce_sum | solution.py:45
  64.0 1.1 multiply_bitcast_fusion
  65.1 8.8 %all-to-all-start.1 = ((f32[9,64,256]{2,0,1:T(8,128)}), f32[9,64,256]{2,0,1:T(8,128)S(1)}, u32[]{:S(2)}, u32[]{:S(2)}) async-start(f32[9,64,256]{2,0,1:T(8,128)} %multiply_bitcast_fusion), calls=%async_computation.1 | async-start | bytes 2097152 | tf_op jit(solution)/shard_map/all_to_all | solution.py:120
  73.9 1.3 fusion.36
  75.8 2.4 %collective-permute-start.2 = (f32[9,4,256]{2,0,1:T(8,128)S(1)}, f32[9,4,256]{2,0,1:T(8,128)}, u32[]{:S(2)}, u32[]{:S(2)}) collective-permute-start(f32[9,4,256]{2,0,1:T(8,128)S(1)} %get-tuple-element.202), channel_id=1, source_target_pairs={{0,32},{32,64},{64,96},{96,128},{128,160},{160,192},{192,224},{224... | collective-permute-start | bytes 110600 | tf_op jit(solution)/shard_map/ppermute | solution.py:27
  78.2 2.9 %collective-permute-start.3 = (f32[9,4,256]{2,0,1:T(8,128)S(1)}, f32[9,4,256]{2,0,1:T(8,128)}, u32[]{:S(2)}, u32[]{:S(2)}) collective-permute-start(f32[9,4,256]{2,0,1:T(8,128)S(1)} %get-tuple-element.203), channel_id=1, source_target_pairs={{32,0},{64,32},{96,64},{128,96},{160,128},{192,160},{224,192},{256... | collective-permute-start | bytes 110600 | tf_op jit(solution)/shard_map/ppermute | solution.py:29
  81.8 2.9 %collective-permute-done.3 = f32[9,4,256]{2,0,1:T(8,128)} collective-permute-done((f32[9,4,256]{2,0,1:T(8,128)S(1)}, f32[9,4,256]{2,0,1:T(8,128)}, u32[]{:S(2)}, u32[]{:S(2)}) %collective-permute-start.3) | collective-permute-done | bytes 36896 | tf_op jit(solution)/shard_map/ppermute | solution.py:29
  84.7 6.1 %all-to-all-done.1 = f32[9,64,256]{2,0,1:T(8,128)S(1)} async-done(((f32[9,64,256]{2,0,1:T(8,128)}), f32[9,64,256]{2,0,1:T(8,128)S(1)}, u32[]{:S(2)}, u32[]{:S(2)}) %all-to-all-start.1) | async-done | bytes 589856 | tf_op jit(solution)/shard_map/all_to_all | solution.py:120
  90.9 1.0 pad_maximum_fusion
  91.9 99.0 %while.21 = (s32[]{:T(128)}, f32[8,3,4,256]{3,1,2,0:T(4,128)}, s32[8,4]{1,0:T(8,128)}, f32[3,32,256]{2,0,1:T(4,128)S(1)}, s32[32,3]{1,0:T(8,128)S(1)}, /*index=5...) while((s32[]{:T(128)}, f32[8,3,4,256]{3,1,2,0:T(4,128)}, ...), condition=%wide.region_12.13_spmd, body=%wide.region_7.12_spmd.sunk | while | flops 35666000 | bytes 1299681 | solution.py:133
  95.5 6.7 %fusion.61 = (f32[4,256]{1,0:T(4,128)S(1)}, f32[4,256]{1,0:T(4,128)S(1)}, f32[4,256]{1,0:T(4,128)S(1)}, f32[4,256]{1,0:T(4,128)S(1)}) fusion(f32[4,4,256]{2,1,0:T(4,128)S(1)} %get-tuple-element.362, f32[4,4,256]{2,1,0:T(4,128)S(1)} %bitcast.192, f32[4,256]{1,0:T(4,128)S(1)} %bitcast.196, f32[4,4,256]{2,1,0:T(4,128)S(1)} %get-tuple-element.367, ...), kind=kLoop, calls=%fused_computation.45.clone.1 | loop fusion | flops 35647488 | bytes 196608 | tf_op jit(solution)/shard_map/while/body/eval_jaxpr/reduce_sum | solution.py:73
  102.2 1.5 gather_fusion.3
  107.9 6.7 %fusion.61 = (f32[4,256]{1,0:T(4,128)S(1)}, f32[4,256]{1,0:T(4,128)S(1)}, f32[4,256]{1,0:T(4,128)S(1)}, f32[4,256]{1,0:T(4,128)S(1)}) fusion(f32[4,4,256]{2,1,0:T(4,128)S(1)} %get-tuple-element.362, f32[4,4,256]{2,1,0:T(4,128)S(1)} %bitcast.192, f32[4,256]{1,0:T(4,128)S(1)} %bitcast.196, f32[4,4,256]{2,1,0:T(4,128)S(1)} %get-tuple-element.367, ...), kind=kLoop, calls=%fused_computation.45.clone.1 | loop fusion | flops 35647488 | bytes 196608 | tf_op jit(solution)/shard_map/while/body/eval_jaxpr/reduce_sum | solution.py:73
  114.6 1.5 gather_fusion.3
  120.2 6.7 %fusion.61 = (f32[4,256]{1,0:T(4,128)S(1)}, f32[4,256]{1,0:T(4,128)S(1)}, f32[4,256]{1,0:T(4,128)S(1)}, f32[4,256]{1,0:T(4,128)S(1)}) fusion(f32[4,4,256]{2,1,0:T(4,128)S(1)} %get-tuple-element.362, f32[4,4,256]{2,1,0:T(4,128)S(1)} %bitcast.192, f32[4,256]{1,0:T(4,128)S(1)} %bitcast.196, f32[4,4,256]{2,1,0:T(4,128)S(1)} %get-tuple-element.367, ...), kind=kLoop, calls=%fused_computation.45.clone.1 | loop fusion | flops 35647488 | bytes 196608 | tf_op jit(solution)/shard_map/while/body/eval_jaxpr/reduce_sum | solution.py:73
  127.0 1.5 gather_fusion.3
  132.6 6.7 %fusion.61 = (f32[4,256]{1,0:T(4,128)S(1)}, f32[4,256]{1,0:T(4,128)S(1)}, f32[4,256]{1,0:T(4,128)S(1)}, f32[4,256]{1,0:T(4,128)S(1)}) fusion(f32[4,4,256]{2,1,0:T(4,128)S(1)} %get-tuple-element.362, f32[4,4,256]{2,1,0:T(4,128)S(1)} %bitcast.192, f32[4,256]{1,0:T(4,128)S(1)} %bitcast.196, f32[4,4,256]{2,1,0:T(4,128)S(1)} %get-tuple-element.367, ...), kind=kLoop, calls=%fused_computation.45.clone.1 | loop fusion | flops 35647488 | bytes 196608 | tf_op jit(solution)/shard_map/while/body/eval_jaxpr/reduce_sum | solution.py:73
  139.4 1.5 gather_fusion.3
  145.0 6.7 %fusion.61 = (f32[4,256]{1,0:T(4,128)S(1)}, f32[4,256]{1,0:T(4,128)S(1)}, f32[4,256]{1,0:T(4,128)S(1)}, f32[4,256]{1,0:T(4,128)S(1)}) fusion(f32[4,4,256]{2,1,0:T(4,128)S(1)} %get-tuple-element.362, f32[4,4,256]{2,1,0:T(4,128)S(1)} %bitcast.192, f32[4,256]{1,0:T(4,128)S(1)} %bitcast.196, f32[4,4,256]{2,1,0:T(4,128)S(1)} %get-tuple-element.367, ...), kind=kLoop, calls=%fused_computation.45.clone.1 | loop fusion | flops 35647488 | bytes 196608 | tf_op jit(solution)/shard_map/while/body/eval_jaxpr/reduce_sum | solution.py:73
  151.7 1.5 gather_fusion.3
  157.3 6.7 %fusion.61 = (f32[4,256]{1,0:T(4,128)S(1)}, f32[4,256]{1,0:T(4,128)S(1)}, f32[4,256]{1,0:T(4,128)S(1)}, f32[4,256]{1,0:T(4,128)S(1)}) fusion(f32[4,4,256]{2,1,0:T(4,128)S(1)} %get-tuple-element.362, f32[4,4,256]{2,1,0:T(4,128)S(1)} %bitcast.192, f32[4,256]{1,0:T(4,128)S(1)} %bitcast.196, f32[4,4,256]{2,1,0:T(4,128)S(1)} %get-tuple-element.367, ...), kind=kLoop, calls=%fused_computation.45.clone.1 | loop fusion | flops 35647488 | bytes 196608 | tf_op jit(solution)/shard_map/while/body/eval_jaxpr/reduce_sum | solution.py:73
  164.1 1.5 gather_fusion.3
  169.7 6.7 %fusion.61 = (f32[4,256]{1,0:T(4,128)S(1)}, f32[4,256]{1,0:T(4,128)S(1)}, f32[4,256]{1,0:T(4,128)S(1)}, f32[4,256]{1,0:T(4,128)S(1)}) fusion(f32[4,4,256]{2,1,0:T(4,128)S(1)} %get-tuple-element.362, f32[4,4,256]{2,1,0:T(4,128)S(1)} %bitcast.192, f32[4,256]{1,0:T(4,128)S(1)} %bitcast.196, f32[4,4,256]{2,1,0:T(4,128)S(1)} %get-tuple-element.367, ...), kind=kLoop, calls=%fused_computation.45.clone.1 | loop fusion | flops 35647488 | bytes 196608 | tf_op jit(solution)/shard_map/while/body/eval_jaxpr/reduce_sum | solution.py:73
  176.5 1.5 gather_fusion.3
  182.1 6.7 %fusion.61 = (f32[4,256]{1,0:T(4,128)S(1)}, f32[4,256]{1,0:T(4,128)S(1)}, f32[4,256]{1,0:T(4,128)S(1)}, f32[4,256]{1,0:T(4,128)S(1)}) fusion(f32[4,4,256]{2,1,0:T(4,128)S(1)} %get-tuple-element.362, f32[4,4,256]{2,1,0:T(4,128)S(1)} %bitcast.192, f32[4,256]{1,0:T(4,128)S(1)} %bitcast.196, f32[4,4,256]{2,1,0:T(4,128)S(1)} %get-tuple-element.367, ...), kind=kLoop, calls=%fused_computation.45.clone.1 | loop fusion | flops 35647488 | bytes 196608 | tf_op jit(solution)/shard_map/while/body/eval_jaxpr/reduce_sum | solution.py:73
  188.8 1.5 gather_fusion.3
  191.0 1.0 multiply_add_fusion
  192.2 0.8 broadcast_in_dim.48
  193.0 4.1 %scatter_fusion = f32[7,64,256]{2,0,1:T(8,128)} fusion(f32[7,64,256]{2,0,1:T(8,128)} %broadcast_in_dim.48, s32[32]{0:T(128)S(1)} %copy-done.12, f32[32,7,256]{2,1,0:T(8,128)S(1)} %copy.56), kind=kCustom, calls=%fused_computation.10 | custom fusion | bytes 688256 | tf_op jit(solution)/shard_map/scatter | solution.py:153
  197.2 4.0 %all-to-all-start.2 = ((f32[7,64,256]{2,0,1:T(8,128)}), f32[7,64,256]{2,0,1:T(8,128)S(1)}, u32[]{:S(2)}, u32[]{:S(2)}) async-start(f32[7,64,256]{2,0,1:T(8,128)} %scatter_fusion), calls=%async_computation.2 | async-start | bytes 1048576 | tf_op jit(solution)/shard_map/all_to_all | solution.py:155
  201.4 11.4 %all-to-all-done.2 = f32[7,64,256]{2,0,1:T(8,128)S(1)} async-done(((f32[7,64,256]{2,0,1:T(8,128)}), f32[7,64,256]{2,0,1:T(8,128)S(1)}, u32[]{:S(2)}, u32[]{:S(2)}) %all-to-all-start.2) | async-done | bytes 458784 | tf_op jit(solution)/shard_map/all_to_all | solution.py:155
  212.8 2.6 %scatter_fusion.1 = f32[7,32,256]{2,0,1:T(8,128)S(1)} fusion(f32[7,32,256]{2,0,1:T(8,128)S(1)} %broadcast_in_dim.44, s32[64]{0:T(128)S(1)} %fusion.34, f32[64,7,256]{2,1,0:T(8,128)S(1)} %bitcast.191), kind=kCustom, calls=%fused_computation.11 | custom fusion | bytes 1376512 | tf_op jit(solution)/shard_map/scatter | solution.py:168
  215.4 1.5 scatter_fusion.2
  (392 shorter events, 58.8 us)
Async XLA Ops:
  0.6 20.4 %copy-start.7 = (s32[32]{0:T(128)S(1)}, s32[32]{0:T(128)}, u32[]{:S(2)}) copy-start(s32[32]{0:T(128)} %param.16) | copy-start | bytes 388
  0.6 21.1 %copy-start.8 = (s32[1,1024]{1,0:T(1,128)S(1)}, s32[1,1024]{1,0:T(1,128)}, u32[]{:S(2)}) copy-start(s32[1,1024]{1,0:T(1,128)} %param.20) | copy-start | bytes 12292
  0.7 21.5 %copy-start.13 = (s32[32,3]{0,1:T(4,128)S(1)}, s32[32,3]{0,1:T(4,128)}, u32[]{:S(2)}) copy-start(s32[32,3]{0,1:T(4,128)} %param.18) | copy-start | bytes 1156
  0.7 21.7 %copy-start.2 = (f32[3,32,256]{2,1,0:T(8,128)S(1)}, f32[3,32,256]{2,1,0:T(8,128)}, u32[]{:S(2)}) copy-start(f32[3,32,256]{2,1,0:T(8,128)} %param.14) | copy-start | bytes 294916
  6.6 18.3 %all-to-all-start = ((f32[4,64,256]{2,0,1:T(4,128)}), f32[4,64,256]{2,0,1:T(4,128)S(1)}, u32[]{:S(2)}, u32[]{:S(2)}) async-start(f32[4,64,256]{2,0,1:T(4,128)} %multiply_bitcast_fusion.1), calls=%async_computation | async-start | bytes 524288 | tf_op jit(solution)/shard_map/all_to_all | solution.py:104
  14.4 9.1 %collective-permute-start = (f32[4,4,256]{2,0,1:T(4,128)S(1)}, f32[4,4,256]{2,0,1:T(4,128)S(1)}, u32[]{:S(2)}, u32[]{:S(2)}) collective-permute-start(f32[4,4,256]{2,0,1:T(4,128)S(1)} %get-tuple-element.204), channel_id=1, source_target_pairs={{0,32},{32,64},{64,96},{96,128},{128,160},{160,192},{192,224},{224... | collective-permute-start | bytes 49160 | tf_op jit(solution)/shard_map/ppermute | solution.py:27
  19.1 5.7 %collective-permute-start.1 = (f32[4,4,256]{2,0,1:T(4,128)S(1)}, f32[4,4,256]{2,0,1:T(4,128)S(1)}, u32[]{:S(2)}, u32[]{:S(2)}) collective-permute-start(f32[4,4,256]{2,0,1:T(4,128)S(1)} %get-tuple-element.205), channel_id=1, source_target_pairs={{32,0},{64,32},{96,64},{128,96},{160,128},{192,160},{224,192},{256... | collective-permute-start | bytes 49160 | tf_op jit(solution)/shard_map/ppermute | solution.py:29
  22.4 40.3 %copy-start = (f32[3,32,256]{2,0,1:T(4,128)}, f32[3,32,256]{2,0,1:T(4,128)S(1)}, u32[]{:S(2)}) copy-start(f32[3,32,256]{2,0,1:T(4,128)S(1)} %copy.49) | copy-start | bytes 294916
  22.6 2.4 %copy-start.9 = (s32[32]{0:T(128)}, s32[32]{0:T(128)S(1)}, u32[]{:S(2)}) copy-start(s32[32]{0:T(128)S(1)} %reduce_sum.73) | copy-start | bytes 388
  22.9 2.1 copy-start.15
  62.5 0.6 copy-start.6
  65.1 25.7 %all-to-all-start.1 = ((f32[9,64,256]{2,0,1:T(8,128)}), f32[9,64,256]{2,0,1:T(8,128)S(1)}, u32[]{:S(2)}, u32[]{:S(2)}) async-start(f32[9,64,256]{2,0,1:T(8,128)} %multiply_bitcast_fusion), calls=%async_computation.1 | async-start | bytes 2097152 | tf_op jit(solution)/shard_map/all_to_all | solution.py:120
  75.8 6.0 %collective-permute-start.2 = (f32[9,4,256]{2,0,1:T(8,128)S(1)}, f32[9,4,256]{2,0,1:T(8,128)}, u32[]{:S(2)}, u32[]{:S(2)}) collective-permute-start(f32[9,4,256]{2,0,1:T(8,128)S(1)} %get-tuple-element.202), channel_id=1, source_target_pairs={{0,32},{32,64},{64,96},{96,128},{128,160},{160,192},{192,224},{224... | collective-permute-start | bytes 110600 | tf_op jit(solution)/shard_map/ppermute | solution.py:27
  78.2 6.5 %collective-permute-start.3 = (f32[9,4,256]{2,0,1:T(8,128)S(1)}, f32[9,4,256]{2,0,1:T(8,128)}, u32[]{:S(2)}, u32[]{:S(2)}) collective-permute-start(f32[9,4,256]{2,0,1:T(8,128)S(1)} %get-tuple-element.203), channel_id=1, source_target_pairs={{32,0},{64,32},{96,64},{128,96},{160,128},{192,160},{224,192},{256... | collective-permute-start | bytes 110600 | tf_op jit(solution)/shard_map/ppermute | solution.py:29
  91.9 99.1 %copy-start.1 = (f32[3,32,256]{2,1,0:T(8,128)S(1)}, f32[3,32,256]{2,1,0:T(8,128)}, u32[]{:S(2)}) copy-start(f32[3,32,256]{2,1,0:T(8,128)} %param.13) | copy-start | bytes 294916
  91.9 99.1 %copy-start.3 = (f32[32,256]{1,0:T(8,128)S(1)}, f32[32,256]{1,0:T(8,128)}, u32[]{:S(2)}) copy-start(f32[32,256]{1,0:T(8,128)} %get-tuple-element.208) | copy-start | bytes 98308
  91.9 99.1 %copy-start.14 = (f32[3]{0:T(128)S(1)}, f32[3]{0:T(128)}, u32[]{:S(2)}) copy-start(f32[3]{0:T(128)} %constant.115) | copy-start | bytes 40
  91.9 100.1 %copy-start.4 = (f32[32,256]{1,0:T(8,128)S(1)}, f32[32,256]{1,0:T(8,128)}, u32[]{:S(2)}) copy-start(f32[32,256]{1,0:T(8,128)} %fusion.28) | copy-start | bytes 98308
  91.9 100.1 %copy-start.5 = (f32[1,32,256]{2,1,0:T(8,128)S(1)}, f32[1,32,256]{2,1,0:T(8,128)}, u32[]{:S(2)}) copy-start(f32[1,32,256]{2,1,0:T(8,128)} %copy.55) | copy-start | bytes 98308
  191.0 2.1 copy-start.12
  192.0 9.2 %copy-start.10 = (s32[32]{0:T(128)S(1)}, s32[32]{0:T(128)}, u32[]{:S(2)}) copy-start(s32[32]{0:T(128)} %copy-done.9) | copy-start | bytes 388
  192.0 9.2 %copy-start.16 = (s32[32]{0:T(128)S(1)}, s32[32]{0:T(128)}, u32[]{:S(2)}) copy-start(s32[32]{0:T(128)} %copy-done.15) | copy-start | bytes 388
  192.0 9.2 %copy-start.17 = (pred[32]{0:T(512)(128)(4,1)S(1)}, pred[32]{0:T(512)(128)(4,1)}, u32[]{:S(2)}) copy-start(pred[32]{0:T(512)(128)(4,1)} %iota_compare_fusion.3) | copy-start | bytes 100
  193.0 22.3 %copy-start.11 = (s32[32]{0:T(128)S(1)}, s32[32]{0:T(128)}, u32[]{:S(2)}) copy-start(s32[32]{0:T(128)} %get-tuple-element.209) | copy-start | bytes 388
  197.2 15.6 %all-to-all-start.2 = ((f32[7,64,256]{2,0,1:T(8,128)}), f32[7,64,256]{2,0,1:T(8,128)S(1)}, u32[]{:S(2)}, u32[]{:S(2)}) async-start(f32[7,64,256]{2,0,1:T(8,128)} %scatter_fusion), calls=%async_computation.2 | async-start | bytes 1048576 | tf_op jit(solution)/shard_map/all_to_all | solution.py:155
where the time goes:
time: 219 us; the launch traced here: 218 us
  other arithmetic  96.9 us (44%)
  local copies, waits for them, and re-layouts  64.5 us (29%)
  starting transfers between devices  32.5 us (15%)
  waiting for transfers between devices  21.8 us (10%)
    reduce_sum x8, other arithmetic, pair_force(): jnp.sum(offsets[component] * pushes + damping * remote[3 + component][:,...  54 us
    reduce_sum x8, other arithmetic, pair_density(): jnp.sum(remote[3][:, None, :, :] * weight * weight * weight, axis=(2, 3))  20 us
    gather x8, local copies, waits for them, and re-layouts, force_block(): velocities[:, cell_ids, :]  11.8 us
    all_to_all x1, waiting for transfers between devices, shards(): lax.all_to_all(outbox, 'dev', split_axis=1, concat_axis=1, tiled=True)  11.4 us
    all_to_all x1, starting transfers between devices, shards(): lax.all_to_all(outgoing(force_field), 'dev', split_axis=1, concat_axis=1,...  8.81 us
    all_to_all x1, starting transfers between devices, shards(): lax.all_to_all(outgoing(dens_field), 'dev', split_axis=1, concat_axis=1,...  7.76 us
    ppermute x2, starting transfers between devices, with_halo(): lax.ppermute(tail, axis, [(i, (i + 1) % count) for i in range(ends)])  7.13 us
    all_to_all x1, waiting for transfers between devices, shards(): lax.all_to_all(outgoing(force_field), 'dev', split_axis=1, concat_axis=1,...  6.15 us
  transfers between devices with their start and end apart: 7, of which 4 were waited for; matrix products, arithmetic and copies ran while one was open for 2% of the time, Pallas kernels for 0%

commit v1 on v0

v1 whole, which is shorter than its diff:
```python
import jax
import jax.numpy as jnp
from jax import lax
from jax.experimental import pallas as pl
from jax.experimental.pallas import tpu as pltpu
from jax.sharding import PartitionSpec as P

RIM = 4
SLOTS = 2
STIFFNESS = 2.0
REST_DENSITY = 0.8
VISCOSITY = 0.5
COHESION = 0.3
ADHESION = 0.8
GRAVITY = 1.0
TIME_STEP = 0.5

F32 = jnp.float32
BF16 = jnp.bfloat16
VMEM = pl.BlockSpec(memory_space=pltpu.VMEM)
SMEM = pl.BlockSpec(memory_space=pltpu.SMEM)


def call(kernel, outs, specs, scratch=(), flops=0):
    return pl.pallas_call(
        kernel,
        out_shape=[jax.ShapeDtypeStruct(s, t) for s, t in outs],
        in_specs=specs,
        out_specs=[VMEM] * len(outs),
        scratch_shapes=list(scratch),
        compiler_params=pltpu.CompilerParams(vmem_limit_bytes=48 * 2**20),
        cost_estimate=pl.CostEstimate(flops=flops, bytes_accessed=2**20, transcendentals=0),
        name=kernel.__name__,
    )


def contract(a, b, dim):
    return lax.dot_general(a, b, (((dim,), (0,)), ((), ())), preferred_element_type=F32)


def pieces(value, count):
    parts = []
    for _ in range(count):
        part = value.astype(BF16).astype(F32)
        parts.append(part)
        value = value - part
    return parts


def prepare(counts, sends, pos, vel, mass, walls, own, send, head, tail, fluid):
    cells, width = mass.shape
    m = mass[...]
    root = jnp.exp(jnp.log(m) * (1.0 / 3.0))
    root = root - (root * root * root - m) / (3.0 * root * root)
    wall = walls[...].astype(F32)
    bond = root * root * (COHESION + (ADHESION - COHESION) * wall)
    free = 1.0 - wall
    lane = lax.broadcasted_iota(jnp.int32, (1, width), 1)
    for c in range(cells):
        row = slice(c, c + 1)
        active = lane < counts[c]
        for k in range(3):
            own[c, k : k + 1, :] = pos[k, row, :]
            own[c, 4 + k : 5 + k, :] = vel[k, row, :]
        own[c, 3:4, :] = jnp.where(active, root[row], 0.0)
        own[c, 7:8, :] = jnp.where(active, bond[row], 0.0)
        fluid[row, :] = jnp.where(active, free[row], 0.0)
    head[...] = own[0:RIM]
    tail[...] = own[cells - RIM : cells]
    for t in range(send.shape[0] // SLOTS):
        for k in range(SLOTS):
            cell = sends[0, 0, t, k]
            tile = own[jnp.maximum(cell, 0)]
            send[t * SLOTS + k] = jnp.where(cell >= 0, tile, 0.0)


def segments(below, own, above, rest):
    start = 0
    for ref in (below, own, above, rest):
        yield start, ref
        start += ref.shape[0]


def weigh(near, tab, mine, c):
    for k in range(near.shape[1] + 1):
        row = RIM + c if k == 0 else near[c, k - 1]
        yield row, jnp.maximum(contract(tab[row], mine[c], 0), 0.0)


def densities(counts, near, sends, below, own, above, rest, rho, q, send_q, tab, mine):
    cells, _, width = own.shape
    sub = lax.broadcasted_iota(jnp.int32, (8, width), 0)

    def squared(tile):
        return jnp.sum(jnp.where(sub < 3, tile * tile, 0.0), axis=0, keepdims=True)

    for start, ref in segments(below, own, above, rest):

        def source(i, carry, start=start, ref=ref):
            tile = ref[i]
            root = tile[3:4]
            far = root * (1.0 - 0.25 * squared(tile))
            value = jnp.where(
                sub < 3,
                tile * (0.5 * root),
                jnp.where(sub == 3, far, jnp.where(sub == 4, -0.25 * root, 0.0)),
            )
            a, b, c = pieces(value, 3)
            tab[start + i] = jnp.concatenate([a, b, a, c, a, b], 0).astype(BF16)
            return carry

        lax.fori_loop(0, ref.shape[0], source, 0, unroll=4)

    def target(i, carry):
        tile = own[i]
        value = jnp.where(
            sub < 3,
            tile,
            jnp.where(sub == 3, 1.0, jnp.where(sub == 4, squared(tile), 0.0)),
        )
        a, b, c = pieces(value, 3)
        mine[i] = jnp.concatenate([a, a, b, a, c, b], 0).astype(BF16)
        return carry

    lax.fori_loop(0, cells, target, 0, unroll=4)

    def cell(i, carry):
        for c in (2 * i, 2 * i + 1):
            total = jnp.zeros((8, width), F32)
            for _, w in weigh(near, tab, mine, c):
                total = total + jnp.sum((w * w * w).reshape(width // 8, 8, width), axis=0)
            rho[pl.ds(c, 1), :] = jnp.sum(total, axis=0, keepdims=True)
        return carry

    lax.fori_loop(0, cells // 2, cell, 0)
    lane = lax.broadcasted_iota(jnp.int32, (1, width), 1)
    for c in range(cells):
        row = rho[c : c + 1, :]
        active = lane < counts[c]
        safe = jnp.where(active, row, 1.0)
        value = STIFFNESS * (row - REST_DENSITY) / (safe * safe)
        q[c : c + 1, :] = jnp.where(active, value, 0.0)
        rho[c : c + 1, :] = jnp.where(active, row, 0.0)
    for t in range(send_q.shape[0] // SLOTS):
        for k in range(SLOTS):
            pick = jnp.maximum(sends[0, 0, t, k], 0)
            send_q[t * SLOTS + k : t * SLOTS + k + 1, :] = q[pl.ds(pick, 1), :]


def forces(
    counts, near, outs, below, own, above, rest, q_below, q, q_above, q_rest, rho, fluid, tab, mine,
    moved, outbox, feat,
):
    cells, _, width = own.shape
    sub = lax.broadcasted_iota(jnp.int32, (8, width), 0)

    for (start, ref), (_, q_ref) in zip(
        segments(below, own, above, rest), segments(q_below, q, q_above, q_rest)
    ):

        def source(i, carry, start=start, ref=ref, q_ref=q_ref):
            tile = ref[i]
            row_q = q_ref[pl.ds(i, 1), :]
            bond = tile[7:8]
            first = jnp.where(
                sub < 3,
                tile * bond,
                jnp.where(sub == 3, bond, jnp.where(sub < 7, tile, 0.0)),
            )
            spot = jnp.where(sub < 3, tile, 1.0)
            spot = jnp.where(sub < 4, spot, row_q * pltpu.roll(spot, 4, 0))
            second = spot * (1.5 * tile[3:4])
            rows = pieces(first, 2) + pieces(second, 3) + [jnp.zeros((8, width), F32)]
            feat[start + i] = jnp.concatenate(rows, 0).astype(BF16)
            return carry

        lax.fori_loop(0, ref.shape[0], source, 0, unroll=4)

    lane = lax.broadcasted_iota(jnp.int32, (1, width), 1)

    def cell(c, carry):
        feats, odd, even = [], [], []
        for row, w in weigh(near, tab, mine, c):
            feats.append(feat[row])
            square = w * w
            high = square.astype(BF16)
            low = (square - high.astype(F32)).astype(BF16)
            once = w.astype(BF16)
            odd.append(jnp.concatenate([once, (square * w).astype(BF16)], 1))
            even.append(jnp.concatenate([high, low], 1))
        feats = jnp.concatenate(feats, 1)
        o13 = contract(feats[0:16], jnp.concatenate(odd, 0), 1)
        o2 = contract(feats[16:48], jnp.concatenate(even, 0), 1)
        o13 = o13[0:8] + o13[8:16]
        o2 = o2[:, :width] + o2[:, width:]
        o2 = o2[0:8] + o2[8:16] + o2[16:24]
        tile = own[c]
        row_rho = rho[pl.ds(c, 1), :]
        mix = q[pl.ds(c, 1), :] * o2 + pltpu.roll(o2, 4, 0) - o13[:, :width]
        speed = pltpu.roll(tile, 4, 0)
        drag = pltpu.roll(o13[:, width:], 4, 0) - speed * row_rho
        acc = tile * mix[3:4] - mix + VISCOSITY * drag
        acc = acc - jnp.where(sub == 2, GRAVITY, 0.0)
        step = TIME_STEP * fluid[pl.ds(c, 1), :]
        speed = speed + step * acc
        place = tile + step * speed
        result = jnp.where(
            sub < 3,
            place,
            jnp.where(sub < 6, pltpu.roll(speed, 3, 0), jnp.where(sub == 6, row_rho, 0.0)),
        )
        moved[c] = jnp.where(lane < counts[c], result, 0.0)
        return carry

    lax.fori_loop(0, cells, cell, 0)
    for t in range(outbox.shape[0] // SLOTS):
        for k in range(SLOTS):
            outbox[t * SLOTS + k] = moved[outs[t, k]]


def settle(kept, arrived, moved, inbox, state, density):
    cells = moved.shape[0]

    def put(place, tile):
        @pl.when(place < cells)
        def _():
            for k in range(6):
                state[k, pl.ds(place, 1), :] = tile[k : k + 1]
            density[pl.ds(place, 1), :] = tile[6:7]

    for c in range(cells):
        put(kept[c], moved[c])
    for t in range(inbox.shape[0] // SLOTS):
        for k in range(SLOTS):
            put(arrived[t, k], inbox[t * SLOTS + k])


def routes(owners, cells, peers):
    me = lax.axis_index("dev")
    ids = jnp.arange(cells, dtype=jnp.int32)
    devs = jnp.arange(peers, dtype=jnp.int32)
    slots = jnp.arange(SLOTS, dtype=jnp.int32)
    per_dev = owners.reshape(peers, cells)
    arrivals = jnp.sum((per_dev == me).astype(jnp.int32), 1)
    before = jnp.sum(jnp.where(devs[None, :] < devs[:, None], arrivals[None, :], 0), 1)
    arrived = jnp.where(
        (slots[None, :] < arrivals[:, None]) & (devs[:, None] != me),
        before[:, None] + slots[None, :],
        cells,
    )
    targets = jnp.sum(jnp.where(devs[:, None] == me, per_dev, 0), 0)
    same = (targets[None, :] == targets[:, None]) & (ids[None, :] < ids[:, None])
    rank = jnp.sum(same.astype(jnp.int32), 1)
    mine = jnp.sum(jnp.where(devs < me, arrivals, 0))
    kept = jnp.where(targets == me, mine + rank, cells)
    hit = (targets[None, None, :] == devs[:, None, None]) & (
        rank[None, None, :] == slots[None, :, None]
    )
    outs = jnp.sum(jnp.where(hit, ids[None, None, :], 0), 2)
    return kept, arrived, outs


def shards(positions, velocities, masses, counts, walls, neighbours, send_cells, owners):
    cells, width = masses.shape
    peers = lax.axis_size("dev")
    total = 2 * RIM + cells + SLOTS * peers
    groups = lax.axis_size("group")
    up = [(i, i + 1) for i in range(groups - 1)]
    down = [(i + 1, i) for i in range(groups - 1)]

    def exchange(x):
        return lax.all_to_all(x, "dev", split_axis=0, concat_axis=0, tiled=True)

    kept, arrived, outs = routes(owners[0], cells, peers)
    own, send, head, tail, fluid = call(
        prepare,
        [
            ((cells, 8, width), F32),
            ((SLOTS * peers, 8, width), F32),
            ((RIM, 8, width), F32),
            ((RIM, 8, width), F32),
            ((cells, width), F32),
        ],
        [SMEM] * 2 + [VMEM] * 4,
    )(counts, send_cells, positions, velocities, masses, walls)
    rest = exchange(send)
    below = lax.ppermute(tail, "group", up)
    above = lax.ppermute(head, "group", down)
    rho, q, send_q, tab, mine = call(
        densities,
        [
            ((cells, width), F32),
            ((cells, width), F32),
            ((SLOTS * peers, width), F32),
            ((total, 48, width), BF16),
            ((cells, 48, width), BF16),
        ],
        [SMEM] * 3 + [VMEM] * 4,
    )(counts, neighbours, send_cells, below, own, above, rest)
    q_rest = exchange(send_q)
    q_below = lax.ppermute(q[cells - RIM :], "group", up)
    q_above = lax.ppermute(q[:RIM], "group", down)
    moved, outbox = call(
        forces,
        [((cells, 8, width), F32), ((SLOTS * peers, 8, width), F32)],
        [SMEM] * 3 + [VMEM] * 12,
        [pltpu.VMEM((total, 48, width), BF16)],
    )(
        counts, neighbours, outs, below, own, above, rest,
        q_below, q, q_above, q_rest, rho, fluid, tab, mine,
    )
    inbox = exchange(outbox)
    state, density = call(
        settle,
        [((6, cells, width), F32), ((cells, width), F32)],
        [SMEM] * 2 + [VMEM] * 2,
    )(kept, arrived, moved, inbox)
    return state, density


def solution(mesh):
    return jax.shard_map(
        shards,
        mesh=mesh,
        in_specs=(
            P(None, ("group", "dev"), None),
            P(None, ("group", "dev"), None),
            P(("group", "dev"), None),
            P(("group", "dev")),
            P(("group", "dev"), None),
            P(("group", "dev"), None),
            P("group", "dev", None, None),
            P("group", None),
        ),
        out_specs=(P(None, ("group", "dev"), None), P(("group", "dev"), None)),
        check_vma=False,
    )
```

time: 219 us -> 122 us (0.56)
  the two profiles are of different devices: /device:TPU:225 before, /device:TPU:257 now
where the time goes in v1:
time: 122 us; the launch traced here: 121 us
  Pallas kernels  43.9 us (36%)
  starting transfers between devices  29.7 us (24%)
  waiting for transfers between devices  24.3 us (20%)
  local copies, waits for them, and re-layouts  17.5 us (14%)
  other arithmetic  4.58 us (4%)
    pallas_call x1, Pallas kernels, shards(): call(forces, [((cells, 8, width), F32), ((SLOTS * peers, 8, width), F32)]...  29.3 us
    all_to_all x3, waiting for transfers between devices, exchange(): return lax.all_to_all(x, 'dev', split_axis=0, concat_axis=0, tiled=True)  24.3 us
    all_to_all x3, starting transfers between devices, exchange(): return lax.all_to_all(x, 'dev', split_axis=0, concat_axis=0, tiled=True)  16.7 us
    unnamed x49, local copies, waits for them, and re-layouts  15.7 us
    pallas_call x1, Pallas kernels, shards(): call(densities, [((cells, width), F32), ((cells, width), F32), ((SLOTS *...  10.3 us
    ppermute x1, starting transfers between devices, shards(): q_above = lax.ppermute(q[:RIM], 'group', down)  4.59 us
    ppermute x1, starting transfers between devices, shards(): above = lax.ppermute(head, 'group', down)  3.85 us
    ppermute x1, starting transfers between devices, shards(): below = lax.ppermute(tail, 'group', up)  2.63 us
  transfers between devices with their start and end apart: 7, of which 3 were waited for; matrix products, arithmetic and copies ran while one was open for 5% of the time, Pallas kernels for 0%

profile of v1, /device:TPU:257, one launch (start us, length us, event | category | flops | bytes accessed | tf_op | source)
XLA Modules:
  0.0 120.8 jit_solution(3836408750420305130)
XLA Ops:
  0.6 0.8 copy.14.sends
  1.4 0.9 copy-done.5
  2.3 0.9 copy-done.6
  3.2 0.8 copy-done.13
  3.9 0.8 copy-done.14
  4.7 0.7 copy-done.15
  5.3 1.9 %prepare.1 = (f32[32,8,256]{2,1,0:T(8,128)S(1)}, f32[64,8,256]{2,1,0:T(8,128)}, f32[4,8,256]{2,1,0:T(8,128)S(1)}, f32[4,8,256]{2,1,0:T(8,128)S(1)}, f32[32,256]{1,0:T(8,128)S(1)}) custom-call(s32[32]{0:T(128)S(1)} %copy-done.15, s32[1,1,32,2]{3,2,1,0:T(8,128)S(1)} %copy.14.sends, f32[3,32,256]{2,1,0:T(8,128)S(1)} %copy-done.5, f32[3,32,256]{2,1,0:T(8,128)S(1)} %copy-done.6, ...), custom_call_target="tpu_custom_call" | custom-call | bytes 1048576 | tf_op jit(solution)/shard_map/prepare/pallas_call | solution.py:275
  7.2 0.6 copy-done.9
  7.8 2.6 %collective-permute-start = (f32[4,8,256]{2,1,0:T(8,128)S(1)}, f32[4,8,256]{2,1,0:T(8,128)S(1)}, u32[]{:S(2)}, u32[]{:S(2)}) collective-permute-start(f32[4,8,256]{2,1,0:T(8,128)S(1)} %get-tuple-element.14), channel_id=1, source_target_pairs={{0,32},{32,64},{64,96},{96,128},{128,160},{160,192},{192,224},{224... | collective-permute-start | bytes 98312 | tf_op jit(solution)/shard_map/ppermute | solution.py:287
  10.5 3.8 %collective-permute-start.1 = (f32[4,8,256]{2,1,0:T(8,128)S(1)}, f32[4,8,256]{2,1,0:T(8,128)S(1)}, u32[]{:S(2)}, u32[]{:S(2)}) collective-permute-start(f32[4,8,256]{2,1,0:T(8,128)S(1)} %get-tuple-element.16), channel_id=1, source_target_pairs={{32,0},{64,32},{96,64},{128,96},{160,128},{192,160},{224,192},{256... | collective-permute-start | bytes 98312 | tf_op jit(solution)/shard_map/ppermute | solution.py:288
  14.3 8.3 %all-to-all-start = ((f32[64,8,256]{2,1,0:T(8,128)}), f32[64,8,256]{2,1,0:T(8,128)S(1)}, u32[]{:S(2)}, u32[]{:S(2)}) async-start(f32[64,8,256]{2,1,0:T(8,128)} %get-tuple-element.17), calls=%async_computation | async-start | bytes 1048576 | tf_op jit(solution)/shard_map/all_to_all | solution.py:272
  22.7 0.5 broadcast.65
  23.2 1.3 %reduce.3 = s32[1024]{0:T(1024)S(1)} reduce(s32[1,1024]{1,0:T(1,128)} %param.15, s32[]{:T(128)} %broadcast.65), dimensions={0}, to_apply=%param.15.reduce_sub_computation.3 | reduce | bytes 8196 | tf_op args[7]
  24.6 0.1 reshape_squeeze.3
  24.6 0.1 convert_reduce_fusion.1
  24.8 0.2 convert_reduce_fusion
  24.9 0.5 copy-done.20
  25.5 0.1 select_reduce_fusion
  25.6 0.7 select_reduce_fusion.1
  26.3 0.8 copy.17.near
  27.0 0.0 collective-permute-done.below
  27.1 7.2 %all-to-all-done.rest = f32[64,8,256]{2,1,0:T(8,128)S(1)} async-done(((f32[64,8,256]{2,1,0:T(8,128)}), f32[64,8,256]{2,1,0:T(8,128)S(1)}, u32[]{:S(2)}, u32[]{:S(2)}) %all-to-all-start) | async-done | bytes 524320 | tf_op jit(solution)/shard_map/all_to_all | solution.py:272
  34.3 0.7 copy-done.16
  35.0 10.3 %densities.1 = (f32[32,256]{1,0:T(8,128)S(1)}, f32[32,256]{1,0:T(8,128)S(1)}, f32[64,256]{1,0:T(8,128)S(1)}, bf16[104,48,256]{2,1,0:T(8,128)(2,1)S(1)}, bf16[32,48,256]{2,1,0:T(8,128)(2,1)S(1)}) custom-call(s32[32]{0:T(128)S(1)} %copy-done.16, s32[32,3]{1,0:T(8,128)S(1)} %copy.17.near, s32[1,1,32,2]{3,2,1,0:T(8,128)S(1)} %copy.14.sends, ...), custom_call_target="tpu_custom_call" | custom-call | bytes 1048576 | tf_op jit(solution)/shard_map/densities/pallas_call | solution.py:289
  45.3 0.9 copy-done
  46.2 0.6 copy-done.11
  46.8 1.9 %collective-permute-start.2 = (f32[4,256]{1,0:T(4,128)S(1)}, f32[4,256]{1,0:T(4,128)}, u32[]{:S(2)}, u32[]{:S(2)}) collective-permute-start(f32[4,256]{1,0:T(4,128)S(1)} %get-tuple-element.29), channel_id=1, source_target_pairs={{0,32},{32,64},{64,96},{96,128},{128,160},{160,192},{192,224},{224... | collective-permute-start | bytes 12296 | tf_op jit(solution)/shard_map/ppermute | solution.py:301
  48.7 4.6 %collective-permute-start.3 = (f32[4,256]{1,0:T(4,128)S(1)}, f32[4,256]{1,0:T(4,128)}, u32[]{:S(2)}, u32[]{:S(2)}) collective-permute-start(f32[4,256]{1,0:T(4,128)S(1)} %get-tuple-element.28), channel_id=1, source_target_pairs={{32,0},{64,32},{96,64},{128,96},{160,128},{192,160},{224,192},{256... | collective-permute-start | bytes 12296 | tf_op jit(solution)/shard_map/ppermute | solution.py:302
  53.3 0.7 all_to_all.14
  54.0 4.5 %all-to-all-start.1 = ((f32[32,2,256]{2,1,0:T(2,128)}), f32[32,2,256]{2,1,0:T(2,128)}, u32[]{:S(2)}, u32[]{:S(2)}) async-start(f32[32,2,256]{2,1,0:T(2,128)} %all_to_all.14), calls=%async_computation.1 | async-start | bytes 131072 | tf_op jit(solution)/shard_map/all_to_all | solution.py:272
  58.5 1.3 %fusion.2 = s32[]{:T(128)} fusion(s32[32]{0:T(128)} %copy-done.18, s32[]{:T(128)S(6)} %axis_index.12), kind=kLoop, calls=%fused_computation.14 | loop fusion | flops 95 | bytes 136 | tf_op jit(solution)/shard_map/reduce_sum | solution.py:254
  59.8 0.1 copy.18.outs
  59.9 6.1 %all-to-all-done.1 = f32[32,2,256]{2,1,0:T(2,128)} async-done(((f32[32,2,256]{2,1,0:T(2,128)}), f32[32,2,256]{2,1,0:T(2,128)}, u32[]{:S(2)}, u32[]{:S(2)}) %all-to-all-start.1) | async-done | bytes 65568 | tf_op jit(solution)/shard_map/all_to_all | solution.py:272
  66.0 0.9 all_to_all.16.q_rest
  66.9 1.1 copy-done.1
  68.0 0.8 copy-done.8
  68.8 0.8 copy-done.10
  69.5 0.8 copy-done.12
  70.3 0.7 copy-done.17
  71.0 29.3 %forces.1 = (f32[32,8,256]{2,1,0:T(8,128)S(1)}, f32[64,8,256]{2,1,0:T(8,128)S(1)}) custom-call(s32[32]{0:T(128)S(1)} %copy-done.17, s32[32,3]{1,0:T(8,128)S(1)} %copy.17.near, s32[32,2]{1,0:T(8,128)S(1)} %copy.18.outs, f32[4,8,256]{2,1,0:T(8,128)S(1)} %collective-permute-done.below, f32[32,8,256]{2,1,0:T(8,128)S(1)} %get-tuple-element.15.own, ...), custom_call_target="tpu_custom_call" | custom-call | bytes 1048576 | tf_op jit(solution)/shard_map/forces/pallas_call | solution.py:303
  100.3 0.8 copy-done.2
  101.1 0.7 copy-done.3
  101.8 3.9 %all-to-all-start.2 = ((f32[64,8,256]{2,1,0:T(8,128)}), f32[64,8,256]{2,1,0:T(8,128)S(1)}, u32[]{:S(2)}, u32[]{:S(2)}) async-start(f32[64,8,256]{2,1,0:T(8,128)} %copy-done.2), calls=%async_computation.2 | async-start | bytes 1048576 | tf_op jit(solution)/shard_map/all_to_all | solution.py:272
  105.7 0.7 compare_select_fusion.1.kept
  106.5 0.1 add_select_fusion.arrived
  106.6 10.9 %all-to-all-done.2.inbox = f32[64,8,256]{2,1,0:T(8,128)S(1)} async-done(((f32[64,8,256]{2,1,0:T(8,128)}), f32[64,8,256]{2,1,0:T(8,128)S(1)}, u32[]{:S(2)}, u32[]{:S(2)}) %all-to-all-start.2) | async-done | bytes 524320 | tf_op jit(solution)/shard_map/all_to_all | solution.py:272
  117.5 0.9 copy-done.4
  118.4 2.4 %settle.1 = (f32[6,32,256]{2,1,0:T(8,128)}, f32[32,256]{1,0:T(8,128)}) custom-call(s32[32]{0:T(128)S(1)} %compare_select_fusion.1.kept, s32[32,2]{1,0:T(8,128)S(1)} %add_select_fusion.arrived, f32[32,8,256]{2,1,0:T(8,128)S(1)} %copy-done.4, f32[64,8,256]{2,1,0:T(8,128)S(1)} %all-to-all-done.2.inbox), custom_call_target="tpu_custom_call" | custom-call | bytes 1048576 | tf_op jit(solution)/shard_map/settle/pallas_call | solution.py:313
  (36 shorter events, 0.1 us)
Async XLA Ops:
  1.4 0.9 copy-start.5
  2.3 0.9 copy-start.6
  3.2 0.8 copy-start.13
  3.9 0.8 copy-start.14
  4.7 0.7 copy-start.15
  7.2 0.6 copy-start.9
  7.8 19.2 %collective-permute-start = (f32[4,8,256]{2,1,0:T(8,128)S(1)}, f32[4,8,256]{2,1,0:T(8,128)S(1)}, u32[]{:S(2)}, u32[]{:S(2)}) collective-permute-start(f32[4,8,256]{2,1,0:T(8,128)S(1)} %get-tuple-element.14), channel_id=1, source_target_pairs={{0,32},{32,64},{64,96},{96,128},{128,160},{160,192},{192,224},{224... | collective-permute-start | bytes 98312 | tf_op jit(solution)/shard_map/ppermute | solution.py:287
  10.5 16.6 %collective-permute-start.1 = (f32[4,8,256]{2,1,0:T(8,128)S(1)}, f32[4,8,256]{2,1,0:T(8,128)S(1)}, u32[]{:S(2)}, u32[]{:S(2)}) collective-permute-start(f32[4,8,256]{2,1,0:T(8,128)S(1)} %get-tuple-element.16), channel_id=1, source_target_pairs={{32,0},{64,32},{96,64},{128,96},{160,128},{192,160},{224,192},{256... | collective-permute-start | bytes 98312 | tf_op jit(solution)/shard_map/ppermute | solution.py:288
  14.3 20.0 %all-to-all-start = ((f32[64,8,256]{2,1,0:T(8,128)}), f32[64,8,256]{2,1,0:T(8,128)S(1)}, u32[]{:S(2)}, u32[]{:S(2)}) async-start(f32[64,8,256]{2,1,0:T(8,128)} %get-tuple-element.17), calls=%async_computation | async-start | bytes 1048576 | tf_op jit(solution)/shard_map/all_to_all | solution.py:272
  24.8 9.6 %copy-start.18 = (s32[32]{0:T(128)}, s32[32]{0:T(128)S(1)}, u32[]{:S(2)}) copy-start(s32[32]{0:T(128)S(1)} %get-tuple-element.26) | copy-start | bytes 388
  24.9 0.5 copy-start.20
  34.3 0.7 copy-start.16
  45.3 0.9 copy-start
  46.2 0.6 copy-start.11
  46.8 13.1 %copy-start.7 = (f32[32,256]{1,0:T(8,128)}, f32[32,256]{1,0:T(8,128)S(1)}, u32[]{:S(2)}) copy-start(f32[32,256]{1,0:T(8,128)S(1)} %get-tuple-element.18.q) | copy-start | bytes 98308
  46.8 20.1 %collective-permute-start.2 = (f32[4,256]{1,0:T(4,128)S(1)}, f32[4,256]{1,0:T(4,128)}, u32[]{:S(2)}, u32[]{:S(2)}) collective-permute-start(f32[4,256]{1,0:T(4,128)S(1)} %get-tuple-element.29), channel_id=1, source_target_pairs={{0,32},{32,64},{64,96},{96,128},{128,160},{160,192},{192,224},{224... | collective-permute-start | bytes 12296 | tf_op jit(solution)/shard_map/ppermute | solution.py:301
  48.7 18.2 %collective-permute-start.3 = (f32[4,256]{1,0:T(4,128)S(1)}, f32[4,256]{1,0:T(4,128)}, u32[]{:S(2)}, u32[]{:S(2)}) collective-permute-start(f32[4,256]{1,0:T(4,128)S(1)} %get-tuple-element.28), channel_id=1, source_target_pairs={{32,0},{64,32},{96,64},{128,96},{160,128},{192,160},{224,192},{256... | collective-permute-start | bytes 12296 | tf_op jit(solution)/shard_map/ppermute | solution.py:302
  54.0 12.0 %all-to-all-start.1 = ((f32[32,2,256]{2,1,0:T(2,128)}), f32[32,2,256]{2,1,0:T(2,128)}, u32[]{:S(2)}, u32[]{:S(2)}) async-start(f32[32,2,256]{2,1,0:T(2,128)} %all_to_all.14), calls=%async_computation.1 | async-start | bytes 131072 | tf_op jit(solution)/shard_map/all_to_all | solution.py:272
  66.9 1.1 copy-start.1
  68.0 0.8 copy-start.8
  68.8 0.8 copy-start.10
  69.5 0.8 copy-start.12
  70.3 0.7 copy-start.17
  71.0 34.8 %copy-start.21 = (s32[32]{0:T(128)S(1)}, s32[32]{0:T(128)}, u32[]{:S(2)}) copy-start(s32[32]{0:T(128)} %copy-done.20) | copy-start | bytes 388
  71.0 35.5 %copy-start.19 = (s32[32]{0:T(128)S(1)}, s32[32]{0:T(128)}, u32[]{:S(2)}) copy-start(s32[32]{0:T(128)} %copy-done.18) | copy-start | bytes 388
  71.0 35.5 %copy-start.22 = (s32[32]{0:T(128)S(1)}, s32[32]{0:T(128)}, u32[]{:S(2)}) copy-start(s32[32]{0:T(128)} %select_reduce_fusion.1) | copy-start | bytes 388
  100.3 0.8 copy-start.2
  101.1 0.7 copy-start.3
  101.8 15.7 %all-to-all-start.2 = ((f32[64,8,256]{2,1,0:T(8,128)}), f32[64,8,256]{2,1,0:T(8,128)S(1)}, u32[]{:S(2)}, u32[]{:S(2)}) async-start(f32[64,8,256]{2,1,0:T(8,128)} %copy-done.2), calls=%async_computation.2 | async-start | bytes 1048576 | tf_op jit(solution)/shard_map/all_to_all | solution.py:272
  117.5 1.0 copy-start.4

commit v2 on v1

--- a/solution.py
+++ b/solution.py
@@ -17,21 +17,63 @@
 
 F32 = jnp.float32
 BF16 = jnp.bfloat16
+HBM = pl.BlockSpec(memory_space=pltpu.HBM)
 VMEM = pl.BlockSpec(memory_space=pltpu.VMEM)
-SMEM = pl.BlockSpec(memory_space=pltpu.SMEM)
-
-
-def call(kernel, outs, specs, scratch=(), flops=0):
+
+
+class Moves:
+    def __init__(self, ins, outs):
+        self.ins, self.outs = list(ins), list(outs)
+        self.waited, self.saved = set(), set()
+        for copy in self.ins:
+            copy.start()
+
+    def need(self, *which):
+        for i in which:
+            if i not in self.waited:
+                self.waited.add(i)
+                self.ins[i].wait()
+
+    def save(self, *which):
+        for i in which:
+            if i not in self.saved:
+                self.saved.add(i)
+                self.outs[i].start()
+
+
+def call(kernel, room, ints, held, near, outs, scratch=()):
+    n_in, n_near, n_out = len(ints) + len(held), len(near), len(outs)
+
+    def body(*refs):
+        sources, refs = refs[:n_in], refs[n_in:]
+        close, refs = refs[:n_near], refs[n_near:]
+        targets, refs = refs[:n_out], refs[n_out:]
+        inner, refs = refs[:n_in], refs[n_in:]
+        results, refs = refs[:n_out], refs[n_out:]
+        in_sems, out_sems, rest = refs[0], refs[1], refs[2:]
+        moves = Moves(
+            [pltpu.make_async_copy(a, b, in_sems.at[i]) for i, (a, b) in enumerate(zip(sources, inner))],
+            [pltpu.make_async_copy(a, b, out_sems.at[i]) for i, (a, b) in enumerate(zip(results, targets))],
+        )
+        kernel(moves, *inner, *close, *results, *rest)
+        moves.need(*range(n_in))
+        moves.save(*range(n_out))
+        for copy in moves.outs:
+            copy.wait()
+
     return pl.pallas_call(
-        kernel,
-        out_shape=[jax.ShapeDtypeStruct(s, t) for s, t in outs],
-        in_specs=specs,
-        out_specs=[VMEM] * len(outs),
-        scratch_shapes=list(scratch),
-        compiler_params=pltpu.CompilerParams(vmem_limit_bytes=48 * 2**20),
-        cost_estimate=pl.CostEstimate(flops=flops, bytes_accessed=2**20, transcendentals=0),
+        body,
+        out_shape=[jax.ShapeDtypeStruct(*o) for o in outs],
+        in_specs=[HBM] * n_in + [VMEM] * n_near,
+        out_specs=[HBM] * n_out,
+        scratch_shapes=[pltpu.SMEM(x.shape, x.dtype) for x in ints]
+        + [pltpu.VMEM(x.shape, x.dtype) for x in held]
+        + [pltpu.VMEM(*o) for o in outs]
+        + [pltpu.SemaphoreType.DMA((n_in,)), pltpu.SemaphoreType.DMA((n_out,))]
+        + list(scratch),
+        compiler_params=pltpu.CompilerParams(vmem_limit_bytes=(64 << 20) - (room << 10)),
         name=kernel.__name__,
-    )
+    )(*ints, *held, *near)
 
 
 def contract(a, b, dim):
@@ -47,8 +89,9 @@
     return parts
 
 
-def prepare(counts, sends, pos, vel, mass, walls, own, send, head, tail, fluid):
+def prepare(moves, counts, sends, pos, vel, mass, walls, own, send, head, tail, fluid):
     cells, width = mass.shape
+    moves.need(*range(6))
     m = mass[...]
     root = jnp.exp(jnp.log(m) * (1.0 / 3.0))
     root = root - (root * root * root - m) / (3.0 * root * root)
@@ -69,7 +112,7 @@
     tail[...] = own[cells - RIM : cells]
     for t in range(send.shape[0] // SLOTS):
         for k in range(SLOTS):
-            cell = sends[0, 0, t, k]
+            cell = sends[0, 0, k, t]
             tile = own[jnp.maximum(cell, 0)]
             send[t * SLOTS + k] = jnp.where(cell >= 0, tile, 0.0)
 
@@ -82,12 +125,15 @@
 
 
 def weigh(near, tab, mine, c):
-    for k in range(near.shape[1] + 1):
-        row = RIM + c if k == 0 else near[c, k - 1]
+    for k in range(near.shape[0] + 1):
+        row = RIM + c if k == 0 else near[k - 1, c]
         yield row, jnp.maximum(contract(tab[row], mine[c], 0), 0.0)
 
 
-def densities(counts, near, sends, below, own, above, rest, rho, q, send_q, tab, mine):
+def densities(
+    moves, counts, near, sends, own, below, above, rest, rho, q, q_head, q_tail, send_q, tab, mine, tiles,
+):
+    moves.need(0, 1, 2, 3)
     cells, _, width = own.shape
     sub = lax.broadcasted_iota(jnp.int32, (8, width), 0)
 
@@ -107,6 +153,7 @@
             )
             a, b, c = pieces(value, 3)
             tab[start + i] = jnp.concatenate([a, b, a, c, a, b], 0).astype(BF16)
+            tiles[start + i] = tile
             return carry
 
         lax.fori_loop(0, ref.shape[0], source, 0, unroll=4)
@@ -123,6 +170,7 @@
         return carry
 
     lax.fori_loop(0, cells, target, 0, unroll=4)
+    moves.save(5, 6, 7)
 
     def cell(i, carry):
         for c in (2 * i, 2 * i + 1):
@@ -141,26 +189,28 @@
         value = STIFFNESS * (row - REST_DENSITY) / (safe * safe)
         q[c : c + 1, :] = jnp.where(active, value, 0.0)
         rho[c : c + 1, :] = jnp.where(active, row, 0.0)
+    for r in range(RIM):
+        q_head[r] = q[r : r + 1, :]
+        q_tail[r] = q[cells - RIM + r : cells - RIM + r + 1, :]
     for t in range(send_q.shape[0] // SLOTS):
         for k in range(SLOTS):
-            pick = jnp.maximum(sends[0, 0, t, k], 0)
-            send_q[t * SLOTS + k : t * SLOTS + k + 1, :] = q[pl.ds(pick, 1), :]
+            pick = jnp.maximum(sends[0, 0, k, t], 0)
+            send_q[t * SLOTS + k] = q[pl.ds(pick, 1), :]
 
 
 def forces(
-    counts, near, outs, below, own, above, rest, q_below, q, q_above, q_rest, rho, fluid, tab, mine,
+    moves, counts, near, outs, tiles, q, rho, fluid, tab, mine, q_below, q_above, q_rest,
     moved, outbox, feat,
 ):
-    cells, _, width = own.shape
+    cells, _, width = moved.shape
+    moves.need(3, 4)
     sub = lax.broadcasted_iota(jnp.int32, (8, width), 0)
 
-    for (start, ref), (_, q_ref) in zip(
-        segments(below, own, above, rest), segments(q_below, q, q_above, q_rest)
-    ):
-
-        def source(i, carry, start=start, ref=ref, q_ref=q_ref):
-            tile = ref[i]
-            row_q = q_ref[pl.ds(i, 1), :]
+    for start, q_ref in segments(q_below, q, q_above, q_rest):
+
+        def source(i, carry, start=start, q_ref=q_ref):
+            tile = tiles[start + i]
+            row_q = q_ref[i] if q_ref.ndim == 3 else q_ref[pl.ds(i, 1), :]
             bond = tile[7:8]
             first = jnp.where(
                 sub < 3,
@@ -174,7 +224,7 @@
             feat[start + i] = jnp.concatenate(rows, 0).astype(BF16)
             return carry
 
-        lax.fori_loop(0, ref.shape[0], source, 0, unroll=4)
+        lax.fori_loop(0, q_ref.shape[0], source, 0, unroll=4)
 
     lane = lax.broadcasted_iota(jnp.int32, (1, width), 1)
 
@@ -194,7 +244,7 @@
         o13 = o13[0:8] + o13[8:16]
         o2 = o2[:, :width] + o2[:, width:]
         o2 = o2[0:8] + o2[8:16] + o2[16:24]
-        tile = own[c]
+        tile = tiles[RIM + c]
         row_rho = rho[pl.ds(c, 1), :]
         mix = q[pl.ds(c, 1), :] * o2 + pltpu.roll(o2, 4, 0) - o13[:, :width]
         speed = pltpu.roll(tile, 4, 0)
@@ -212,14 +262,17 @@
         moved[c] = jnp.where(lane < counts[c], result, 0.0)
         return carry
 
+    moves.need(*range(9))
     lax.fori_loop(0, cells, cell, 0)
+    moves.save(0)
     for t in range(outbox.shape[0] // SLOTS):
         for k in range(SLOTS):
             outbox[t * SLOTS + k] = moved[outs[t, k]]
 
 
-def settle(kept, arrived, moved, inbox, state, density):
+def settle(moves, kept, arrived, moved, inbox, state, density):
     cells = moved.shape[0]
+    moves.need(0, 1, 2)
 
     def put(place, tile):
         @pl.when(place < cells)
@@ -272,8 +325,14 @@
         return lax.all_to_all(x, "dev", split_axis=0, concat_axis=0, tiled=True)
 
     kept, arrived, outs = routes(owners[0], cells, peers)
+    near = neighbours.T
+    sends = jnp.swapaxes(send_cells, 2, 3)
     own, send, head, tail, fluid = call(
         prepare,
+        4096,
+        [counts, sends],
+        [positions, velocities, masses, walls],
+        [],
         [
             ((cells, 8, width), F32),
             ((SLOTS * peers, 8, width), F32),
@@ -281,41 +340,48 @@
             ((RIM, 8, width), F32),
             ((cells, width), F32),
         ],
-        [SMEM] * 2 + [VMEM] * 4,
-    )(counts, send_cells, positions, velocities, masses, walls)
+    )
     rest = exchange(send)
     below = lax.ppermute(tail, "group", up)
     above = lax.ppermute(head, "group", down)
-    rho, q, send_q, tab, mine = call(
+    rho, q, q_head, q_tail, send_q, tab, mine, tiles = call(
         densities,
+        4096,
+        [counts, near, sends],
+        [own],
+        [below, above, rest],
         [
             ((cells, width), F32),
             ((cells, width), F32),
-            ((SLOTS * peers, width), F32),
+            ((RIM, 1, width), F32),
+            ((RIM, 1, width), F32),
+            ((SLOTS * peers, 1, width), F32),
             ((total, 48, width), BF16),
             ((cells, 48, width), BF16),
+            ((total, 8, width), F32),
         ],
-        [SMEM] * 3 + [VMEM] * 4,
-    )(counts, neighbours, send_cells, below, own, above, rest)
+    )
     q_rest = exchange(send_q)
-    q_below = lax.ppermute(q[cells - RIM :], "group", up)
-    q_above = lax.ppermute(q[:RIM], "group", down)
+    q_below = lax.ppermute(q_tail, "group", up)
+    q_above = lax.ppermute(q_head, "group", down)
     moved, outbox = call(
         forces,
+        4096,
+        [counts, near, outs],
+        [tiles, q, rho, fluid, tab, mine],
+        [q_below, q_above, q_rest],
         [((cells, 8, width), F32), ((SLOTS * peers, 8, width), F32)],
-        [SMEM] * 3 + [VMEM] * 12,
         [pltpu.VMEM((total, 48, width), BF16)],
-    )(
-        counts, neighbours, outs, below, own, above, rest,
-        q_below, q, q_above, q_rest, rho, fluid, tab, mine,
     )
     inbox = exchange(outbox)
-    state, density = call(
+    return call(
         settle,
+        12000,
+        [kept, arrived],
+        [moved],
+        [inbox],
         [((6, cells, width), F32), ((cells, width), F32)],
-        [SMEM] * 2 + [VMEM] * 2,
-    )(kept, arrived, moved, inbox)
-    return state, density
+    )
 
 
 def solution(mesh):

time: 122 us -> 112 us (0.918)
  local copies, waits for them, and re-layouts: 17.5 us -> 3.7 us
  Pallas kernels: 43.9 us -> 48.1 us
  waiting for transfers between devices: 24.3 us -> 26.1 us
  other arithmetic: 4.58 us -> 3.19 us
    unnamed x49 -> x15, local copies, waits for them, and re-layouts: 15.7 us -> 2.93 us
    pallas_call x4, Pallas kernels: 43.9 us -> 48.1 us  [call(): pl.pallas_call(body, out_shape=[jax.ShapeDtypeStruct(*o) for o in outs],...]
    all_to_all x3, waiting for transfers between devices: 24.3 us -> 26.1 us  [exchange(): return lax.all_to_all(x, 'dev', split_axis=0, concat_axis=0, tiled=True)]
    all_to_all x2 -> x0, local copies, waits for them, and re-layouts: 1.55 us -> none  [exchange(): return lax.all_to_all(x, 'dev', split_axis=0, concat_axis=0, tiled=True)]
  transfers between devices with their start and end apart: 7 -> 7, of which waited for: 3 -> 3; matrix products, arithmetic and copies ran while one was open for 5% -> 4% of each run, Pallas kernels for 0% -> 0%
where the time goes in v2:
time: 112 us; the launch traced here: 111 us
  Pallas kernels  48.1 us (43%)
  starting transfers between devices  29.5 us (26%)
  waiting for transfers between devices  26.1 us (23%)
  local copies, waits for them, and re-layouts  3.7 us (3%)
  other arithmetic  3.19 us (3%)
    pallas_call x4, Pallas kernels, call(): pl.pallas_call(body, out_shape=[jax.ShapeDtypeStruct(*o) for o in outs],...  48.1 us
    all_to_all x3, waiting for transfers between devices, exchange(): return lax.all_to_all(x, 'dev', split_axis=0, concat_axis=0, tiled=True)  26.1 us
    all_to_all x3, starting transfers between devices, exchange(): return lax.all_to_all(x, 'dev', split_axis=0, concat_axis=0, tiled=True)  16.5 us
    ppermute x1, starting transfers between devices, shards(): q_above = lax.ppermute(q_head, 'group', down)  4.6 us
    ppermute x1, starting transfers between devices, shards(): above = lax.ppermute(head, 'group', down)  3.85 us
    unnamed x15, local copies, waits for them, and re-layouts  2.93 us
    ppermute x1, starting transfers between devices, shards(): below = lax.ppermute(tail, 'group', up)  2.65 us
  transfers between devices with their start and end apart: 7, of which 3 were waited for; matrix products, arithmetic and copies ran while one was open for 4% of the time, Pallas kernels for 0%

profile of v2, /device:TPU:257, one launch (start us, length us, event | category | flops | bytes accessed | tf_op | source)
XLA Modules:
  0.0 111.4 jit_solution(9584693959356196658)
XLA Ops:
  0.6 2.2 %prepare.1 = (f32[32,8,256]{2,1,0:T(8,128)}, f32[64,8,256]{2,1,0:T(8,128)}, f32[4,8,256]{2,1,0:T(8,128)}, f32[4,8,256]{2,1,0:T(8,128)}, f32[32,256]{1,0:T(8,128)}) custom-call(s32[32]{0:T(128)} %refs_0_.5, s32[1,1,2,32]{3,2,1,0:T(2,128)} %bitcast.4, f32[3,32,256]{2,1,0:T(8,128)} %refs_2_.1, f32[3,32,256]{2,1,0:T(8,128)} %refs_3_.1, f32[32,256]{1,0:T(8,128)} %refs_4_.1, ...), custom_call_target="tpu_custom_call" | custom-call | tf_op jit(solution)/shard_map/prepare/pallas_call | solution.py:64
  2.9 2.6 %collective-permute-start = (f32[4,8,256]{2,1,0:T(8,128)}, f32[4,8,256]{2,1,0:T(8,128)S(1)}, u32[]{:S(2)}, u32[]{:S(2)}) collective-permute-start(f32[4,8,256]{2,1,0:T(8,128)} %get-tuple-element.18), channel_id=1, source_target_pairs={{0,32},{32,64},{64,96},{96,128},{128,160},{160,192},{192,224},{224... | collective-permute-start | bytes 98312 | tf_op jit(solution)/shard_map/ppermute | solution.py:345
  5.5 3.8 %collective-permute-start.1 = (f32[4,8,256]{2,1,0:T(8,128)}, f32[4,8,256]{2,1,0:T(8,128)S(1)}, u32[]{:S(2)}, u32[]{:S(2)}) collective-permute-start(f32[4,8,256]{2,1,0:T(8,128)} %get-tuple-element.19), channel_id=1, source_target_pairs={{32,0},{64,32},{96,64},{128,96},{160,128},{192,160},{224,192},{256... | collective-permute-start | bytes 98312 | tf_op jit(solution)/shard_map/ppermute | solution.py:346
  9.4 8.3 %all-to-all-start = ((f32[64,8,256]{2,1,0:T(8,128)}), f32[64,8,256]{2,1,0:T(8,128)S(1)}, u32[]{:S(2)}, u32[]{:S(2)}) async-start(f32[64,8,256]{2,1,0:T(8,128)} %get-tuple-element.20), calls=%async_computation | async-start | bytes 1048576 | tf_op jit(solution)/shard_map/all_to_all | solution.py:325
  17.7 0.5 broadcast.65
  18.3 1.3 %reduce.3 = s32[1024]{0:T(1024)S(1)} reduce(s32[1,1024]{1,0:T(1,128)} %param.15, s32[]{:T(128)} %broadcast.65), dimensions={0}, to_apply=%param.15.reduce_sub_computation.3 | reduce | bytes 8196 | tf_op args[7]
  19.6 0.1 reshape_squeeze.3
  19.7 0.1 convert_reduce_fusion.1
  19.8 0.2 convert_reduce_fusion
  20.0 0.1 select_reduce_fusion
  20.1 0.1 select_reduce_fusion.1
  20.2 0.0 collective-permute-done.refs_4_
  20.2 0.0 copy-start.3
  20.2 0.0 collective-permute-done.1.refs_5_
  20.2 0.0 copy-start.4
  20.3 9.1 %all-to-all-done.refs_6_ = f32[64,8,256]{2,1,0:T(8,128)S(1)} async-done(((f32[64,8,256]{2,1,0:T(8,128)}), f32[64,8,256]{2,1,0:T(8,128)S(1)}, u32[]{:S(2)}, u32[]{:S(2)}) %all-to-all-start) | async-done | bytes 524320 | tf_op jit(solution)/shard_map/all_to_all | solution.py:325
  29.3 0.0 copy-start.1
  29.3 0.0 copy-done.3
  29.3 0.0 copy-done.4
  29.3 0.8 copy-done.1
  30.1 12.0 %densities.1 = (f32[32,256]{1,0:T(8,128)}, f32[32,256]{1,0:T(8,128)}, f32[4,1,256]{2,1,0:T(1,128)}, f32[4,1,256]{2,1,0:T(1,128)}, f32[64,1,256]{2,1,0:T(1,128)},...) custom-call(s32[32]{0:T(128)} %refs_0_.5, s32[3,32]{1,0:T(4,128)} %bitcast.2, ...), custom_call_target="tpu_custom_call" | custom-call | tf_op jit(solution)/shard_map/densities/pallas_call | solution.py:64
  42.2 1.9 %collective-permute-start.2 = (f32[4,1,256]{2,1,0:T(1,128)}, f32[4,1,256]{2,1,0:T(1,128)S(1)}, u32[]{:S(2)}, u32[]{:S(2)}) collective-permute-start(f32[4,1,256]{2,1,0:T(1,128)} %get-tuple-element.27), channel_id=1, source_target_pairs={{0,32},{32,64},{64,96},{96,128},{128,160},{160,192},{192,224},{224... | collective-permute-start | bytes 12296 | tf_op jit(solution)/shard_map/ppermute | solution.py:365
  44.1 4.6 %collective-permute-start.3 = (f32[4,1,256]{2,1,0:T(1,128)}, f32[4,1,256]{2,1,0:T(1,128)S(1)}, u32[]{:S(2)}, u32[]{:S(2)}) collective-permute-start(f32[4,1,256]{2,1,0:T(1,128)} %get-tuple-element.28), channel_id=1, source_target_pairs={{32,0},{64,32},{96,64},{128,96},{160,128},{192,160},{224,192},{256... | collective-permute-start | bytes 12296 | tf_op jit(solution)/shard_map/ppermute | solution.py:366
  48.7 4.2 %all-to-all-start.1 = ((f32[64,1,256]{2,1,0:T(1,128)}), f32[64,1,256]{2,1,0:T(1,128)S(1)}, u32[]{:S(2)}, u32[]{:S(2)}) async-start(f32[64,1,256]{2,1,0:T(1,128)} %get-tuple-element.29), calls=%async_computation.1 | async-start | bytes 131072 | tf_op jit(solution)/shard_map/all_to_all | solution.py:325
  52.9 0.6 fusion.2
  53.5 0.7 copy.10.refs_2_
  54.2 0.0 collective-permute-done.2.refs_9_
  54.2 0.0 copy-start.5
  54.2 0.0 collective-permute-done.3.refs_10_
  54.2 0.0 copy-start.6
  54.2 6.0 %all-to-all-done.1.refs_11_ = f32[64,1,256]{2,1,0:T(1,128)S(1)} async-done(((f32[64,1,256]{2,1,0:T(1,128)}), f32[64,1,256]{2,1,0:T(1,128)S(1)}, u32[]{:S(2)}, u32[]{:S(2)}) %all-to-all-start.1) | async-done | bytes 65568 | tf_op jit(solution)/shard_map/all_to_all | solution.py:325
  60.3 0.0 copy-start.2
  60.3 0.0 copy-done.5
  60.3 0.0 copy-done.6
  60.3 0.6 copy-done.2
  60.9 31.4 %forces.1 = (f32[32,8,256]{2,1,0:T(8,128)}, f32[64,8,256]{2,1,0:T(8,128)}) custom-call(s32[32]{0:T(128)} %refs_0_.5, s32[3,32]{1,0:T(4,128)} %bitcast.3, s32[32,2]{1,0:T(8,128)} %copy.10.refs_2_, f32[104,8,256]{2,1,0:T(8,128)} %get-tuple-element.21.refs_3_, f32[32,256]{1,0:T(8,128)} %get-tuple-element.22.refs_4_, f32[32,256]{1,0:T(8,128)} %get-tuple-element.23.refs_5_, ...), custom_call_target="tpu_custom_call" | custom-call | tf_op jit(solution)/shard_map/forces/pallas_call | solution.py:64
  92.3 3.9 %all-to-all-start.2 = ((f32[64,8,256]{2,1,0:T(8,128)}), f32[64,8,256]{2,1,0:T(8,128)S(1)}, u32[]{:S(2)}, u32[]{:S(2)}) async-start(f32[64,8,256]{2,1,0:T(8,128)} %get-tuple-element.31), calls=%async_computation.2 | async-start | bytes 1048576 | tf_op jit(solution)/shard_map/all_to_all | solution.py:325
  96.3 0.6 compare_select_fusion.1.refs_0_
  96.9 0.1 add_select_fusion.refs_1_
  97.0 11.0 %all-to-all-done.2.refs_3_ = f32[64,8,256]{2,1,0:T(8,128)S(1)} async-done(((f32[64,8,256]{2,1,0:T(8,128)}), f32[64,8,256]{2,1,0:T(8,128)S(1)}, u32[]{:S(2)}, u32[]{:S(2)}) %all-to-all-start.2) | async-done | bytes 524320 | tf_op jit(solution)/shard_map/all_to_all | solution.py:325
  108.0 0.0 copy-start
  108.0 0.9 copy-done
  109.0 2.5 %settle.1 = (f32[6,32,256]{2,1,0:T(8,128)}, f32[32,256]{1,0:T(8,128)}) custom-call(s32[32]{0:T(128)S(1)} %compare_select_fusion.1.refs_0_, s32[32,2]{1,0:T(8,128)S(1)} %add_select_fusion.refs_1_, f32[32,8,256]{2,1,0:T(8,128)S(1)} %copy-done, f32[64,8,256]{2,1,0:T(8,128)S(1)} %all-to-all-done.2.refs_3_), custom_call_target="tpu_custom_call" | custom-call | tf_op jit(solution)/shard_map/settle/pallas_call | solution.py:64
  (4 shorter events, 0.0 us)
Async XLA Ops:
  2.9 17.3 %collective-permute-start = (f32[4,8,256]{2,1,0:T(8,128)}, f32[4,8,256]{2,1,0:T(8,128)S(1)}, u32[]{:S(2)}, u32[]{:S(2)}) collective-permute-start(f32[4,8,256]{2,1,0:T(8,128)} %get-tuple-element.18), channel_id=1, source_target_pairs={{0,32},{32,64},{64,96},{96,128},{128,160},{160,192},{192,224},{224... | collective-permute-start | bytes 98312 | tf_op jit(solution)/shard_map/ppermute | solution.py:345
  5.5 14.7 %collective-permute-start.1 = (f32[4,8,256]{2,1,0:T(8,128)}, f32[4,8,256]{2,1,0:T(8,128)S(1)}, u32[]{:S(2)}, u32[]{:S(2)}) collective-permute-start(f32[4,8,256]{2,1,0:T(8,128)} %get-tuple-element.19), channel_id=1, source_target_pairs={{32,0},{64,32},{96,64},{128,96},{160,128},{192,160},{224,192},{256... | collective-permute-start | bytes 98312 | tf_op jit(solution)/shard_map/ppermute | solution.py:346
  9.4 20.0 %all-to-all-start = ((f32[64,8,256]{2,1,0:T(8,128)}), f32[64,8,256]{2,1,0:T(8,128)S(1)}, u32[]{:S(2)}, u32[]{:S(2)}) async-start(f32[64,8,256]{2,1,0:T(8,128)} %get-tuple-element.20), calls=%async_computation | async-start | bytes 1048576 | tf_op jit(solution)/shard_map/all_to_all | solution.py:325
  20.2 9.1 %copy-start.3 = (f32[4,8,256]{2,1,0:T(8,128)}, f32[4,8,256]{2,1,0:T(8,128)S(1)}, u32[]{:S(2)}) copy-start(f32[4,8,256]{2,1,0:T(8,128)S(1)} %collective-permute-done.refs_4_) | copy-start | bytes 98308
  20.2 9.1 %copy-start.4 = (f32[4,8,256]{2,1,0:T(8,128)}, f32[4,8,256]{2,1,0:T(8,128)S(1)}, u32[]{:S(2)}) copy-start(f32[4,8,256]{2,1,0:T(8,128)S(1)} %collective-permute-done.1.refs_5_) | copy-start | bytes 98308
  29.3 0.8 copy-start.1
  42.2 12.1 %collective-permute-start.2 = (f32[4,1,256]{2,1,0:T(1,128)}, f32[4,1,256]{2,1,0:T(1,128)S(1)}, u32[]{:S(2)}, u32[]{:S(2)}) collective-permute-start(f32[4,1,256]{2,1,0:T(1,128)} %get-tuple-element.27), channel_id=1, source_target_pairs={{0,32},{32,64},{64,96},{96,128},{128,160},{160,192},{192,224},{224... | collective-permute-start | bytes 12296 | tf_op jit(solution)/shard_map/ppermute | solution.py:365
  44.1 10.1 %collective-permute-start.3 = (f32[4,1,256]{2,1,0:T(1,128)}, f32[4,1,256]{2,1,0:T(1,128)S(1)}, u32[]{:S(2)}, u32[]{:S(2)}) collective-permute-start(f32[4,1,256]{2,1,0:T(1,128)} %get-tuple-element.28), channel_id=1, source_target_pairs={{32,0},{64,32},{96,64},{128,96},{160,128},{192,160},{224,192},{256... | collective-permute-start | bytes 12296 | tf_op jit(solution)/shard_map/ppermute | solution.py:366
  48.7 11.6 %all-to-all-start.1 = ((f32[64,1,256]{2,1,0:T(1,128)}), f32[64,1,256]{2,1,0:T(1,128)S(1)}, u32[]{:S(2)}, u32[]{:S(2)}) async-start(f32[64,1,256]{2,1,0:T(1,128)} %get-tuple-element.29), calls=%async_computation.1 | async-start | bytes 131072 | tf_op jit(solution)/shard_map/all_to_all | solution.py:325
  54.2 6.0 %copy-start.5 = (f32[4,1,256]{2,1,0:T(1,128)}, f32[4,1,256]{2,1,0:T(1,128)S(1)}, u32[]{:S(2)}) copy-start(f32[4,1,256]{2,1,0:T(1,128)S(1)} %collective-permute-done.2.refs_9_) | copy-start | bytes 12292
  54.2 6.0 %copy-start.6 = (f32[4,1,256]{2,1,0:T(1,128)}, f32[4,1,256]{2,1,0:T(1,128)S(1)}, u32[]{:S(2)}) copy-start(f32[4,1,256]{2,1,0:T(1,128)S(1)} %collective-permute-done.3.refs_10_) | copy-start | bytes 12292
  60.3 0.6 copy-start.2
  92.3 15.7 %all-to-all-start.2 = ((f32[64,8,256]{2,1,0:T(8,128)}), f32[64,8,256]{2,1,0:T(8,128)S(1)}, u32[]{:S(2)}, u32[]{:S(2)}) async-start(f32[64,8,256]{2,1,0:T(8,128)} %get-tuple-element.31), calls=%async_computation.2 | async-start | bytes 1048576 | tf_op jit(solution)/shard_map/all_to_all | solution.py:325
  108.0 1.0 copy-start

commit v3 on v2

--- a/solution.py
+++ b/solution.py
@@ -7,6 +7,7 @@
 
 RIM = 4
 SLOTS = 2
+MOVERS = 16
 STIFFNESS = 2.0
 REST_DENSITY = 0.8
 VISCOSITY = 0.5
@@ -198,94 +199,161 @@
             send_q[t * SLOTS + k] = q[pl.ds(pick, 1), :]
 
 
-def forces(
-    moves, counts, near, outs, tiles, q, rho, fluid, tab, mine, q_below, q_above, q_rest,
-    moved, outbox, feat,
-):
-    cells, _, width = moved.shape
-    moves.need(3, 4)
-    sub = lax.broadcasted_iota(jnp.int32, (8, width), 0)
-
-    for start, q_ref in segments(q_below, q, q_above, q_rest):
-
-        def source(i, carry, start=start, q_ref=q_ref):
-            tile = tiles[start + i]
-            row_q = q_ref[i] if q_ref.ndim == 3 else q_ref[pl.ds(i, 1), :]
-            bond = tile[7:8]
-            first = jnp.where(
-                sub < 3,
-                tile * bond,
-                jnp.where(sub == 3, bond, jnp.where(sub < 7, tile, 0.0)),
-            )
-            spot = jnp.where(sub < 3, tile, 1.0)
-            spot = jnp.where(sub < 4, spot, row_q * pltpu.roll(spot, 4, 0))
-            second = spot * (1.5 * tile[3:4])
-            rows = pieces(first, 2) + pieces(second, 3) + [jnp.zeros((8, width), F32)]
-            feat[start + i] = jnp.concatenate(rows, 0).astype(BF16)
-            return carry
-
-        lax.fori_loop(0, q_ref.shape[0], source, 0, unroll=4)
-
-    lane = lax.broadcasted_iota(jnp.int32, (1, width), 1)
-
-    def cell(c, carry):
-        feats, odd, even = [], [], []
-        for row, w in weigh(near, tab, mine, c):
-            feats.append(feat[row])
-            square = w * w
+def first_features(tile, sub):
+    bond = tile[7:8]
+    value = jnp.where(
+        sub < 3,
+        tile * bond,
+        jnp.where(sub == 3, bond, jnp.where(sub < 7, tile, 0.0)),
+    )
+    return jnp.concatenate(pieces(value, 2), 0).astype(BF16)
+
+
+def second_features(tile, row_q, sub):
+    spot = jnp.where(sub < 3, tile, 1.0)
+    spot = jnp.where(sub < 4, spot, row_q * pltpu.roll(spot, 4, 0))
+    value = spot * (1.5 * tile[3:4])
+    rows = pieces(value, 3) + [jnp.zeros_like(value)]
+    return jnp.concatenate(rows, 0).astype(BF16)
+
+
+def pair_sums(near, tab, mine, feat1, feat2, c, sub):
+    feats1, feats2, odd, even = [], [], [], []
+    for row, w in weigh(near, tab, mine, c):
+        square = w * w
+        if feat1 is not None:
+            feats1.append(feat1[row])
+            odd.append(jnp.concatenate([w.astype(BF16), (square * w).astype(BF16)], 1))
+        if feat2 is not None:
+            feats2.append(feat2[row])
             high = square.astype(BF16)
             low = (square - high.astype(F32)).astype(BF16)
-            once = w.astype(BF16)
-            odd.append(jnp.concatenate([once, (square * w).astype(BF16)], 1))
             even.append(jnp.concatenate([high, low], 1))
-        feats = jnp.concatenate(feats, 1)
-        o13 = contract(feats[0:16], jnp.concatenate(odd, 0), 1)
-        o2 = contract(feats[16:48], jnp.concatenate(even, 0), 1)
-        o13 = o13[0:8] + o13[8:16]
-        o2 = o2[:, :width] + o2[:, width:]
-        o2 = o2[0:8] + o2[8:16] + o2[16:24]
-        tile = tiles[RIM + c]
-        row_rho = rho[pl.ds(c, 1), :]
-        mix = q[pl.ds(c, 1), :] * o2 + pltpu.roll(o2, 4, 0) - o13[:, :width]
-        speed = pltpu.roll(tile, 4, 0)
-        drag = pltpu.roll(o13[:, width:], 4, 0) - speed * row_rho
-        acc = tile * mix[3:4] - mix + VISCOSITY * drag
-        acc = acc - jnp.where(sub == 2, GRAVITY, 0.0)
-        step = TIME_STEP * fluid[pl.ds(c, 1), :]
-        speed = speed + step * acc
-        place = tile + step * speed
-        result = jnp.where(
-            sub < 3,
-            place,
-            jnp.where(sub < 6, pltpu.roll(speed, 3, 0), jnp.where(sub == 6, row_rho, 0.0)),
+    first = second = None
+    if feat1 is not None:
+        first = contract(jnp.concatenate(feats1, 1), jnp.concatenate(odd, 0), 1)
+        first = first[0:8] + first[8:16]
+        width = first.shape[1] // 2
+        first = jnp.where(sub < 4, first[:, :width], first[:, width:])
+    if feat2 is not None:
+        second = contract(jnp.concatenate(feats2, 1), jnp.concatenate(even, 0), 1)
+        width = second.shape[1] // 2
+        second = second[:, :width] + second[:, width:]
+        second = second[0:8] + second[8:16] + second[16:24]
+    return first, second
+
+
+def advance(first, second, tile, row_q, row_rho, row_fluid, active, sub):
+    mix = row_q * second + pltpu.roll(second, 4, 0) - first
+    speed = pltpu.roll(tile, 4, 0)
+    drag = pltpu.roll(first, 4, 0) - speed * row_rho
+    acc = tile * mix[3:4] - mix + VISCOSITY * drag
+    acc = acc - jnp.where(sub == 2, GRAVITY, 0.0)
+    step = TIME_STEP * row_fluid
+    speed = speed + step * acc
+    place = tile + step * speed
+    result = jnp.where(
+        sub < 3,
+        place,
+        jnp.where(sub < 6, pltpu.roll(speed, 3, 0), jnp.where(sub == 6, row_rho, 0.0)),
+    )
+    return jnp.where(active, result, 0.0)
+
+
+def rows_and_lanes(width):
+    return (
+        lax.broadcasted_iota(jnp.int32, (8, width), 0),
+        lax.broadcasted_iota(jnp.int32, (1, width), 1),
+    )
+
+
+def forces_early(moves, near, movers, tiles, tab, mine, early, feat1):
+    sub, _ = rows_and_lanes(tiles.shape[2])
+    moves.need(0, 1, 2)
+
+    def source(i, carry):
+        feat1[i] = first_features(tiles[i], sub)
+        return carry
+
+    lax.fori_loop(0, tiles.shape[0], source, 0, unroll=8)
+    moves.save(1)
+    moves.need(3, 4)
+
+    def cell(i, carry):
+        early[i], _ = pair_sums(near, tab, mine, feat1, None, movers[i], sub)
+        return carry
+
+    lax.fori_loop(0, early.shape[0], cell, 0)
+
+
+def forces_late(
+    moves, counts, near, movers, outs, tiles, q, rho, fluid, tab, mine, early, q_below, q_above, q_rest,
+    outbox, feat2, moved,
+):
+    sub, lane = rows_and_lanes(tiles.shape[2])
+    moves.need(4, 5)
+    for start, q_ref in segments(q_below, q, q_above, q_rest):
+
+        def source(i, carry, start=start, q_ref=q_ref):
+            row_q = q_ref[i] if q_ref.ndim == 3 else q_ref[pl.ds(i, 1), :]
+            feat2[start + i] = second_features(tiles[start + i], row_q, sub)
+            return carry
+
+        lax.fori_loop(0, q_ref.shape[0], source, 0, unroll=4)
+
+    moves.save(1)
+    moves.need(*range(11))
+
+    def cell(i, carry):
+        c = movers[i]
+        _, second = pair_sums(near, tab, mine, None, feat2, c, sub)
+        row = pl.ds(c, 1)
+        moved[i] = advance(
+            early[i], second, tiles[RIM + c], q[row, :], rho[row, :], fluid[row, :], lane < counts[c], sub
         )
-        moved[c] = jnp.where(lane < counts[c], result, 0.0)
-        return carry
-
-    moves.need(*range(9))
-    lax.fori_loop(0, cells, cell, 0)
-    moves.save(0)
+        return carry
+
+    lax.fori_loop(0, early.shape[0], cell, 0)
     for t in range(outbox.shape[0] // SLOTS):
         for k in range(SLOTS):
             outbox[t * SLOTS + k] = moved[outs[t, k]]
 
 
-def settle(moves, kept, arrived, moved, inbox, state, density):
-    cells = moved.shape[0]
+def forces_staying(
+    moves, counts, near, stayers, tiles, q, rho, fluid, tab, mine, feat1, feat2, stayed
+):
+    sub, lane = rows_and_lanes(tiles.shape[2])
+    moves.need(*range(11))
+
+    def cell(i, carry):
+        c = stayers[i]
+        first, second = pair_sums(near, tab, mine, feat1, feat2, c, sub)
+        row = pl.ds(c, 1)
+        stayed[i] = advance(
+            first, second, tiles[RIM + c], q[row, :], rho[row, :], fluid[row, :], lane < counts[c], sub
+        )
+        return carry
+
+    lax.fori_loop(0, stayed.shape[0], cell, 0)
+
+
+def settle(moves, first, arrived, stayed, inbox, state, density):
+    cells = state.shape[1]
     moves.need(0, 1, 2)
 
     def put(place, tile):
-        @pl.when(place < cells)
+        for k in range(6):
+            state[k, pl.ds(place, 1), :] = tile[k : k + 1]
+        density[pl.ds(place, 1), :] = tile[6:7]
+
+    for i in range(stayed.shape[0]):
+        put(first[0] + i, stayed[i])
+    for t in range(inbox.shape[0] // SLOTS):
+
+        @pl.when(arrived[t] < cells)
         def _():
-            for k in range(6):
-                state[k, pl.ds(place, 1), :] = tile[k : k + 1]
-            density[pl.ds(place, 1), :] = tile[6:7]
-
-    for c in range(cells):
-        put(kept[c], moved[c])
-    for t in range(inbox.shape[0] // SLOTS):
-        for k in range(SLOTS):
-            put(arrived[t, k], inbox[t * SLOTS + k])
+            for k in range(SLOTS):
+                put(arrived[t] + k, inbox[t * SLOTS + k])
 
 
 def routes(owners, cells, peers):
@@ -293,24 +361,26 @@
     ids = jnp.arange(cells, dtype=jnp.int32)
     devs = jnp.arange(peers, dtype=jnp.int32)
     slots = jnp.arange(SLOTS, dtype=jnp.int32)
+    halves = jnp.arange(MOVERS, dtype=jnp.int32)
     per_dev = owners.reshape(peers, cells)
     arrivals = jnp.sum((per_dev == me).astype(jnp.int32), 1)
     before = jnp.sum(jnp.where(devs[None, :] < devs[:, None], arrivals[None, :], 0), 1)
-    arrived = jnp.where(
-        (slots[None, :] < arrivals[:, None]) & (devs[:, None] != me),
-        before[:, None] + slots[None, :],
-        cells,
-    )
+    arrived = jnp.where((arrivals > 0) & (devs != me), before, cells)
+    first = jnp.sum(jnp.where(devs == me, before, 0)).reshape(1)
     targets = jnp.sum(jnp.where(devs[:, None] == me, per_dev, 0), 0)
-    same = (targets[None, :] == targets[:, None]) & (ids[None, :] < ids[:, None])
-    rank = jnp.sum(same.astype(jnp.int32), 1)
-    mine = jnp.sum(jnp.where(devs < me, arrivals, 0))
-    kept = jnp.where(targets == me, mine + rank, cells)
+    earlier = ids[None, :] < ids[:, None]
+    rank = jnp.sum(((targets[None, :] == targets[:, None]) & earlier).astype(jnp.int32), 1)
+    leaves = targets != me
+    order = jnp.sum(((leaves[None, :] == leaves[:, None]) & earlier).astype(jnp.int32), 1)
+    spot = order[None, :] == halves[:, None]
+    movers = jnp.sum(jnp.where(spot & leaves[None, :], ids[None, :], 0), 1)
+    stayers = jnp.sum(jnp.where(spot & ~leaves[None, :], ids[None, :], 0), 1)
     hit = (targets[None, None, :] == devs[:, None, None]) & (
         rank[None, None, :] == slots[None, :, None]
     )
-    outs = jnp.sum(jnp.where(hit, ids[None, None, :], 0), 2)
-    return kept, arrived, outs
+    hit = hit & (devs != me)[:, None, None]
+    outs = jnp.sum(jnp.where(hit, order[None, None, :], 0), 2)
+    return first, arrived, movers, stayers, outs
 
 
 def shards(positions, velocities, masses, counts, walls, neighbours, send_cells, owners):
@@ -324,7 +394,7 @@
     def exchange(x):
         return lax.all_to_all(x, "dev", split_axis=0, concat_axis=0, tiled=True)
 
-    kept, arrived, outs = routes(owners[0], cells, peers)
+    first, arrived, movers, stayers, outs = routes(owners[0], cells, peers)
     near = neighbours.T
     sends = jnp.swapaxes(send_cells, 2, 3)
     own, send, head, tail, fluid = call(
@@ -364,21 +434,37 @@
     q_rest = exchange(send_q)
     q_below = lax.ppermute(q_tail, "group", up)
     q_above = lax.ppermute(q_head, "group", down)
-    moved, outbox = call(
-        forces,
+    early, feat1 = call(
+        forces_early,
         4096,
-        [counts, near, outs],
-        [tiles, q, rho, fluid, tab, mine],
+        [near, movers],
+        [tiles, tab, mine],
+        [],
+        [((MOVERS, 8, width), F32), ((total, 16, width), BF16)],
+    )
+    outbox, feat2 = call(
+        forces_late,
+        4096,
+        [counts, near, movers, outs],
+        [tiles, q, rho, fluid, tab, mine, early],
         [q_below, q_above, q_rest],
-        [((cells, 8, width), F32), ((SLOTS * peers, 8, width), F32)],
-        [pltpu.VMEM((total, 48, width), BF16)],
+        [((SLOTS * peers, 8, width), F32), ((total, 32, width), BF16)],
+        [pltpu.VMEM((MOVERS, 8, width), F32)],
     )
     inbox = exchange(outbox)
+    [stayed] = call(
+        forces_staying,
+        4096,
+        [counts, near, stayers],
+        [tiles, q, rho, fluid, tab, mine, feat1, feat2],
+        [],
+        [((cells - MOVERS, 8, width), F32)],
+    )
     return call(
         settle,
         12000,
-        [kept, arrived],
-        [moved],
+        [first, arrived],
+        [stayed],
         [inbox],
         [((6, cells, width), F32), ((cells, width), F32)],
     )

time: 112 us -> 107 us (0.955)
  the two profiles are of different devices: /device:TPU:257 before, /device:TPU:227 now
where the time goes in v3:
time: 107 us; the launch traced here: 106 us
  Pallas kernels  60.1 us (56%)
  starting transfers between devices  36.7 us (34%)
  local copies, waits for them, and re-layouts  3.66 us (3%)
  other arithmetic  3.54 us (3%)
  waiting for transfers between devices  1.37 us (1%)
    pallas_call x6, Pallas kernels, call(): pl.pallas_call(body, out_shape=[jax.ShapeDtypeStruct(*o) for o in outs],...  60.1 us
    all_to_all x3, starting transfers between devices, exchange(): return lax.all_to_all(x, 'dev', split_axis=0, concat_axis=0, tiled=True)  24.7 us
    ppermute x1, starting transfers between devices, shards(): below = lax.ppermute(tail, 'group', up)  4.76 us
    ppermute x1, starting transfers between devices, shards(): q_above = lax.ppermute(q_head, 'group', down)  2.93 us
    unnamed x15, local copies, waits for them, and re-layouts  2.9 us
    ppermute x1, starting transfers between devices, shards(): q_below = lax.ppermute(q_tail, 'group', up)  2.35 us
  transfers between devices with their start and end apart: 7, of which 1 were waited for; matrix products, arithmetic and copies ran while one was open for 5% of the time, Pallas kernels for 26%

profile of v3, /device:TPU:227, one launch (start us, length us, event | category | flops | bytes accessed | tf_op | source)
XLA Modules:
  0.0 106.2 jit_solution(4803851902401566354)
XLA Ops:
  0.6 2.2 %prepare.1 = (f32[32,8,256]{2,1,0:T(8,128)}, f32[64,8,256]{2,1,0:T(8,128)}, f32[4,8,256]{2,1,0:T(8,128)}, f32[4,8,256]{2,1,0:T(8,128)}, f32[32,256]{1,0:T(8,128)}) custom-call(s32[32]{0:T(128)} %refs_0_.7, s32[1,1,2,32]{3,2,1,0:T(2,128)} %bitcast.7, f32[3,32,256]{2,1,0:T(8,128)} %refs_2_.1, f32[3,32,256]{2,1,0:T(8,128)} %refs_3_.1, f32[32,256]{1,0:T(8,128)} %refs_4_.1, ...), custom_call_target="tpu_custom_call" | custom-call | tf_op jit(solution)/shard_map/prepare/pallas_call | solution.py:65
  2.9 7.9 %all-to-all-start = ((f32[64,8,256]{2,1,0:T(8,128)}), f32[64,8,256]{2,1,0:T(8,128)S(1)}, u32[]{:S(2)}, u32[]{:S(2)}) async-start(f32[64,8,256]{2,1,0:T(8,128)} %get-tuple-element.22), calls=%async_computation | async-start | bytes 1048576 | tf_op jit(solution)/shard_map/all_to_all | solution.py:395
  10.8 4.8 %collective-permute-start = (f32[4,8,256]{2,1,0:T(8,128)}, f32[4,8,256]{2,1,0:T(8,128)S(1)}, u32[]{:S(2)}, u32[]{:S(2)}) collective-permute-start(f32[4,8,256]{2,1,0:T(8,128)} %get-tuple-element.20), channel_id=1, source_target_pairs={{0,32},{32,64},{64,96},{96,128},{128,160},{160,192},{192,224},{224... | collective-permute-start | bytes 98312 | tf_op jit(solution)/shard_map/ppermute | solution.py:415
  15.6 1.9 %collective-permute-start.1 = (f32[4,8,256]{2,1,0:T(8,128)}, f32[4,8,256]{2,1,0:T(8,128)S(1)}, u32[]{:S(2)}, u32[]{:S(2)}) collective-permute-start(f32[4,8,256]{2,1,0:T(8,128)} %get-tuple-element.21), channel_id=1, source_target_pairs={{32,0},{64,32},{96,64},{128,96},{160,128},{192,160},{224,192},{256... | collective-permute-start | bytes 98312 | tf_op jit(solution)/shard_map/ppermute | solution.py:416
  17.5 0.6 broadcast.75
  18.1 1.4 %reduce.3 = s32[1024]{0:T(1024)S(1)} reduce(s32[1,1024]{1,0:T(1,128)} %param.15, s32[]{:T(128)} %broadcast.75), dimensions={0}, to_apply=%param.15.reduce_sub_computation.3 | reduce | bytes 8196 | tf_op args[7]
  19.5 0.1 reshape_squeeze.3
  19.6 0.1 select_reduce_fusion.1
  19.7 0.2 convert_reduce_fusion
  19.9 0.2 convert_reduce_fusion.1
  20.1 0.2 select_reduce_fusion
  20.3 0.0 collective-permute-done.refs_4_
  20.3 0.0 copy-start.3
  20.3 1.4 %collective-permute-done.1.refs_5_ = f32[4,8,256]{2,1,0:T(8,128)S(1)} collective-permute-done((f32[4,8,256]{2,1,0:T(8,128)}, f32[4,8,256]{2,1,0:T(8,128)S(1)}, u32[]{:S(2)}, u32[]{:S(2)}) %collective-permute-start.1) | collective-permute-done | bytes 32800 | tf_op jit(solution)/shard_map/ppermute | solution.py:416
  21.7 0.0 copy-start.4
  21.7 0.0 all-to-all-done.refs_6_
  21.7 0.0 copy-start.1
  21.7 0.0 copy-done.3
  21.7 0.6 copy-done.4
  22.3 0.2 copy-done.1
  22.4 12.0 %densities.1 = (f32[32,256]{1,0:T(8,128)}, f32[32,256]{1,0:T(8,128)}, f32[4,1,256]{2,1,0:T(1,128)}, f32[4,1,256]{2,1,0:T(1,128)}, f32[64,1,256]{2,1,0:T(1,128)},...) custom-call(s32[32]{0:T(128)} %refs_0_.7, s32[3,32]{1,0:T(4,128)} %bitcast.3, ...), custom_call_target="tpu_custom_call" | custom-call | tf_op jit(solution)/shard_map/densities/pallas_call | solution.py:65
  34.5 8.8 %all-to-all-start.1 = ((f32[64,1,256]{2,1,0:T(1,128)}), f32[64,1,256]{2,1,0:T(1,128)S(1)}, u32[]{:S(2)}, u32[]{:S(2)}) async-start(f32[64,1,256]{2,1,0:T(1,128)} %get-tuple-element.33), calls=%async_computation.1 | async-start | bytes 131072 | tf_op jit(solution)/shard_map/all_to_all | solution.py:395
  43.3 2.4 %collective-permute-start.2 = (f32[4,1,256]{2,1,0:T(1,128)}, f32[4,1,256]{2,1,0:T(1,128)S(1)}, u32[]{:S(2)}, u32[]{:S(2)}) collective-permute-start(f32[4,1,256]{2,1,0:T(1,128)} %get-tuple-element.31), channel_id=1, source_target_pairs={{0,32},{32,64},{64,96},{96,128},{128,160},{160,192},{192,224},{224... | collective-permute-start | bytes 12296 | tf_op jit(solution)/shard_map/ppermute | solution.py:435
  45.7 2.9 %collective-permute-start.3 = (f32[4,1,256]{2,1,0:T(1,128)}, f32[4,1,256]{2,1,0:T(1,128)S(1)}, u32[]{:S(2)}, u32[]{:S(2)}) collective-permute-start(f32[4,1,256]{2,1,0:T(1,128)} %get-tuple-element.32), channel_id=1, source_target_pairs={{32,0},{64,32},{96,64},{128,96},{160,128},{192,160},{224,192},{256... | collective-permute-start | bytes 12296 | tf_op jit(solution)/shard_map/ppermute | solution.py:436
  48.6 0.7 select_reduce_fusion.3
  49.3 0.7 copy.10.refs_3_
  50.0 10.6 %forces_early.1 = (f32[16,8,256]{2,1,0:T(8,128)}, bf16[104,16,256]{2,1,0:T(8,128)(2,1)}) custom-call(s32[3,32]{1,0:T(4,128)} %bitcast.4, s32[16]{0:T(128)} %get-tuple-element.38.refs_1_.refs_2_, f32[104,8,256]{2,1,0:T(8,128)} %get-tuple-element.23.refs_2_.refs_4_.refs_3_, bf16[104,48,256]{2,1,0:T(8,128)(2,1)} %get-tuple-element.27.refs_3_.refs_8_.refs_7_, ...), custom_call_target="tpu_custom_call" | custom-call | tf_op jit(solution)/shard_map/forces_early/pallas_call | solution.py:65
  60.6 0.0 collective-permute-done.2.refs_11_
  60.6 0.0 copy-start.5
  60.6 0.0 collective-permute-done.3.refs_12_
  60.6 0.0 copy-start.6
  60.6 0.0 all-to-all-done.1.refs_13_
  60.7 0.0 copy-start.2
  60.7 0.5 copy-done.5
  61.2 0.0 copy-done.6
  61.2 0.0 copy-done.2
  61.3 15.5 %forces_late.1 = (f32[64,8,256]{2,1,0:T(8,128)}, bf16[104,32,256]{2,1,0:T(8,128)(2,1)}) custom-call(s32[32]{0:T(128)} %refs_0_.7, s32[3,32]{1,0:T(4,128)} %bitcast.5, s32[16]{0:T(128)} %get-tuple-element.38.refs_1_.refs_2_, s32[32,2]{1,0:T(8,128)} %copy.10.refs_3_, f32[104,8,256]{2,1,0:T(8,128)} %get-tuple-element.23.refs_2_.refs_4_.refs_3_, ...), custom_call_target="tpu_custom_call" | custom-call | tf_op jit(solution)/shard_map/forces_late/pallas_call | solution.py:65
  76.8 8.0 %all-to-all-start.2 = ((f32[64,8,256]{2,1,0:T(8,128)}), f32[64,8,256]{2,1,0:T(8,128)S(1)}, u32[]{:S(2)}, u32[]{:S(2)}) async-start(f32[64,8,256]{2,1,0:T(8,128)} %get-tuple-element.35), calls=%async_computation.2 | async-start | bytes 1048576 | tf_op jit(solution)/shard_map/all_to_all | solution.py:395
  84.8 0.1 select_reduce_fusion.2
  84.9 0.7 and_select_fusion
  85.5 17.5 %forces_staying.1.refs_2_ = f32[16,8,256]{2,1,0:T(8,128)} custom-call(s32[32]{0:T(128)} %refs_0_.7, s32[3,32]{1,0:T(4,128)} %bitcast.6, s32[16]{0:T(128)} %get-tuple-element.39.refs_2_, f32[104,8,256]{2,1,0:T(8,128)} %get-tuple-element.23.refs_2_.refs_4_.refs_3_, f32[32,256]{1,0:T(8,128)} %get-tuple-element.24.refs_5_.refs_4_, ...), custom_call_target="tpu_custom_call" | custom-call | tf_op jit(solution)/shard_map/forces_staying/pallas_call | solution.py:65
  103.0 0.0 all-to-all-done.2.refs_3_
  103.1 0.0 copy-start
  103.1 0.9 copy-done
  104.0 2.3 %settle.1 = (f32[6,32,256]{2,1,0:T(8,128)}, f32[32,256]{1,0:T(8,128)}) custom-call(s32[1]{0:T(128)} %bitcast.refs_0_, s32[32]{0:T(128)S(1)} %get-tuple-element.42.refs_1_, f32[16,8,256]{2,1,0:T(8,128)S(1)} %copy-done, f32[64,8,256]{2,1,0:T(8,128)S(1)} %all-to-all-done.2.refs_3_), custom_call_target="tpu_custom_call" | custom-call | tf_op jit(solution)/shard_map/settle/pallas_call | solution.py:65
  (4 shorter events, 0.0 us)
Async XLA Ops:
  2.9 18.8 %all-to-all-start = ((f32[64,8,256]{2,1,0:T(8,128)}), f32[64,8,256]{2,1,0:T(8,128)S(1)}, u32[]{:S(2)}, u32[]{:S(2)}) async-start(f32[64,8,256]{2,1,0:T(8,128)} %get-tuple-element.22), calls=%async_computation | async-start | bytes 1048576 | tf_op jit(solution)/shard_map/all_to_all | solution.py:395
  10.8 9.5 %collective-permute-start = (f32[4,8,256]{2,1,0:T(8,128)}, f32[4,8,256]{2,1,0:T(8,128)S(1)}, u32[]{:S(2)}, u32[]{:S(2)}) collective-permute-start(f32[4,8,256]{2,1,0:T(8,128)} %get-tuple-element.20), channel_id=1, source_target_pairs={{0,32},{32,64},{64,96},{96,128},{128,160},{160,192},{192,224},{224... | collective-permute-start | bytes 98312 | tf_op jit(solution)/shard_map/ppermute | solution.py:415
  15.6 6.1 %collective-permute-start.1 = (f32[4,8,256]{2,1,0:T(8,128)}, f32[4,8,256]{2,1,0:T(8,128)S(1)}, u32[]{:S(2)}, u32[]{:S(2)}) collective-permute-start(f32[4,8,256]{2,1,0:T(8,128)} %get-tuple-element.21), channel_id=1, source_target_pairs={{32,0},{64,32},{96,64},{128,96},{160,128},{192,160},{224,192},{256... | collective-permute-start | bytes 98312 | tf_op jit(solution)/shard_map/ppermute | solution.py:416
  20.3 1.4 %copy-start.3 = (f32[4,8,256]{2,1,0:T(8,128)}, f32[4,8,256]{2,1,0:T(8,128)S(1)}, u32[]{:S(2)}) copy-start(f32[4,8,256]{2,1,0:T(8,128)S(1)} %collective-permute-done.refs_4_) | copy-start | bytes 98308
  21.7 0.6 copy-start.4
  21.7 0.8 copy-start.1
  34.5 26.2 %all-to-all-start.1 = ((f32[64,1,256]{2,1,0:T(1,128)}), f32[64,1,256]{2,1,0:T(1,128)S(1)}, u32[]{:S(2)}, u32[]{:S(2)}) async-start(f32[64,1,256]{2,1,0:T(1,128)} %get-tuple-element.33), calls=%async_computation.1 | async-start | bytes 131072 | tf_op jit(solution)/shard_map/all_to_all | solution.py:395
  43.3 17.3 %collective-permute-start.2 = (f32[4,1,256]{2,1,0:T(1,128)}, f32[4,1,256]{2,1,0:T(1,128)S(1)}, u32[]{:S(2)}, u32[]{:S(2)}) collective-permute-start(f32[4,1,256]{2,1,0:T(1,128)} %get-tuple-element.31), channel_id=1, source_target_pairs={{0,32},{32,64},{64,96},{96,128},{128,160},{160,192},{192,224},{224... | collective-permute-start | bytes 12296 | tf_op jit(solution)/shard_map/ppermute | solution.py:435
  45.7 15.0 %collective-permute-start.3 = (f32[4,1,256]{2,1,0:T(1,128)}, f32[4,1,256]{2,1,0:T(1,128)S(1)}, u32[]{:S(2)}, u32[]{:S(2)}) collective-permute-start(f32[4,1,256]{2,1,0:T(1,128)} %get-tuple-element.32), channel_id=1, source_target_pairs={{32,0},{64,32},{96,64},{128,96},{160,128},{192,160},{224,192},{256... | collective-permute-start | bytes 12296 | tf_op jit(solution)/shard_map/ppermute | solution.py:436
  60.6 0.6 copy-start.5
  60.6 0.6 copy-start.6
  60.7 0.6 copy-start.2
  76.8 26.2 %all-to-all-start.2 = ((f32[64,8,256]{2,1,0:T(8,128)}), f32[64,8,256]{2,1,0:T(8,128)S(1)}, u32[]{:S(2)}, u32[]{:S(2)}) async-start(f32[64,8,256]{2,1,0:T(8,128)} %get-tuple-element.35), calls=%async_computation.2 | async-start | bytes 1048576 | tf_op jit(solution)/shard_map/all_to_all | solution.py:395
  103.1 0.9 copy-start

commit v4 on v3

--- a/solution.py
+++ b/solution.py
@@ -8,6 +8,7 @@
 RIM = 4
 SLOTS = 2
 MOVERS = 16
+STEP = 8
 STIFFNESS = 2.0
 REST_DENSITY = 0.8
 VISCOSITY = 0.5
@@ -174,14 +175,14 @@
     moves.save(5, 6, 7)
 
     def cell(i, carry):
-        for c in (2 * i, 2 * i + 1):
+        for c in [STEP * i + k for k in range(STEP)]:
             total = jnp.zeros((8, width), F32)
             for _, w in weigh(near, tab, mine, c):
                 total = total + jnp.sum((w * w * w).reshape(width // 8, 8, width), axis=0)
             rho[pl.ds(c, 1), :] = jnp.sum(total, axis=0, keepdims=True)
         return carry
 
-    lax.fori_loop(0, cells // 2, cell, 0)
+    lax.fori_loop(0, cells // STEP, cell, 0)
     lane = lax.broadcasted_iota(jnp.int32, (1, width), 1)
     for c in range(cells):
         row = rho[c : c + 1, :]
@@ -217,30 +218,59 @@
     return jnp.concatenate(rows, 0).astype(BF16)
 
 
-def pair_sums(near, tab, mine, feat1, feat2, c, sub):
-    feats1, feats2, odd, even = [], [], [], []
-    for row, w in weigh(near, tab, mine, c):
+class Pairs:
+    def __init__(self, near, tab, mine, feat1, feat2):
+        self.near, self.tab, self.mine, self.feat1, self.feat2 = near, tab, mine, feat1, feat2
+
+    def row(self, c, k):
+        return RIM + c if k == 0 else self.near[k - 1, c]
+
+    def make(self, c, k, part, odd, even):
+        width = odd.shape[1] // 2
+        half = width // 2
+        source = self.tab[self.row(c, k), :, part * half : part * half + half]
+        w = jnp.maximum(contract(source, self.mine[c], 0), 0.0)
         square = w * w
-        if feat1 is not None:
-            feats1.append(feat1[row])
-            odd.append(jnp.concatenate([w.astype(BF16), (square * w).astype(BF16)], 1))
-        if feat2 is not None:
-            feats2.append(feat2[row])
-            high = square.astype(BF16)
-            low = (square - high.astype(F32)).astype(BF16)
-            even.append(jnp.concatenate([high, low], 1))
-    first = second = None
-    if feat1 is not None:
-        first = contract(jnp.concatenate(feats1, 1), jnp.concatenate(odd, 0), 1)
+        once, high = w.astype(BF16), square.astype(BF16)
+        rows = slice(k * width + part * half, k * width + part * half + half)
+        odd[rows, :width] = once
+        odd[rows, width:] = once * high
+        even[rows, :width] = high
+        even[rows, width:] = (square - high.astype(F32)).astype(BF16)
+
+    def fill(self, c, odd, even):
+        for k in range(self.near.shape[0] + 1):
+            self.make(c, k, 0, odd, even)
+            self.make(c, k, 1, odd, even)
+
+    def step(self, c, odd, even, later, next_odd, next_even, sub):
+        width = odd.shape[1] // 2
+        first = second = 0.0
+        for k in range(self.near.shape[0] + 1):
+            row = self.row(c, k)
+            rows = slice(k * width, k * width + width)
+            self.make(later, k, 0, next_odd, next_even)
+            first = first + contract(self.feat1[row], odd[rows], 1)
+            self.make(later, k, 1, next_odd, next_even)
+            second = second + contract(self.feat2[row], even[rows], 1)
         first = first[0:8] + first[8:16]
-        width = first.shape[1] // 2
         first = jnp.where(sub < 4, first[:, :width], first[:, width:])
-    if feat2 is not None:
-        second = contract(jnp.concatenate(feats2, 1), jnp.concatenate(even, 0), 1)
-        width = second.shape[1] // 2
         second = second[:, :width] + second[:, width:]
-        second = second[0:8] + second[8:16] + second[16:24]
-    return first, second
+        return first, second[0:8] + second[8:16] + second[16:24]
+
+
+def sweep(pairs, order, count, buffers, finish, sub):
+    a, b = buffers[0:2], buffers[2:4]
+    pairs.fill(order[0], *a)
+
+    def two(t, carry):
+        for i, now, then in ((2 * t, a, b), (2 * t + 1, b, a)):
+            c = order[i]
+            later = order[jnp.minimum(i + 1, count - 1)]
+            finish(i, c, *pairs.step(c, *now, later, *then, sub))
+        return carry
+
+    lax.fori_loop(0, count // 2, two, 0)
 
 
 def advance(first, second, tile, row_q, row_rho, row_fluid, active, sub):
@@ -267,28 +297,9 @@
     )
 
 
-def forces_early(moves, near, movers, tiles, tab, mine, early, feat1):
-    sub, _ = rows_and_lanes(tiles.shape[2])
-    moves.need(0, 1, 2)
-
-    def source(i, carry):
-        feat1[i] = first_features(tiles[i], sub)
-        return carry
-
-    lax.fori_loop(0, tiles.shape[0], source, 0, unroll=8)
-    moves.save(1)
-    moves.need(3, 4)
-
-    def cell(i, carry):
-        early[i], _ = pair_sums(near, tab, mine, feat1, None, movers[i], sub)
-        return carry
-
-    lax.fori_loop(0, early.shape[0], cell, 0)
-
-
-def forces_late(
-    moves, counts, near, movers, outs, tiles, q, rho, fluid, tab, mine, early, q_below, q_above, q_rest,
-    outbox, feat2, moved,
+def forces_moving(
+    moves, counts, near, movers, outs, tiles, q, rho, fluid, tab, mine, q_below, q_above, q_rest,
+    outbox, feat1, feat2, moved, *buffers,
 ):
     sub, lane = rows_and_lanes(tiles.shape[2])
     moves.need(4, 5)
@@ -296,45 +307,41 @@
 
         def source(i, carry, start=start, q_ref=q_ref):
             row_q = q_ref[i] if q_ref.ndim == 3 else q_ref[pl.ds(i, 1), :]
-            feat2[start + i] = second_features(tiles[start + i], row_q, sub)
+            tile = tiles[start + i]
+            feat1[start + i] = first_features(tile, sub)
+            feat2[start + i] = second_features(tile, row_q, sub)
             return carry
 
         lax.fori_loop(0, q_ref.shape[0], source, 0, unroll=4)
 
-    moves.save(1)
-    moves.need(*range(11))
-
-    def cell(i, carry):
-        c = movers[i]
-        _, second = pair_sums(near, tab, mine, None, feat2, c, sub)
+    moves.save(1, 2)
+    moves.need(*range(10))
+
+    def finish(i, c, first, second):
         row = pl.ds(c, 1)
         moved[i] = advance(
-            early[i], second, tiles[RIM + c], q[row, :], rho[row, :], fluid[row, :], lane < counts[c], sub
+            first, second, tiles[RIM + c], q[row, :], rho[row, :], fluid[row, :], lane < counts[c], sub
         )
-        return carry
-
-    lax.fori_loop(0, early.shape[0], cell, 0)
+
+    sweep(Pairs(near, tab, mine, feat1, feat2), movers, MOVERS, buffers, finish, sub)
     for t in range(outbox.shape[0] // SLOTS):
         for k in range(SLOTS):
             outbox[t * SLOTS + k] = moved[outs[t, k]]
 
 
 def forces_staying(
-    moves, counts, near, stayers, tiles, q, rho, fluid, tab, mine, feat1, feat2, stayed
+    moves, counts, near, stayers, tiles, q, rho, fluid, tab, mine, feat1, feat2, stayed, *buffers
 ):
     sub, lane = rows_and_lanes(tiles.shape[2])
     moves.need(*range(11))
 
-    def cell(i, carry):
-        c = stayers[i]
-        first, second = pair_sums(near, tab, mine, feat1, feat2, c, sub)
+    def finish(i, c, first, second):
         row = pl.ds(c, 1)
         stayed[i] = advance(
             first, second, tiles[RIM + c], q[row, :], rho[row, :], fluid[row, :], lane < counts[c], sub
         )
-        return carry
-
-    lax.fori_loop(0, stayed.shape[0], cell, 0)
+
+    sweep(Pairs(near, tab, mine, feat1, feat2), stayers, stayed.shape[0], buffers, finish, sub)
 
 
 def settle(moves, first, arrived, stayed, inbox, state, density):
@@ -434,22 +441,20 @@
     q_rest = exchange(send_q)
     q_below = lax.ppermute(q_tail, "group", up)
     q_above = lax.ppermute(q_head, "group", down)
-    early, feat1 = call(
-        forces_early,
-        4096,
-        [near, movers],
-        [tiles, tab, mine],
-        [],
-        [((MOVERS, 8, width), F32), ((total, 16, width), BF16)],
-    )
-    outbox, feat2 = call(
-        forces_late,
+    partners = neighbours.shape[1] + 1
+    buffers = [pltpu.VMEM((partners * width, 2 * width), BF16)] * 4
+    outbox, feat1, feat2 = call(
+        forces_moving,
         4096,
         [counts, near, movers, outs],
-        [tiles, q, rho, fluid, tab, mine, early],
+        [tiles, q, rho, fluid, tab, mine],
         [q_below, q_above, q_rest],
-        [((SLOTS * peers, 8, width), F32), ((total, 32, width), BF16)],
-        [pltpu.VMEM((MOVERS, 8, width), F32)],
+        [
+            ((SLOTS * peers, 8, width), F32),
+            ((total, 16, width), BF16),
+            ((total, 32, width), BF16),
+        ],
+        [pltpu.VMEM((MOVERS, 8, width), F32)] + buffers,
     )
     inbox = exchange(outbox)
     [stayed] = call(
@@ -459,6 +464,7 @@
         [tiles, q, rho, fluid, tab, mine, feat1, feat2],
         [],
         [((cells - MOVERS, 8, width), F32)],
+        buffers,
     )
     return call(
         settle,

time: 107 us -> 86.5 us (0.81)
  Pallas kernels: 60.1 us -> 37.5 us
  waiting for transfers between devices: 1.37 us -> 2.83 us
    pallas_call x6 -> x5, Pallas kernels: 60.1 us -> 37.5 us  [call(): pl.pallas_call(body, out_shape=[jax.ShapeDtypeStruct(*o) for o in outs],...]
    ppermute x1, waiting for transfers between devices: 0.01 us -> 1.45 us  [shards(): q_above = lax.ppermute(q_head, 'group', down)]
  transfers between devices with their start and end apart: 7 -> 7, of which waited for: 1 -> 2; matrix products, arithmetic and copies ran while one was open for 5% -> 6% of each run, Pallas kernels for 26% -> 14%
where the time goes in v4:
time: 86.5 us; the launch traced here: 85.9 us
  starting transfers between devices  37.6 us (43%)
  Pallas kernels  37.5 us (43%)
  local copies, waits for them, and re-layouts  3.67 us (4%)
  other arithmetic  3.56 us (4%)
  waiting for transfers between devices  2.83 us (3%)
    pallas_call x5, Pallas kernels, call(): pl.pallas_call(body, out_shape=[jax.ShapeDtypeStruct(*o) for o in outs],...  37.5 us
    all_to_all x3, starting transfers between devices, exchange(): return lax.all_to_all(x, 'dev', split_axis=0, concat_axis=0, tiled=True)  25.6 us
    ppermute x1, starting transfers between devices, shards(): below = lax.ppermute(tail, 'group', up)  4.76 us
    ppermute x1, starting transfers between devices, shards(): q_above = lax.ppermute(q_head, 'group', down)  2.91 us
    unnamed x15, local copies, waits for them, and re-layouts  2.91 us
    ppermute x1, starting transfers between devices, shards(): q_below = lax.ppermute(q_tail, 'group', up)  2.37 us
    ppermute x1, starting transfers between devices, shards(): above = lax.ppermute(head, 'group', down)  1.92 us
  transfers between devices with their start and end apart: 7, of which 2 were waited for; matrix products, arithmetic and copies ran while one was open for 6% of the time, Pallas kernels for 14%

profile of v4, /device:TPU:227, one launch (start us, length us, event | category | flops | bytes accessed | tf_op | source)
XLA Modules:
  0.0 85.9 jit_solution(3714904059340429619)
XLA Ops:
  0.6 2.2 %prepare.1 = (f32[32,8,256]{2,1,0:T(8,128)}, f32[64,8,256]{2,1,0:T(8,128)}, f32[4,8,256]{2,1,0:T(8,128)}, f32[4,8,256]{2,1,0:T(8,128)}, f32[32,256]{1,0:T(8,128)}) custom-call(s32[32]{0:T(128)} %refs_0_.7, s32[1,1,2,32]{3,2,1,0:T(2,128)} %bitcast.6, f32[3,32,256]{2,1,0:T(8,128)} %refs_2_.1, f32[3,32,256]{2,1,0:T(8,128)} %refs_3_.1, f32[32,256]{1,0:T(8,128)} %refs_4_.1, ...), custom_call_target="tpu_custom_call" | custom-call | tf_op jit(solution)/shard_map/prepare/pallas_call | solution.py:66
  2.9 7.9 %all-to-all-start = ((f32[64,8,256]{2,1,0:T(8,128)}), f32[64,8,256]{2,1,0:T(8,128)S(1)}, u32[]{:S(2)}, u32[]{:S(2)}) async-start(f32[64,8,256]{2,1,0:T(8,128)} %get-tuple-element.21), calls=%async_computation | async-start | bytes 1048576 | tf_op jit(solution)/shard_map/all_to_all | solution.py:402
  10.8 4.8 %collective-permute-start = (f32[4,8,256]{2,1,0:T(8,128)}, f32[4,8,256]{2,1,0:T(8,128)S(1)}, u32[]{:S(2)}, u32[]{:S(2)}) collective-permute-start(f32[4,8,256]{2,1,0:T(8,128)} %get-tuple-element.19), channel_id=1, source_target_pairs={{0,32},{32,64},{64,96},{96,128},{128,160},{160,192},{192,224},{224... | collective-permute-start | bytes 98312 | tf_op jit(solution)/shard_map/ppermute | solution.py:422
  15.6 1.9 %collective-permute-start.1 = (f32[4,8,256]{2,1,0:T(8,128)}, f32[4,8,256]{2,1,0:T(8,128)S(1)}, u32[]{:S(2)}, u32[]{:S(2)}) collective-permute-start(f32[4,8,256]{2,1,0:T(8,128)} %get-tuple-element.20), channel_id=1, source_target_pairs={{32,0},{64,32},{96,64},{128,96},{160,128},{192,160},{224,192},{256... | collective-permute-start | bytes 98312 | tf_op jit(solution)/shard_map/ppermute | solution.py:423
  17.5 0.6 broadcast.75
  18.1 1.4 %reduce.3 = s32[1024]{0:T(1024)S(1)} reduce(s32[1,1024]{1,0:T(1,128)} %param.15, s32[]{:T(128)} %broadcast.75), dimensions={0}, to_apply=%param.15.reduce_sub_computation.3 | reduce | bytes 8196 | tf_op args[7]
  19.5 0.1 reshape_squeeze.3
  19.6 0.1 select_reduce_fusion.1
  19.7 0.2 convert_reduce_fusion
  19.9 0.2 convert_reduce_fusion.1
  20.1 0.2 select_reduce_fusion
  20.3 0.0 collective-permute-done.refs_4_
  20.3 0.0 copy-start.3
  20.3 1.4 %collective-permute-done.1.refs_5_ = f32[4,8,256]{2,1,0:T(8,128)S(1)} collective-permute-done((f32[4,8,256]{2,1,0:T(8,128)}, f32[4,8,256]{2,1,0:T(8,128)S(1)}, u32[]{:S(2)}, u32[]{:S(2)}) %collective-permute-start.1) | collective-permute-done | bytes 32800 | tf_op jit(solution)/shard_map/ppermute | solution.py:423
  21.7 0.0 copy-start.4
  21.7 0.0 all-to-all-done.refs_6_
  21.7 0.0 copy-start.1
  21.7 0.0 copy-done.3
  21.7 0.6 copy-done.4
  22.3 0.2 copy-done.1
  22.4 9.6 %densities.1 = (f32[32,256]{1,0:T(8,128)}, f32[32,256]{1,0:T(8,128)}, f32[4,1,256]{2,1,0:T(1,128)}, f32[4,1,256]{2,1,0:T(1,128)}, f32[64,1,256]{2,1,0:T(1,128)},...) custom-call(s32[32]{0:T(128)} %refs_0_.7, s32[3,32]{1,0:T(4,128)} %bitcast.3, ...), custom_call_target="tpu_custom_call" | custom-call | tf_op jit(solution)/shard_map/densities/pallas_call | solution.py:66
  32.1 8.8 %all-to-all-start.1 = ((f32[64,1,256]{2,1,0:T(1,128)}), f32[64,1,256]{2,1,0:T(1,128)S(1)}, u32[]{:S(2)}, u32[]{:S(2)}) async-start(f32[64,1,256]{2,1,0:T(1,128)} %get-tuple-element.30), calls=%async_computation.1 | async-start | bytes 131072 | tf_op jit(solution)/shard_map/all_to_all | solution.py:402
  40.9 2.4 %collective-permute-start.2 = (f32[4,1,256]{2,1,0:T(1,128)}, f32[4,1,256]{2,1,0:T(1,128)S(1)}, u32[]{:S(2)}, u32[]{:S(2)}) collective-permute-start(f32[4,1,256]{2,1,0:T(1,128)} %get-tuple-element.28), channel_id=1, source_target_pairs={{0,32},{32,64},{64,96},{96,128},{128,160},{160,192},{192,224},{224... | collective-permute-start | bytes 12296 | tf_op jit(solution)/shard_map/ppermute | solution.py:442
  43.3 2.9 %collective-permute-start.3 = (f32[4,1,256]{2,1,0:T(1,128)}, f32[4,1,256]{2,1,0:T(1,128)S(1)}, u32[]{:S(2)}, u32[]{:S(2)}) collective-permute-start(f32[4,1,256]{2,1,0:T(1,128)} %get-tuple-element.29), channel_id=1, source_target_pairs={{32,0},{64,32},{96,64},{128,96},{160,128},{192,160},{224,192},{256... | collective-permute-start | bytes 12296 | tf_op jit(solution)/shard_map/ppermute | solution.py:443
  46.2 0.7 select_reduce_fusion.3
  46.9 0.7 copy.10.refs_3_
  47.6 0.0 collective-permute-done.2.refs_10_
  47.6 0.0 copy-start.5
  47.6 1.5 %collective-permute-done.3.refs_11_ = f32[4,1,256]{2,1,0:T(1,128)S(1)} collective-permute-done((f32[4,1,256]{2,1,0:T(1,128)}, f32[4,1,256]{2,1,0:T(1,128)S(1)}, u32[]{:S(2)}, u32[]{:S(2)}) %collective-permute-start.3) | collective-permute-done | bytes 4128 | tf_op jit(solution)/shard_map/ppermute | solution.py:443
  49.0 0.0 copy-start.6
  49.0 0.0 all-to-all-done.1.refs_12_
  49.0 0.0 copy-start.2
  49.0 0.0 copy-done.5
  49.0 0.6 copy-done.6
  49.6 0.0 copy-done.2
  49.7 11.8 %forces_moving.1 = (f32[64,8,256]{2,1,0:T(8,128)}, bf16[104,16,256]{2,1,0:T(8,128)(2,1)}, bf16[104,32,256]{2,1,0:T(8,128)(2,1)}) custom-call(s32[32]{0:T(128)} %refs_0_.7, s32[3,32]{1,0:T(4,128)} %bitcast.4, s32[16]{0:T(128)} %get-tuple-element.36.refs_2_, s32[32,2]{1,0:T(8,128)} %copy.10.refs_3_, f32[104,8,256]{2,1,0:T(8,128)} %get-tuple-element.22.refs_4_.refs_3_, ...), custom_call_target="tpu_custom_call" | custom-call | tf_op jit(solution)/shard_map/forces_moving/pallas_call | solution.py:66
  61.5 8.8 %all-to-all-start.2 = ((f32[64,8,256]{2,1,0:T(8,128)}), f32[64,8,256]{2,1,0:T(8,128)S(1)}, u32[]{:S(2)}, u32[]{:S(2)}) async-start(f32[64,8,256]{2,1,0:T(8,128)} %get-tuple-element.33), calls=%async_computation.2 | async-start | bytes 1048576 | tf_op jit(solution)/shard_map/all_to_all | solution.py:402
  70.4 0.1 select_reduce_fusion.2
  70.5 0.7 and_select_fusion
  71.1 11.6 %forces_staying.1.refs_2_ = f32[16,8,256]{2,1,0:T(8,128)} custom-call(s32[32]{0:T(128)} %refs_0_.7, s32[3,32]{1,0:T(4,128)} %bitcast.5, s32[16]{0:T(128)} %get-tuple-element.37.refs_2_, f32[104,8,256]{2,1,0:T(8,128)} %get-tuple-element.22.refs_4_.refs_3_, f32[32,256]{1,0:T(8,128)} %get-tuple-element.23.refs_5_.refs_4_, ...), custom_call_target="tpu_custom_call" | custom-call | tf_op jit(solution)/shard_map/forces_staying/pallas_call | solution.py:66
  82.8 0.0 all-to-all-done.2.refs_3_
  82.8 0.0 copy-start
  82.8 0.9 %copy-done = f32[16,8,256]{2,1,0:T(8,128)S(1)} copy-done((f32[16,8,256]{2,1,0:T(8,128)S(1)}, f32[16,8,256]{2,1,0:T(8,128)}, u32[]{:S(2)}) %copy-start) | copy-done | bytes 131096
  83.7 2.2 %settle.1 = (f32[6,32,256]{2,1,0:T(8,128)}, f32[32,256]{1,0:T(8,128)}) custom-call(s32[1]{0:T(128)} %bitcast.refs_0_, s32[32]{0:T(128)S(1)} %get-tuple-element.40.refs_1_, f32[16,8,256]{2,1,0:T(8,128)S(1)} %copy-done, f32[64,8,256]{2,1,0:T(8,128)S(1)} %all-to-all-done.2.refs_3_), custom_call_target="tpu_custom_call" | custom-call | tf_op jit(solution)/shard_map/settle/pallas_call | solution.py:66
  (4 shorter events, 0.0 us)
Async XLA Ops:
  2.9 18.8 %all-to-all-start = ((f32[64,8,256]{2,1,0:T(8,128)}), f32[64,8,256]{2,1,0:T(8,128)S(1)}, u32[]{:S(2)}, u32[]{:S(2)}) async-start(f32[64,8,256]{2,1,0:T(8,128)} %get-tuple-element.21), calls=%async_computation | async-start | bytes 1048576 | tf_op jit(solution)/shard_map/all_to_all | solution.py:402
  10.8 9.5 %collective-permute-start = (f32[4,8,256]{2,1,0:T(8,128)}, f32[4,8,256]{2,1,0:T(8,128)S(1)}, u32[]{:S(2)}, u32[]{:S(2)}) collective-permute-start(f32[4,8,256]{2,1,0:T(8,128)} %get-tuple-element.19), channel_id=1, source_target_pairs={{0,32},{32,64},{64,96},{96,128},{128,160},{160,192},{192,224},{224... | collective-permute-start | bytes 98312 | tf_op jit(solution)/shard_map/ppermute | solution.py:422
  15.6 6.1 %collective-permute-start.1 = (f32[4,8,256]{2,1,0:T(8,128)}, f32[4,8,256]{2,1,0:T(8,128)S(1)}, u32[]{:S(2)}, u32[]{:S(2)}) collective-permute-start(f32[4,8,256]{2,1,0:T(8,128)} %get-tuple-element.20), channel_id=1, source_target_pairs={{32,0},{64,32},{96,64},{128,96},{160,128},{192,160},{224,192},{256... | collective-permute-start | bytes 98312 | tf_op jit(solution)/shard_map/ppermute | solution.py:423
  20.3 1.4 %copy-start.3 = (f32[4,8,256]{2,1,0:T(8,128)}, f32[4,8,256]{2,1,0:T(8,128)S(1)}, u32[]{:S(2)}) copy-start(f32[4,8,256]{2,1,0:T(8,128)S(1)} %collective-permute-done.refs_4_) | copy-start | bytes 98308
  21.7 0.6 copy-start.4
  21.7 0.8 copy-start.1
  32.1 17.0 %all-to-all-start.1 = ((f32[64,1,256]{2,1,0:T(1,128)}), f32[64,1,256]{2,1,0:T(1,128)S(1)}, u32[]{:S(2)}, u32[]{:S(2)}) async-start(f32[64,1,256]{2,1,0:T(1,128)} %get-tuple-element.30), calls=%async_computation.1 | async-start | bytes 131072 | tf_op jit(solution)/shard_map/all_to_all | solution.py:402
  40.9 6.7 %collective-permute-start.2 = (f32[4,1,256]{2,1,0:T(1,128)}, f32[4,1,256]{2,1,0:T(1,128)S(1)}, u32[]{:S(2)}, u32[]{:S(2)}) collective-permute-start(f32[4,1,256]{2,1,0:T(1,128)} %get-tuple-element.28), channel_id=1, source_target_pairs={{0,32},{32,64},{64,96},{96,128},{128,160},{160,192},{192,224},{224... | collective-permute-start | bytes 12296 | tf_op jit(solution)/shard_map/ppermute | solution.py:442
  43.3 5.8 %collective-permute-start.3 = (f32[4,1,256]{2,1,0:T(1,128)}, f32[4,1,256]{2,1,0:T(1,128)S(1)}, u32[]{:S(2)}, u32[]{:S(2)}) collective-permute-start(f32[4,1,256]{2,1,0:T(1,128)} %get-tuple-element.29), channel_id=1, source_target_pairs={{32,0},{64,32},{96,64},{128,96},{160,128},{192,160},{224,192},{256... | collective-permute-start | bytes 12296 | tf_op jit(solution)/shard_map/ppermute | solution.py:443
  47.6 1.5 %copy-start.5 = (f32[4,1,256]{2,1,0:T(1,128)}, f32[4,1,256]{2,1,0:T(1,128)S(1)}, u32[]{:S(2)}) copy-start(f32[4,1,256]{2,1,0:T(1,128)S(1)} %collective-permute-done.2.refs_10_) | copy-start | bytes 12292
  49.0 0.6 copy-start.6
  49.0 0.6 copy-start.2
  61.5 21.3 %all-to-all-start.2 = ((f32[64,8,256]{2,1,0:T(8,128)}), f32[64,8,256]{2,1,0:T(8,128)S(1)}, u32[]{:S(2)}, u32[]{:S(2)}) async-start(f32[64,8,256]{2,1,0:T(8,128)} %get-tuple-element.33), calls=%async_computation.2 | async-start | bytes 1048576 | tf_op jit(solution)/shard_map/all_to_all | solution.py:402
  82.8 0.9 %copy-start = (f32[16,8,256]{2,1,0:T(8,128)S(1)}, f32[16,8,256]{2,1,0:T(8,128)}, u32[]{:S(2)}) copy-start(f32[16,8,256]{2,1,0:T(8,128)} %forces_staying.1.refs_2_) | copy-start | bytes 393220

commit v5 on v4

--- a/solution.py
+++ b/solution.py
@@ -9,6 +9,7 @@
 SLOTS = 2
 MOVERS = 16
 STEP = 8
+JOB_ROW, JOB_CELL, JOB_COUNT, MOVING, STAYING, OUTS, PLAN = 0, 128, 256, 272, 304, 336, 512
 STIFFNESS = 2.0
 REST_DENSITY = 0.8
 VISCOSITY = 0.5
@@ -43,15 +44,18 @@
                 self.outs[i].start()
 
 
-def call(kernel, room, ints, held, near, outs, scratch=()):
+def call(kernel, room, ints, held, near, outs, scratch=(), into=()):
     n_in, n_near, n_out = len(ints) + len(held), len(near), len(outs)
 
     def body(*refs):
         sources, refs = refs[:n_in], refs[n_in:]
         close, refs = refs[:n_near], refs[n_near:]
         targets, refs = refs[:n_out], refs[n_out:]
-        inner, refs = refs[:n_in], refs[n_in:]
+        inner, refs = list(refs[: n_in - len(into)]), refs[n_in - len(into) :]
         results, refs = refs[:n_out], refs[n_out:]
+        for i, (out, start) in enumerate(into):
+            rows = pl.ds(start, held[i].shape[0])
+            inner.insert(len(ints) + i, results[out].at[rows])
         in_sems, out_sems, rest = refs[0], refs[1], refs[2:]
         moves = Moves(
             [pltpu.make_async_copy(a, b, in_sems.at[i]) for i, (a, b) in enumerate(zip(sources, inner))],
@@ -69,8 +73,8 @@
         in_specs=[HBM] * n_in + [VMEM] * n_near,
         out_specs=[HBM] * n_out,
         scratch_shapes=[pltpu.SMEM(x.shape, x.dtype) for x in ints]
-        + [pltpu.VMEM(x.shape, x.dtype) for x in held]
-        + [pltpu.VMEM(*o) for o in outs]
+        + [pltpu.VMEM(x.shape, x.dtype) for x in held[len(into) :]]
+        + [(pltpu.SMEM if len(o[0]) == 1 else pltpu.VMEM)(*o) for o in outs]
         + [pltpu.SemaphoreType.DMA((n_in,)), pltpu.SemaphoreType.DMA((n_out,))]
         + list(scratch),
         compiler_params=pltpu.CompilerParams(vmem_limit_bytes=(64 << 20) - (room << 10)),
@@ -126,66 +130,149 @@
         start += ref.shape[0]
 
 
-def weigh(near, tab, mine, c):
-    for k in range(near.shape[0] + 1):
-        row = RIM + c if k == 0 else near[k - 1, c]
-        yield row, jnp.maximum(contract(tab[row], mine[c], 0), 0.0)
+def squared(tile, sub):
+    return jnp.sum(jnp.where(sub < 3, tile * tile, 0.0), axis=0, keepdims=True)
+
+
+def source_rows(tile, sub):
+    root = tile[3:4]
+    far = root * (1.0 - 0.25 * squared(tile, sub))
+    value = jnp.where(
+        sub < 3,
+        tile * (0.5 * root),
+        jnp.where(sub == 3, far, jnp.where(sub == 4, -0.25 * root, 0.0)),
+    )
+    a, b, c = pieces(value, 3)
+    return jnp.concatenate([a, b, a, c, a, b], 0).astype(BF16)
+
+
+def target_rows(tile, sub):
+    value = jnp.where(
+        sub < 3,
+        tile,
+        jnp.where(sub == 3, 1.0, jnp.where(sub == 4, squared(tile, sub), 0.0)),
+    )
+    a, b, c = pieces(value, 3)
+    return jnp.concatenate([a, a, b, a, c, b], 0).astype(BF16)
+
+
+def cubes(source, target):
+    w = jnp.maximum(contract(source, target, 0), 0.0)
+    return jnp.sum((w * w * w).reshape(w.shape[0] // 8, 8, w.shape[1]), axis=0)
+
+
+def run_jobs(rows, cells, count, tab, first_row, mine, sums):
+    last = mine.shape[0] - 1
+
+    def some(t, carry):
+        for k in range(STEP):
+            c = cells(t * STEP + k)
+            value = cubes(tab[rows(t * STEP + k) - first_row], mine[jnp.minimum(c, last)])
+            sums[c] = sums[c] + value
+        return carry
+
+    lax.fori_loop(0, lax.div(count + (STEP - 1), STEP), some, 0)
+
+
+def home(moves, near, owners, tiles, owners_v, sums, tab, mine, plan, landing, jobs, seen):
+    cells, _, width = tiles.shape
+    sub, _ = rows_and_lanes(width)
+    me = lax.axis_index("dev")
+    moves.need(0, 2)
+
+    def build(i, carry):
+        tab[i] = source_rows(tiles[i], sub)
+        mine[i] = target_rows(tiles[i], sub)
+        return carry
+
+    lax.fori_loop(0, cells, build, 0, unroll=4)
+    moves.save(1, 2)
+
+    def alone(t, carry):
+        for k in range(STEP):
+            c = t * STEP + k
+            sums[c] = cubes(tab[c], mine[c])
+        return carry
+
+    lax.fori_loop(0, cells // STEP, alone, 0)
+    sums[cells] = jnp.zeros((8, width), F32)
+    local, away = jnp.int32(0), jnp.int32(0)
+    for k in range(near.shape[0]):
+        for c in range(cells):
+            row = near[k, c]
+            inside = (row >= RIM) & (row < RIM + cells)
+            jobs[local] = row
+            jobs[128 + local] = c
+            plan[JOB_ROW + away] = row
+            plan[JOB_CELL + away] = c
+            local = local + inside.astype(jnp.int32)
+            away = away + 1 - inside.astype(jnp.int32)
+    for k in range(STEP):
+        jobs[local + k] = RIM
+        jobs[128 + local + k] = cells
+        plan[JOB_ROW + away + k] = RIM
+        plan[JOB_CELL + away + k] = cells
+    plan[JOB_COUNT] = away
+    run_jobs(lambda i: jobs[i], lambda i: jobs[128 + i], local, tab, RIM, mine, sums)
+    moves.save(0)
+
+    moves.need(1, 3)
+    for d in range(seen.shape[0]):
+        seen[d] = 0
+    for i in range(seen.shape[0] * SLOTS):
+        plan[OUTS + i] = 0
+    moving, staying = jnp.int32(0), jnp.int32(0)
+    for c in range(cells):
+        to = owners[0, me * cells + c]
+        leaves = (to != me).astype(jnp.int32)
+        plan[MOVING + moving] = c
+        plan[STAYING + staying] = c
+        spot = jnp.where(to != me, to * SLOTS + seen[to], seen.shape[0] * SLOTS)
+        plan[OUTS + spot] = moving
+        seen[to] = seen[to] + leaves
+        moving = moving + leaves
+        staying = staying + 1 - leaves
+    moves.save(3)
+    entries = owners_v.shape[1]
+    dev = lax.broadcasted_iota(jnp.int32, (entries, 128), 1)
+    entry = lax.broadcasted_iota(jnp.int32, (entries, 128), 0)
+    belongs = (entry >= dev * cells) & (entry < dev * cells + cells)
+    ours = jnp.broadcast_to((owners_v[...] == me).astype(F32), (8, entries)).astype(BF16)
+    arrivals = contract(ours, jnp.where(belongs, 1.0, 0.0).astype(BF16), 1)
+    earlier = lax.broadcasted_iota(jnp.int32, (128, 128), 0) < lax.broadcasted_iota(
+        jnp.int32, (128, 128), 1
+    )
+    before = contract(arrivals.astype(BF16), jnp.where(earlier, 1.0, 0.0).astype(BF16), 1)
+    lane = lax.broadcasted_iota(jnp.int32, (8, 128), 1)
+    kind = lax.broadcasted_iota(jnp.int32, (8, 128), 0)
+    place = before.astype(jnp.int32)
+    comes = (arrivals > 0.0) & (lane != me)
+    landing[...] = jnp.where((kind == 0) & ~comes, cells, place)
 
 
 def densities(
-    moves, counts, near, sends, own, below, above, rest, rho, q, q_head, q_tail, send_q, tab, mine, tiles,
+    moves, counts, plan, sends, tab_own, tiles_own, mine, sums, below, above, rest,
+    rho, q, q_head, q_tail, send_q, tab, tiles,
 ):
-    moves.need(0, 1, 2, 3)
-    cells, _, width = own.shape
-    sub = lax.broadcasted_iota(jnp.int32, (8, width), 0)
-
-    def squared(tile):
-        return jnp.sum(jnp.where(sub < 3, tile * tile, 0.0), axis=0, keepdims=True)
-
-    for start, ref in segments(below, own, above, rest):
+    cells, _, width = mine.shape
+    sub, lane = rows_and_lanes(width)
+    for start, ref in ((0, below), (RIM + cells, above), (2 * RIM + cells, rest)):
 
         def source(i, carry, start=start, ref=ref):
             tile = ref[i]
-            root = tile[3:4]
-            far = root * (1.0 - 0.25 * squared(tile))
-            value = jnp.where(
-                sub < 3,
-                tile * (0.5 * root),
-                jnp.where(sub == 3, far, jnp.where(sub == 4, -0.25 * root, 0.0)),
-            )
-            a, b, c = pieces(value, 3)
-            tab[start + i] = jnp.concatenate([a, b, a, c, a, b], 0).astype(BF16)
+            tab[start + i] = source_rows(tile, sub)
             tiles[start + i] = tile
             return carry
 
         lax.fori_loop(0, ref.shape[0], source, 0, unroll=4)
 
-    def target(i, carry):
-        tile = own[i]
-        value = jnp.where(
-            sub < 3,
-            tile,
-            jnp.where(sub == 3, 1.0, jnp.where(sub == 4, squared(tile), 0.0)),
-        )
-        a, b, c = pieces(value, 3)
-        mine[i] = jnp.concatenate([a, a, b, a, c, b], 0).astype(BF16)
-        return carry
-
-    lax.fori_loop(0, cells, target, 0, unroll=4)
-    moves.save(5, 6, 7)
-
-    def cell(i, carry):
-        for c in [STEP * i + k for k in range(STEP)]:
-            total = jnp.zeros((8, width), F32)
-            for _, w in weigh(near, tab, mine, c):
-                total = total + jnp.sum((w * w * w).reshape(width // 8, 8, width), axis=0)
-            rho[pl.ds(c, 1), :] = jnp.sum(total, axis=0, keepdims=True)
-        return carry
-
-    lax.fori_loop(0, cells // STEP, cell, 0)
-    lane = lax.broadcasted_iota(jnp.int32, (1, width), 1)
+    moves.need(*range(7))
+    moves.save(5, 6)
+    run_jobs(
+        lambda i: plan[JOB_ROW + i], lambda i: plan[JOB_CELL + i], plan[JOB_COUNT], tab, 0, mine, sums
+    )
     for c in range(cells):
-        row = rho[c : c + 1, :]
+        row = jnp.sum(sums[c], axis=0, keepdims=True)
         active = lane < counts[c]
         safe = jnp.where(active, row, 1.0)
         value = STIFFNESS * (row - REST_DENSITY) / (safe * safe)
@@ -259,14 +346,14 @@
         return first, second[0:8] + second[8:16] + second[16:24]
 
 
-def sweep(pairs, order, count, buffers, finish, sub):
+def sweep(pairs, order, start, count, buffers, finish, sub):
     a, b = buffers[0:2], buffers[2:4]
-    pairs.fill(order[0], *a)
+    pairs.fill(order[start], *a)
 
     def two(t, carry):
         for i, now, then in ((2 * t, a, b), (2 * t + 1, b, a)):
-            c = order[i]
-            later = order[jnp.minimum(i + 1, count - 1)]
+            c = order[start + i]
+            later = order[start + jnp.minimum(i + 1, count - 1)]
             finish(i, c, *pairs.step(c, *now, later, *then, sub))
         return carry
 
@@ -298,11 +385,11 @@
 
 
 def forces_moving(
-    moves, counts, near, movers, outs, tiles, q, rho, fluid, tab, mine, q_below, q_above, q_rest,
+    moves, counts, near, plan, tiles, q, rho, fluid, tab, mine, q_below, q_above, q_rest,
     outbox, feat1, feat2, moved, *buffers,
 ):
     sub, lane = rows_and_lanes(tiles.shape[2])
-    moves.need(4, 5)
+    moves.need(3, 4)
     for start, q_ref in segments(q_below, q, q_above, q_rest):
 
         def source(i, carry, start=start, q_ref=q_ref):
@@ -315,7 +402,7 @@
         lax.fori_loop(0, q_ref.shape[0], source, 0, unroll=4)
 
     moves.save(1, 2)
-    moves.need(*range(10))
+    moves.need(*range(9))
 
     def finish(i, c, first, second):
         row = pl.ds(c, 1)
@@ -323,14 +410,16 @@
             first, second, tiles[RIM + c], q[row, :], rho[row, :], fluid[row, :], lane < counts[c], sub
         )
 
-    sweep(Pairs(near, tab, mine, feat1, feat2), movers, MOVERS, buffers, finish, sub)
+    sweep(
+        Pairs(near, tab, mine, feat1, feat2), plan, MOVING, MOVERS, buffers, finish, sub
+    )
     for t in range(outbox.shape[0] // SLOTS):
         for k in range(SLOTS):
-            outbox[t * SLOTS + k] = moved[outs[t, k]]
+            outbox[t * SLOTS + k] = moved[plan[OUTS + t * SLOTS + k]]
 
 
 def forces_staying(
-    moves, counts, near, stayers, tiles, q, rho, fluid, tab, mine, feat1, feat2, stayed, *buffers
+    moves, counts, near, plan, tiles, q, rho, fluid, tab, mine, feat1, feat2, stayed, *buffers
 ):
     sub, lane = rows_and_lanes(tiles.shape[2])
     moves.need(*range(11))
@@ -341,12 +430,15 @@
             first, second, tiles[RIM + c], q[row, :], rho[row, :], fluid[row, :], lane < counts[c], sub
         )
 
-    sweep(Pairs(near, tab, mine, feat1, feat2), stayers, stayed.shape[0], buffers, finish, sub)
-
-
-def settle(moves, first, arrived, stayed, inbox, state, density):
+    sweep(
+        Pairs(near, tab, mine, feat1, feat2), plan, STAYING, stayed.shape[0], buffers, finish, sub
+    )
+
+
+def settle(moves, landing, stayed, inbox, state, density):
     cells = state.shape[1]
-    moves.need(0, 1, 2)
+    me = lax.axis_index("dev")
+    moves.need(0, 1)
 
     def put(place, tile):
         for k in range(6):
@@ -354,40 +446,13 @@
         density[pl.ds(place, 1), :] = tile[6:7]
 
     for i in range(stayed.shape[0]):
-        put(first[0] + i, stayed[i])
+        put(landing[1, me] + i, stayed[i])
     for t in range(inbox.shape[0] // SLOTS):
 
-        @pl.when(arrived[t] < cells)
+        @pl.when(landing[0, t] < cells)
         def _():
             for k in range(SLOTS):
-                put(arrived[t] + k, inbox[t * SLOTS + k])
-
-
-def routes(owners, cells, peers):
-    me = lax.axis_index("dev")
-    ids = jnp.arange(cells, dtype=jnp.int32)
-    devs = jnp.arange(peers, dtype=jnp.int32)
-    slots = jnp.arange(SLOTS, dtype=jnp.int32)
-    halves = jnp.arange(MOVERS, dtype=jnp.int32)
-    per_dev = owners.reshape(peers, cells)
-    arrivals = jnp.sum((per_dev == me).astype(jnp.int32), 1)
-    before = jnp.sum(jnp.where(devs[None, :] < devs[:, None], arrivals[None, :], 0), 1)
-    arrived = jnp.where((arrivals > 0) & (devs != me), before, cells)
-    first = jnp.sum(jnp.where(devs == me, before, 0)).reshape(1)
-    targets = jnp.sum(jnp.where(devs[:, None] == me, per_dev, 0), 0)
-    earlier = ids[None, :] < ids[:, None]
-    rank = jnp.sum(((targets[None, :] == targets[:, None]) & earlier).astype(jnp.int32), 1)
-    leaves = targets != me
-    order = jnp.sum(((leaves[None, :] == leaves[:, None]) & earlier).astype(jnp.int32), 1)
-    spot = order[None, :] == halves[:, None]
-    movers = jnp.sum(jnp.where(spot & leaves[None, :], ids[None, :], 0), 1)
-    stayers = jnp.sum(jnp.where(spot & ~leaves[None, :], ids[None, :], 0), 1)
-    hit = (targets[None, None, :] == devs[:, None, None]) & (
-        rank[None, None, :] == slots[None, :, None]
-    )
-    hit = hit & (devs != me)[:, None, None]
-    outs = jnp.sum(jnp.where(hit, order[None, None, :], 0), 2)
-    return first, arrived, movers, stayers, outs
+                put(landing[0, t] + k, inbox[t * SLOTS + k])
 
 
 def shards(positions, velocities, masses, counts, walls, neighbours, send_cells, owners):
@@ -401,7 +466,6 @@
     def exchange(x):
         return lax.all_to_all(x, "dev", split_axis=0, concat_axis=0, tiled=True)
 
-    first, arrived, movers, stayers, outs = routes(owners[0], cells, peers)
     near = neighbours.T
     sends = jnp.swapaxes(send_cells, 2, 3)
     own, send, head, tail, fluid = call(
@@ -421,11 +485,26 @@
     rest = exchange(send)
     below = lax.ppermute(tail, "group", up)
     above = lax.ppermute(head, "group", down)
-    rho, q, q_head, q_tail, send_q, tab, mine, tiles = call(
+    sums, tab_own, mine, plan, landing = call(
+        home,
+        4096,
+        [near, owners],
+        [own, owners],
+        [],
+        [
+            ((cells + 1, 8, width), F32),
+            ((cells, 48, width), BF16),
+            ((cells, 48, width), BF16),
+            ((PLAN,), jnp.int32),
+            ((8, 128), jnp.int32),
+        ],
+        [pltpu.SMEM((256,), jnp.int32), pltpu.SMEM((peers,), jnp.int32)],
+    )
+    rho, q, q_head, q_tail, send_q, tab, tiles = call(
         densities,
         4096,
-        [counts, near, sends],
-        [own],
+        [counts, plan, sends],
+        [tab_own, own, mine, sums],
         [below, above, rest],
         [
             ((cells, width), F32),
@@ -434,9 +513,9 @@
             ((RIM, 1, width), F32),
             ((SLOTS * peers, 1, width), F32),
             ((total, 48, width), BF16),
-            ((cells, 48, width), BF16),
             ((total, 8, width), F32),
         ],
+        into=[(5, RIM), (6, RIM)],
     )
     q_rest = exchange(send_q)
     q_below = lax.ppermute(q_tail, "group", up)
@@ -446,7 +525,7 @@
     outbox, feat1, feat2 = call(
         forces_moving,
         4096,
-        [counts, near, movers, outs],
+        [counts, near, plan],
         [tiles, q, rho, fluid, tab, mine],
         [q_below, q_above, q_rest],
         [
@@ -460,7 +539,7 @@
     [stayed] = call(
         forces_staying,
         4096,
-        [counts, near, stayers],
+        [counts, near, plan],
         [tiles, q, rho, fluid, tab, mine, feat1, feat2],
         [],
         [((cells - MOVERS, 8, width), F32)],
@@ -469,7 +548,7 @@
     return call(
         settle,
         12000,
-        [first, arrived],
+        [landing],
         [stayed],
         [inbox],
         [((6, cells, width), F32), ((cells, width), F32)],

time: 86.5 us -> 87.5 us (1.012)
  the two profiles are of different devices: /device:TPU:227 before, /device:TPU:99 now
where the time goes in v5:
time: 87.5 us; the launch traced here: 86.9 us
  Pallas kernels  42 us (48%)
  starting transfers between devices  37.9 us (43%)
  waiting for transfers between devices  3.84 us (4%)
  local copies, waits for them, and re-layouts  2.34 us (3%)
    pallas_call x6, Pallas kernels, call(): pl.pallas_call(body, out_shape=[jax.ShapeDtypeStruct(*o) for o in outs],...  42 us
    all_to_all x3, starting transfers between devices, exchange(): return lax.all_to_all(x, 'dev', split_axis=0, concat_axis=0, tiled=True)  24.4 us
    ppermute x1, starting transfers between devices, shards(): q_below = lax.ppermute(q_tail, 'group', up)  4.86 us
    ppermute x1, starting transfers between devices, shards(): below = lax.ppermute(tail, 'group', up)  4.76 us
    ppermute x1, waiting for transfers between devices, shards(): q_above = lax.ppermute(q_head, 'group', down)  3.82 us
    unnamed x16, local copies, waits for them, and re-layouts  2.34 us
    ppermute x1, starting transfers between devices, shards(): above = lax.ppermute(head, 'group', down)  1.92 us
    ppermute x1, starting transfers between devices, shards(): q_above = lax.ppermute(q_head, 'group', down)  1.92 us
  transfers between devices with their start and end apart: 7, of which 1 were waited for; matrix products, arithmetic and copies ran while one was open for 0% of the time, Pallas kernels for 22%

profile of v5, /device:TPU:99, one launch (start us, length us, event | category | flops | bytes accessed | tf_op | source)
XLA Modules:
  0.0 86.9 jit_solution(17524653320412566101)
XLA Ops:
  0.6 2.3 %prepare.1 = (f32[32,8,256]{2,1,0:T(8,128)}, f32[64,8,256]{2,1,0:T(8,128)}, f32[4,8,256]{2,1,0:T(8,128)}, f32[4,8,256]{2,1,0:T(8,128)}, f32[32,256]{1,0:T(8,128)}) custom-call(s32[32]{0:T(128)} %refs_0_.7, s32[1,1,2,32]{3,2,1,0:T(2,128)} %bitcast.5, f32[3,32,256]{2,1,0:T(8,128)} %refs_2_.1, f32[3,32,256]{2,1,0:T(8,128)} %refs_3_.2, f32[32,256]{1,0:T(8,128)} %refs_4_.1, ...), custom_call_target="tpu_custom_call" | custom-call | tf_op jit(solution)/shard_map/prepare/pallas_call | solution.py:70
  2.9 7.9 %all-to-all-start = ((f32[64,8,256]{2,1,0:T(8,128)}), f32[64,8,256]{2,1,0:T(8,128)S(1)}, u32[]{:S(2)}, u32[]{:S(2)}) async-start(f32[64,8,256]{2,1,0:T(8,128)} %get-tuple-element.30), calls=%async_computation | async-start | bytes 1048576 | tf_op jit(solution)/shard_map/all_to_all | solution.py:467
  10.8 4.8 %collective-permute-start = (f32[4,8,256]{2,1,0:T(8,128)}, f32[4,8,256]{2,1,0:T(8,128)S(1)}, u32[]{:S(2)}, u32[]{:S(2)}) collective-permute-start(f32[4,8,256]{2,1,0:T(8,128)} %get-tuple-element.28), channel_id=1, source_target_pairs={{0,32},{32,64},{64,96},{96,128},{128,160},{160,192},{192,224},{224... | collective-permute-start | bytes 98312 | tf_op jit(solution)/shard_map/ppermute | solution.py:486
  15.6 1.9 %collective-permute-start.1 = (f32[4,8,256]{2,1,0:T(8,128)}, f32[4,8,256]{2,1,0:T(8,128)S(1)}, u32[]{:S(2)}, u32[]{:S(2)}) collective-permute-start(f32[4,8,256]{2,1,0:T(8,128)} %get-tuple-element.29), channel_id=1, source_target_pairs={{32,0},{64,32},{96,64},{128,96},{160,128},{192,160},{224,192},{256... | collective-permute-start | bytes 98312 | tf_op jit(solution)/shard_map/ppermute | solution.py:487
  17.5 7.2 %home.1 = (f32[33,8,256]{2,1,0:T(8,128)}, bf16[32,48,256]{2,1,0:T(8,128)(2,1)}, bf16[32,48,256]{2,1,0:T(8,128)(2,1)}, s32[512]{0:T(512)}, s32[8,128]{1,0:T(8,128)}) custom-call(s32[3,32]{1,0:T(4,128)} %bitcast.2, s32[1,1024]{1,0:T(1,128)} %refs_3_.3, f32[32,8,256]{2,1,0:T(8,128)} %get-tuple-element.22.refs_2_.refs_4_, s32[1,1024]{1,0:T(1,128)} %refs_3_.3), custom_call_target="tpu_custom_call" | custom-call | tf_op jit(solution)/shard_map/home/pallas_call | solution.py:70
  24.7 0.0 collective-permute-done.refs_7_
  24.7 0.0 copy-start.4
  24.7 0.0 collective-permute-done.1.refs_8_
  24.7 0.0 copy-start.5
  24.7 0.0 all-to-all-done.refs_9_
  24.8 0.0 copy-start.2
  24.8 0.5 copy-done.4
  25.3 0.0 copy-done.5
  25.4 0.2 copy-done.2
  25.6 7.5 %densities.1 = (f32[32,256]{1,0:T(8,128)}, f32[32,256]{1,0:T(8,128)}, f32[4,1,256]{2,1,0:T(1,128)}, f32[4,1,256]{2,1,0:T(1,128)}, f32[64,1,256]{2,1,0:T(1,128)},...) custom-call(s32[32]{0:T(128)} %refs_0_.7, s32[512]{0:T(512)} %get-tuple-element.24.refs_1_.refs_2_, ...), custom_call_target="tpu_custom_call" | custom-call | tf_op jit(solution)/shard_map/densities/pallas_call | solution.py:70
  33.1 7.7 %all-to-all-start.1 = ((f32[64,1,256]{2,1,0:T(1,128)}), f32[64,1,256]{2,1,0:T(1,128)S(1)}, u32[]{:S(2)}, u32[]{:S(2)}) async-start(f32[64,1,256]{2,1,0:T(1,128)} %get-tuple-element.38), calls=%async_computation.1 | async-start | bytes 131072 | tf_op jit(solution)/shard_map/all_to_all | solution.py:467
  40.8 4.9 %collective-permute-start.2 = (f32[4,1,256]{2,1,0:T(1,128)}, f32[4,1,256]{2,1,0:T(1,128)S(1)}, u32[]{:S(2)}, u32[]{:S(2)}) collective-permute-start(f32[4,1,256]{2,1,0:T(1,128)} %get-tuple-element.36), channel_id=1, source_target_pairs={{0,32},{32,64},{64,96},{96,128},{128,160},{160,192},{192,224},{224... | collective-permute-start | bytes 12296 | tf_op jit(solution)/shard_map/ppermute | solution.py:521
  45.6 1.9 %collective-permute-start.3 = (f32[4,1,256]{2,1,0:T(1,128)}, f32[4,1,256]{2,1,0:T(1,128)S(1)}, u32[]{:S(2)}, u32[]{:S(2)}) collective-permute-start(f32[4,1,256]{2,1,0:T(1,128)} %get-tuple-element.37), channel_id=1, source_target_pairs={{32,0},{64,32},{96,64},{128,96},{160,128},{192,160},{224,192},{256... | collective-permute-start | bytes 12296 | tf_op jit(solution)/shard_map/ppermute | solution.py:522
  47.6 0.0 collective-permute-done.2.refs_9_
  47.6 0.0 copy-start.6
  47.6 3.8 %collective-permute-done.3.refs_10_ = f32[4,1,256]{2,1,0:T(1,128)S(1)} collective-permute-done((f32[4,1,256]{2,1,0:T(1,128)}, f32[4,1,256]{2,1,0:T(1,128)S(1)}, u32[]{:S(2)}, u32[]{:S(2)}) %collective-permute-start.3) | collective-permute-done | bytes 4128 | tf_op jit(solution)/shard_map/ppermute | solution.py:522
  51.4 0.0 copy-start.7
  51.4 0.0 all-to-all-done.1.refs_11_
  51.4 0.0 copy-start.3
  51.4 0.0 copy-done.6
  51.4 0.6 copy-done.7
  52.0 0.0 copy-done.3
  52.0 11.8 %forces_moving.1 = (f32[64,8,256]{2,1,0:T(8,128)}, bf16[104,16,256]{2,1,0:T(8,128)(2,1)}, bf16[104,32,256]{2,1,0:T(8,128)(2,1)}) custom-call(s32[32]{0:T(128)} %refs_0_.7, s32[3,32]{1,0:T(4,128)} %bitcast.3, s32[512]{0:T(512)} %get-tuple-element.24.refs_1_.refs_2_, f32[104,8,256]{2,1,0:T(8,128)} %get-tuple-element.31.refs_3_, ...), custom_call_target="tpu_custom_call" | custom-call | tf_op jit(solution)/shard_map/forces_moving/pallas_call | solution.py:70
  63.9 8.8 %all-to-all-start.2 = ((f32[64,8,256]{2,1,0:T(8,128)}), f32[64,8,256]{2,1,0:T(8,128)S(1)}, u32[]{:S(2)}, u32[]{:S(2)}) async-start(f32[64,8,256]{2,1,0:T(8,128)} %get-tuple-element.41), calls=%async_computation.2 | async-start | bytes 1048576 | tf_op jit(solution)/shard_map/all_to_all | solution.py:467
  72.7 0.0 copy-start.1
  72.7 11.6 %forces_staying.1.refs_1_ = f32[16,8,256]{2,1,0:T(8,128)} custom-call(s32[32]{0:T(128)} %refs_0_.7, s32[3,32]{1,0:T(4,128)} %bitcast.4, s32[512]{0:T(512)} %get-tuple-element.24.refs_1_.refs_2_, f32[104,8,256]{2,1,0:T(8,128)} %get-tuple-element.31.refs_3_, f32[32,256]{1,0:T(8,128)} %get-tuple-element.32.refs_4_, f32[32,256]{1,0:T(8,128)} %get-tuple-element.33.refs_5_, ...), custom_call_target="tpu_custom_call" | custom-call | tf_op jit(solution)/shard_map/forces_staying/pallas_call | solution.py:70
  84.3 0.0 all-to-all-done.2.refs_2_
  84.3 0.0 copy-done.1
  84.3 0.0 copy-start
  84.4 0.9 %copy-done = f32[16,8,256]{2,1,0:T(8,128)S(1)} copy-done((f32[16,8,256]{2,1,0:T(8,128)S(1)}, f32[16,8,256]{2,1,0:T(8,128)}, u32[]{:S(2)}) %copy-start) | copy-done | bytes 131096
  85.2 1.7 %settle.1 = (f32[6,32,256]{2,1,0:T(8,128)}, f32[32,256]{1,0:T(8,128)}) custom-call(s32[8,128]{1,0:T(8,128)S(1)} %copy-done.1, f32[16,8,256]{2,1,0:T(8,128)S(1)} %copy-done, f32[64,8,256]{2,1,0:T(8,128)S(1)} %all-to-all-done.2.refs_2_), custom_call_target="tpu_custom_call" | custom-call | tf_op jit(solution)/shard_map/settle/pallas_call | solution.py:70
Async XLA Ops:
  2.9 21.9 %all-to-all-start = ((f32[64,8,256]{2,1,0:T(8,128)}), f32[64,8,256]{2,1,0:T(8,128)S(1)}, u32[]{:S(2)}, u32[]{:S(2)}) async-start(f32[64,8,256]{2,1,0:T(8,128)} %get-tuple-element.30), calls=%async_computation | async-start | bytes 1048576 | tf_op jit(solution)/shard_map/all_to_all | solution.py:467
  10.8 13.9 %collective-permute-start = (f32[4,8,256]{2,1,0:T(8,128)}, f32[4,8,256]{2,1,0:T(8,128)S(1)}, u32[]{:S(2)}, u32[]{:S(2)}) collective-permute-start(f32[4,8,256]{2,1,0:T(8,128)} %get-tuple-element.28), channel_id=1, source_target_pairs={{0,32},{32,64},{64,96},{96,128},{128,160},{160,192},{192,224},{224... | collective-permute-start | bytes 98312 | tf_op jit(solution)/shard_map/ppermute | solution.py:486
  15.6 9.1 %collective-permute-start.1 = (f32[4,8,256]{2,1,0:T(8,128)}, f32[4,8,256]{2,1,0:T(8,128)S(1)}, u32[]{:S(2)}, u32[]{:S(2)}) collective-permute-start(f32[4,8,256]{2,1,0:T(8,128)} %get-tuple-element.29), channel_id=1, source_target_pairs={{32,0},{64,32},{96,64},{128,96},{160,128},{192,160},{224,192},{256... | collective-permute-start | bytes 98312 | tf_op jit(solution)/shard_map/ppermute | solution.py:487
  24.7 0.6 copy-start.4
  24.7 0.6 copy-start.5
  24.8 0.8 copy-start.2
  33.1 18.3 %all-to-all-start.1 = ((f32[64,1,256]{2,1,0:T(1,128)}), f32[64,1,256]{2,1,0:T(1,128)S(1)}, u32[]{:S(2)}, u32[]{:S(2)}) async-start(f32[64,1,256]{2,1,0:T(1,128)} %get-tuple-element.38), calls=%async_computation.1 | async-start | bytes 131072 | tf_op jit(solution)/shard_map/all_to_all | solution.py:467
  40.8 6.8 %collective-permute-start.2 = (f32[4,1,256]{2,1,0:T(1,128)}, f32[4,1,256]{2,1,0:T(1,128)S(1)}, u32[]{:S(2)}, u32[]{:S(2)}) collective-permute-start(f32[4,1,256]{2,1,0:T(1,128)} %get-tuple-element.36), channel_id=1, source_target_pairs={{0,32},{32,64},{64,96},{96,128},{128,160},{160,192},{192,224},{224... | collective-permute-start | bytes 12296 | tf_op jit(solution)/shard_map/ppermute | solution.py:521
  45.6 5.8 %collective-permute-start.3 = (f32[4,1,256]{2,1,0:T(1,128)}, f32[4,1,256]{2,1,0:T(1,128)S(1)}, u32[]{:S(2)}, u32[]{:S(2)}) collective-permute-start(f32[4,1,256]{2,1,0:T(1,128)} %get-tuple-element.37), channel_id=1, source_target_pairs={{32,0},{64,32},{96,64},{128,96},{160,128},{192,160},{224,192},{256... | collective-permute-start | bytes 12296 | tf_op jit(solution)/shard_map/ppermute | solution.py:522
  47.6 3.8 %copy-start.6 = (f32[4,1,256]{2,1,0:T(1,128)}, f32[4,1,256]{2,1,0:T(1,128)S(1)}, u32[]{:S(2)}) copy-start(f32[4,1,256]{2,1,0:T(1,128)S(1)} %collective-permute-done.2.refs_9_) | copy-start | bytes 12292
  51.4 0.6 copy-start.7
  51.4 0.6 copy-start.3
  63.9 20.5 %all-to-all-start.2 = ((f32[64,8,256]{2,1,0:T(8,128)}), f32[64,8,256]{2,1,0:T(8,128)S(1)}, u32[]{:S(2)}, u32[]{:S(2)}) async-start(f32[64,8,256]{2,1,0:T(8,128)} %get-tuple-element.41), calls=%async_computation.2 | async-start | bytes 1048576 | tf_op jit(solution)/shard_map/all_to_all | solution.py:467
  72.7 11.7 %copy-start.1 = (s32[8,128]{1,0:T(8,128)S(1)}, s32[8,128]{1,0:T(8,128)}, u32[]{:S(2)}) copy-start(s32[8,128]{1,0:T(8,128)} %get-tuple-element.23.refs_0_) | copy-start | bytes 12292
  84.3 0.9 %copy-start = (f32[16,8,256]{2,1,0:T(8,128)S(1)}, f32[16,8,256]{2,1,0:T(8,128)}, u32[]{:S(2)}) copy-start(f32[16,8,256]{2,1,0:T(8,128)} %forces_staying.1.refs_1_) | copy-start | bytes 393220

commit v6 on v5

--- a/solution.py
+++ b/solution.py
@@ -1,3 +1,5 @@
+import functools
+
 import jax
 import jax.numpy as jnp
 from jax import lax
@@ -53,9 +55,11 @@
         targets, refs = refs[:n_out], refs[n_out:]
         inner, refs = list(refs[: n_in - len(into)]), refs[n_in - len(into) :]
         results, refs = refs[:n_out], refs[n_out:]
-        for i, (out, start) in enumerate(into):
-            rows = pl.ds(start, held[i].shape[0])
-            inner.insert(len(ints) + i, results[out].at[rows])
+        sources = list(sources)
+        for i, (out, start, count) in enumerate(into):
+            target = (*results, *refs[2:])[out]
+            inner.insert(len(ints) + i, target.at[pl.ds(start, count)])
+            sources[len(ints) + i] = sources[len(ints) + i].at[pl.ds(0, count)]
         in_sems, out_sems, rest = refs[0], refs[1], refs[2:]
         moves = Moves(
             [pltpu.make_async_copy(a, b, in_sems.at[i]) for i, (a, b) in enumerate(zip(sources, inner))],
@@ -78,7 +82,7 @@
         + [pltpu.SemaphoreType.DMA((n_in,)), pltpu.SemaphoreType.DMA((n_out,))]
         + list(scratch),
         compiler_params=pltpu.CompilerParams(vmem_limit_bytes=(64 << 20) - (room << 10)),
-        name=kernel.__name__,
+        name=getattr(kernel, "func", kernel).__name__,
     )(*ints, *held, *near)
 
 
@@ -115,19 +119,13 @@
         own[c, 7:8, :] = jnp.where(active, bond[row], 0.0)
         fluid[row, :] = jnp.where(active, free[row], 0.0)
     head[...] = own[0:RIM]
-    tail[...] = own[cells - RIM : cells]
+    tail[...] = jnp.zeros(tail.shape, F32)
+    tail[0:RIM] = own[cells - RIM : cells]
     for t in range(send.shape[0] // SLOTS):
         for k in range(SLOTS):
             cell = sends[0, 0, k, t]
             tile = own[jnp.maximum(cell, 0)]
             send[t * SLOTS + k] = jnp.where(cell >= 0, tile, 0.0)
-
-
-def segments(below, own, above, rest):
-    start = 0
-    for ref in (below, own, above, rest):
-        yield start, ref
-        start += ref.shape[0]
 
 
 def squared(tile, sub):
@@ -174,11 +172,10 @@
     lax.fori_loop(0, lax.div(count + (STEP - 1), STEP), some, 0)
 
 
-def home(moves, near, owners, tiles, owners_v, sums, tab, mine, plan, landing, jobs, seen):
+def home(moves, near, tiles, sums, tab, mine, plan, jobs):
     cells, _, width = tiles.shape
     sub, _ = rows_and_lanes(width)
-    me = lax.axis_index("dev")
-    moves.need(0, 2)
+    moves.need(0, 1)
 
     def build(i, carry):
         tab[i] = source_rows(tiles[i], sub)
@@ -216,7 +213,10 @@
     run_jobs(lambda i: jobs[i], lambda i: jobs[128 + i], local, tab, RIM, mine, sums)
     moves.save(0)
 
-    moves.need(1, 3)
+
+def routing(moves, owners, owners_v, after, plan, landing, seen, *, cells):
+    me = lax.axis_index("dev")
+    moves.need(0, 1)
     for d in range(seen.shape[0]):
         seen[d] = 0
     for i in range(seen.shape[0] * SLOTS):
@@ -232,7 +232,7 @@
         seen[to] = seen[to] + leaves
         moving = moving + leaves
         staying = staying + 1 - leaves
-    moves.save(3)
+    moves.save(0)
     entries = owners_v.shape[1]
     dev = lax.broadcasted_iota(jnp.int32, (entries, 128), 1)
     entry = lax.broadcasted_iota(jnp.int32, (entries, 128), 0)
@@ -251,22 +251,21 @@
 
 
 def densities(
-    moves, counts, plan, sends, tab_own, tiles_own, mine, sums, below, above, rest,
+    moves, counts, plan, sends, tab_own, tiles_own, below, above, rest, mine, sums,
     rho, q, q_head, q_tail, send_q, tab, tiles,
 ):
     cells, _, width = mine.shape
     sub, lane = rows_and_lanes(width)
-    for start, ref in ((0, below), (RIM + cells, above), (2 * RIM + cells, rest)):
-
-        def source(i, carry, start=start, ref=ref):
-            tile = ref[i]
-            tab[start + i] = source_rows(tile, sub)
-            tiles[start + i] = tile
+    moves.need(5, 6, 7)
+    for start, count in ((0, RIM), (RIM + cells, tab.shape[0] - RIM - cells)):
+
+        def source(i, carry, start=start):
+            tab[start + i] = source_rows(tiles[start + i], sub)
             return carry
 
-        lax.fori_loop(0, ref.shape[0], source, 0, unroll=4)
-
-    moves.need(*range(7))
+        lax.fori_loop(0, count, source, 0, unroll=4)
+
+    moves.need(*range(10))
     moves.save(5, 6)
     run_jobs(
         lambda i: plan[JOB_ROW + i], lambda i: plan[JOB_CELL + i], plan[JOB_COUNT], tab, 0, mine, sums
@@ -276,15 +275,16 @@
         active = lane < counts[c]
         safe = jnp.where(active, row, 1.0)
         value = STIFFNESS * (row - REST_DENSITY) / (safe * safe)
-        q[c : c + 1, :] = jnp.where(active, value, 0.0)
+        q[c] = jnp.where(active, value, 0.0)
         rho[c : c + 1, :] = jnp.where(active, row, 0.0)
+    q_tail[...] = jnp.zeros(q_tail.shape, F32)
     for r in range(RIM):
-        q_head[r] = q[r : r + 1, :]
-        q_tail[r] = q[cells - RIM + r : cells - RIM + r + 1, :]
+        q_head[r] = q[r]
+        q_tail[r] = q[cells - RIM + r]
     for t in range(send_q.shape[0] // SLOTS):
         for k in range(SLOTS):
             pick = jnp.maximum(sends[0, 0, k, t], 0)
-            send_q[t * SLOTS + k] = q[pl.ds(pick, 1), :]
+            send_q[t * SLOTS + k] = q[pick]
 
 
 def first_features(tile, sub):
@@ -346,9 +346,10 @@
         return first, second[0:8] + second[8:16] + second[16:24]
 
 
-def sweep(pairs, order, start, count, buffers, finish, sub):
+def sweep(pairs, order, start, count, buffers, finish, sub, moves):
     a, b = buffers[0:2], buffers[2:4]
     pairs.fill(order[start], *a)
+    moves.need(*range(len(moves.ins)))
 
     def two(t, carry):
         for i, now, then in ((2 * t, a, b), (2 * t + 1, b, a)):
@@ -385,33 +386,30 @@
 
 
 def forces_moving(
-    moves, counts, near, plan, tiles, q, rho, fluid, tab, mine, q_below, q_above, q_rest,
-    outbox, feat1, feat2, moved, *buffers,
+    moves, counts, near, plan, q_below, q_own, q_above, q_rest, tiles, rho, fluid, tab, mine,
+    outbox, feat1, feat2, q, moved, *buffers,
 ):
     sub, lane = rows_and_lanes(tiles.shape[2])
-    moves.need(3, 4)
-    for start, q_ref in segments(q_below, q, q_above, q_rest):
-
-        def source(i, carry, start=start, q_ref=q_ref):
-            row_q = q_ref[i] if q_ref.ndim == 3 else q_ref[pl.ds(i, 1), :]
-            tile = tiles[start + i]
-            feat1[start + i] = first_features(tile, sub)
-            feat2[start + i] = second_features(tile, row_q, sub)
-            return carry
-
-        lax.fori_loop(0, q_ref.shape[0], source, 0, unroll=4)
-
+    moves.need(3, 4, 5, 6, 7)
+
+    def source(i, carry):
+        tile = tiles[i]
+        feat1[i] = first_features(tile, sub)
+        feat2[i] = second_features(tile, q[i], sub)
+        return carry
+
+    lax.fori_loop(0, tiles.shape[0], source, 0, unroll=8)
     moves.save(1, 2)
-    moves.need(*range(9))
+    moves.need(*range(12))
 
     def finish(i, c, first, second):
         row = pl.ds(c, 1)
         moved[i] = advance(
-            first, second, tiles[RIM + c], q[row, :], rho[row, :], fluid[row, :], lane < counts[c], sub
+            first, second, tiles[RIM + c], q[RIM + c], rho[row, :], fluid[row, :], lane < counts[c], sub
         )
 
     sweep(
-        Pairs(near, tab, mine, feat1, feat2), plan, MOVING, MOVERS, buffers, finish, sub
+        Pairs(near, tab, mine, feat1, feat2), plan, MOVING, MOVERS, buffers, finish, sub, moves
     )
     for t in range(outbox.shape[0] // SLOTS):
         for k in range(SLOTS):
@@ -419,19 +417,19 @@
 
 
 def forces_staying(
-    moves, counts, near, plan, tiles, q, rho, fluid, tab, mine, feat1, feat2, stayed, *buffers
+    moves, counts, near, plan, tab, mine, feat1, feat2, tiles, q, rho, fluid, stayed, *buffers
 ):
     sub, lane = rows_and_lanes(tiles.shape[2])
-    moves.need(*range(11))
+    moves.need(1, 2, 3, 4)
 
     def finish(i, c, first, second):
         row = pl.ds(c, 1)
         stayed[i] = advance(
-            first, second, tiles[RIM + c], q[row, :], rho[row, :], fluid[row, :], lane < counts[c], sub
+            first, second, tiles[RIM + c], q[c], rho[row, :], fluid[row, :], lane < counts[c], sub
         )
 
     sweep(
-        Pairs(near, tab, mine, feat1, feat2), plan, STAYING, stayed.shape[0], buffers, finish, sub
+        Pairs(near, tab, mine, feat1, feat2), plan, STAYING, stayed.shape[0], buffers, finish, sub, moves
     )
 
 
@@ -478,69 +476,86 @@
             ((cells, 8, width), F32),
             ((SLOTS * peers, 8, width), F32),
             ((RIM, 8, width), F32),
-            ((RIM, 8, width), F32),
+            ((SLOTS * peers, 8, width), F32),
             ((cells, width), F32),
         ],
     )
+    below = lax.ppermute(tail, "group", up)
     rest = exchange(send)
-    below = lax.ppermute(tail, "group", up)
     above = lax.ppermute(head, "group", down)
-    sums, tab_own, mine, plan, landing = call(
+    row_type, small = ((RIM, 1, width), F32), ((SLOTS * peers, 1, width), F32)
+    pair_type, own_type = ((total, 48, width), BF16), ((cells, 48, width), BF16)
+    sums, tab_own, mine, jobs = call(
         home,
         4096,
-        [near, owners],
-        [own, owners],
+        [near],
+        [own],
         [],
-        [
-            ((cells + 1, 8, width), F32),
-            ((cells, 48, width), BF16),
-            ((cells, 48, width), BF16),
-            ((PLAN,), jnp.int32),
-            ((8, 128), jnp.int32),
-        ],
-        [pltpu.SMEM((256,), jnp.int32), pltpu.SMEM((peers,), jnp.int32)],
+        [((cells + 1, 8, width), F32), own_type, own_type, ((PLAN,), jnp.int32)],
+        [pltpu.SMEM((256,), jnp.int32)],
     )
     rho, q, q_head, q_tail, send_q, tab, tiles = call(
         densities,
         4096,
-        [counts, plan, sends],
-        [tab_own, own, mine, sums],
-        [below, above, rest],
+        [counts, jobs, sends],
+        [tab_own, own, below, above, rest, mine, sums],
+        [],
         [
             ((cells, width), F32),
-            ((cells, width), F32),
-            ((RIM, 1, width), F32),
-            ((RIM, 1, width), F32),
-            ((SLOTS * peers, 1, width), F32),
-            ((total, 48, width), BF16),
+            ((cells, 1, width), F32),
+            row_type,
+            small,
+            small,
+            pair_type,
             ((total, 8, width), F32),
         ],
-        into=[(5, RIM), (6, RIM)],
-    )
+        into=[
+            (5, RIM, cells),
+            (6, RIM, cells),
+            (6, 0, RIM),
+            (6, RIM + cells, RIM),
+            (6, 2 * RIM + cells, SLOTS * peers),
+        ],
+    )
+    q_below = lax.ppermute(q_tail, "group", up)
     q_rest = exchange(send_q)
-    q_below = lax.ppermute(q_tail, "group", up)
     q_above = lax.ppermute(q_head, "group", down)
+    plan, landing = call(
+        functools.partial(routing, cells=cells),
+        4096,
+        [owners],
+        [owners, q_head],
+        [],
+        [((PLAN,), jnp.int32), ((8, 128), jnp.int32)],
+        [pltpu.SMEM((peers,), jnp.int32)],
+    )
     partners = neighbours.shape[1] + 1
     buffers = [pltpu.VMEM((partners * width, 2 * width), BF16)] * 4
     outbox, feat1, feat2 = call(
         forces_moving,
         4096,
         [counts, near, plan],
-        [tiles, q, rho, fluid, tab, mine],
-        [q_below, q_above, q_rest],
+        [q_below, q, q_above, q_rest, tiles, rho, fluid, tab, mine],
+        [],
         [
             ((SLOTS * peers, 8, width), F32),
             ((total, 16, width), BF16),
             ((total, 32, width), BF16),
         ],
-        [pltpu.VMEM((MOVERS, 8, width), F32)] + buffers,
+        [pltpu.VMEM((total, 1, width), F32), pltpu.VMEM((MOVERS, 8, width), F32)] + buffers,
+        into=[
+            (3, 0, RIM),
+            (3, RIM, cells),
+            (3, RIM + cells, RIM),
+            (3, 2 * RIM + cells, SLOTS * peers),
+        ],
     )
     inbox = exchange(outbox)
     [stayed] = call(
         forces_staying,
         4096,
         [counts, near, plan],
-        [tiles, q, rho, fluid, tab, mine, feat1, feat2],
+        [tab, mine, feat1, feat2, tiles, q, rho, fluid],
         [],
         [((cells - MOVERS, 8, width), F32)],
         buffers,

time: 87.5 us -> 86.2 us (0.985)
  the two profiles are of different devices: /device:TPU:99 before, /device:TPU:97 now
where the time goes in v6:
time: 86.2 us; the launch traced here: 85.6 us
  Pallas kernels  41.4 us (48%)
  starting transfers between devices  34.4 us (40%)
  waiting for transfers between devices  6.57 us (8%)
  local copies, waits for them, and re-layouts  2.51 us (3%)
    pallas_call x7, Pallas kernels, call(): pl.pallas_call(body, out_shape=[jax.ShapeDtypeStruct(*o) for o in outs],...  41.4 us
    all_to_all x3, starting transfers between devices, exchange(): return lax.all_to_all(x, 'dev', split_axis=0, concat_axis=0, tiled=True)  21.8 us
    ppermute x1, starting transfers between devices, shards(): below = lax.ppermute(tail, 'group', up)  4.76 us
    all_to_all x3, waiting for transfers between devices, exchange(): return lax.all_to_all(x, 'dev', split_axis=0, concat_axis=0, tiled=True)  4.11 us
    ppermute x1, starting transfers between devices, shards(): q_below = lax.ppermute(q_tail, 'group', up)  4.03 us
    unnamed x16, local copies, waits for them, and re-layouts  2.51 us
    ppermute x1, waiting for transfers between devices, shards(): q_above = lax.ppermute(q_head, 'group', down)  2.45 us
    ppermute x1, starting transfers between devices, shards(): above = lax.ppermute(head, 'group', down)  1.92 us
  transfers between devices with their start and end apart: 7, of which 4 were waited for; matrix products, arithmetic and copies ran while one was open for 0% of the time, Pallas kernels for 24%

profile of v6, /device:TPU:97, one launch (start us, length us, event | category | flops | bytes accessed | tf_op | source)
XLA Modules:
  0.0 85.6 jit_solution(2167196411550239410)
XLA Ops:
  0.6 2.4 %prepare.1 = (f32[32,8,256]{2,1,0:T(8,128)}, f32[64,8,256]{2,1,0:T(8,128)}, f32[4,8,256]{2,1,0:T(8,128)}, f32[64,8,256]{2,1,0:T(8,128)}, f32[32,256]{1,0:T(8,128)}) custom-call(s32[32]{0:T(128)} %refs_0_.9, s32[1,1,2,32]{3,2,1,0:T(2,128)} %bitcast.5, f32[3,32,256]{2,1,0:T(8,128)} %refs_2_.1, f32[3,32,256]{2,1,0:T(8,128)} %refs_3_.1, f32[32,256]{1,0:T(8,128)} %refs_4_.1, ...), custom_call_target="tpu_custom_call" | custom-call | tf_op jit(solution)/shard_map/prepare/pallas_call | solution.py:74
  3.1 4.8 %collective-permute-start = (f32[64,8,256]{2,1,0:T(8,128)}, f32[64,8,256]{2,1,0:T(8,128)S(1)}, u32[]{:S(2)}, u32[]{:S(2)}) collective-permute-start(f32[64,8,256]{2,1,0:T(8,128)} %get-tuple-element.26), channel_id=1, source_target_pairs={{0,32},{32,64},{64,96},{96,128},{128,160},{160,192},{192,224},{224... | collective-permute-start | bytes 1572872 | tf_op jit(solution)/shard_map/ppermute | solution.py:483
  7.8 8.1 %all-to-all-start = ((f32[64,8,256]{2,1,0:T(8,128)}), f32[64,8,256]{2,1,0:T(8,128)S(1)}, u32[]{:S(2)}, u32[]{:S(2)}) async-start(f32[64,8,256]{2,1,0:T(8,128)} %get-tuple-element.28), calls=%async_computation | async-start | bytes 1048576 | tf_op jit(solution)/shard_map/all_to_all | solution.py:465
  15.9 1.9 %collective-permute-start.1 = (f32[4,8,256]{2,1,0:T(8,128)}, f32[4,8,256]{2,1,0:T(8,128)S(1)}, u32[]{:S(2)}, u32[]{:S(2)}) collective-permute-start(f32[4,8,256]{2,1,0:T(8,128)} %get-tuple-element.27), channel_id=1, source_target_pairs={{32,0},{64,32},{96,64},{128,96},{160,128},{192,160},{224,192},{256... | collective-permute-start | bytes 98312 | tf_op jit(solution)/shard_map/ppermute | solution.py:485
  17.8 7.4 %home.1 = (f32[33,8,256]{2,1,0:T(8,128)}, bf16[32,48,256]{2,1,0:T(8,128)(2,1)}, bf16[32,48,256]{2,1,0:T(8,128)(2,1)}, s32[512]{0:T(512)}) custom-call(s32[3,32]{1,0:T(4,128)} %bitcast.2, f32[32,8,256]{2,1,0:T(8,128)} %get-tuple-element.23.refs_1_.refs_4_), custom_call_target="tpu_custom_call" | custom-call | tf_op jit(solution)/shard_map/home/pallas_call | solution.py:74
  25.2 0.0 collective-permute-done.1.refs_6_
  25.2 0.0 copy-start.6
  25.2 2.3 %all-to-all-done.refs_7_ = f32[64,8,256]{2,1,0:T(8,128)S(1)} async-done(((f32[64,8,256]{2,1,0:T(8,128)}), f32[64,8,256]{2,1,0:T(8,128)S(1)}, u32[]{:S(2)}, u32[]{:S(2)}) %all-to-all-start) | async-done | bytes 524320 | tf_op jit(solution)/shard_map/all_to_all | solution.py:465
  27.5 0.0 copy-start.2
  27.5 0.0 collective-permute-done.refs_5_
  27.5 0.0 copy-start.3
  27.5 0.0 copy-done.6
  27.5 0.8 copy-done.2
  28.3 0.2 copy-done.3
  28.5 6.1 %densities.1 = (f32[32,256]{1,0:T(8,128)}, f32[32,1,256]{2,1,0:T(1,128)}, f32[4,1,256]{2,1,0:T(1,128)}, f32[64,1,256]{2,1,0:T(1,128)}, f32[64,1,256]{2,1,0:T(1,1...) custom-call(s32[32]{0:T(128)} %refs_0_.9, s32[512]{0:T(512)} %get-tuple-element.24.refs_1_, ...), custom_call_target="tpu_custom_call" | custom-call | tf_op jit(solution)/shard_map/densities/pallas_call | solution.py:74
  34.6 4.0 %collective-permute-start.2 = (f32[64,1,256]{2,1,0:T(1,128)}, f32[64,1,256]{2,1,0:T(1,128)S(1)}, u32[]{:S(2)}, u32[]{:S(2)}) collective-permute-start(f32[64,1,256]{2,1,0:T(1,128)} %get-tuple-element.35), channel_id=1, source_target_pairs={{0,32},{32,64},{64,96},{96,128},{128,160},{160,192},{192,224},{224... | collective-permute-start | bytes 196616 | tf_op jit(solution)/shard_map/ppermute | solution.py:520
  38.6 6.7 %all-to-all-start.1 = ((f32[64,1,256]{2,1,0:T(1,128)}), f32[64,1,256]{2,1,0:T(1,128)S(1)}, u32[]{:S(2)}, u32[]{:S(2)}) async-start(f32[64,1,256]{2,1,0:T(1,128)} %get-tuple-element.37), calls=%async_computation.1 | async-start | bytes 131072 | tf_op jit(solution)/shard_map/all_to_all | solution.py:465
  45.4 1.9 %collective-permute-start.3 = (f32[4,1,256]{2,1,0:T(1,128)}, f32[4,1,256]{2,1,0:T(1,128)S(1)}, u32[]{:S(2)}, u32[]{:S(2)}) collective-permute-start(f32[4,1,256]{2,1,0:T(1,128)} %get-tuple-element.31.refs_2_), channel_id=1, source_target_pairs={{32,0},{64,32},{96,64},{128,96},{160,128},{192,160},{224,192},{256... | collective-permute-start | bytes 12296 | tf_op jit(solution)/shard_map/ppermute | solution.py:522
  47.3 1.7 %routing.1 = (s32[512]{0:T(512)}, s32[8,128]{1,0:T(8,128)}) custom-call(s32[1,1024]{1,0:T(1,128)} %refs_1_.1, s32[1,1024]{1,0:T(1,128)} %refs_1_.1, f32[4,1,256]{2,1,0:T(1,128)} %get-tuple-element.31.refs_2_), custom_call_target="tpu_custom_call" | custom-call | tf_op jit(solution)/shard_map/routing/pallas_call | solution.py:74
  49.0 2.5 %collective-permute-done.3.refs_5_ = f32[4,1,256]{2,1,0:T(1,128)S(1)} collective-permute-done((f32[4,1,256]{2,1,0:T(1,128)}, f32[4,1,256]{2,1,0:T(1,128)S(1)}, u32[]{:S(2)}, u32[]{:S(2)}) %collective-permute-start.3) | collective-permute-done | bytes 4128 | tf_op jit(solution)/shard_map/ppermute | solution.py:522
  51.4 0.0 copy-start.7
  51.4 1.3 %all-to-all-done.1.refs_6_ = f32[64,1,256]{2,1,0:T(1,128)S(1)} async-done(((f32[64,1,256]{2,1,0:T(1,128)}), f32[64,1,256]{2,1,0:T(1,128)S(1)}, u32[]{:S(2)}, u32[]{:S(2)}) %all-to-all-start.1) | async-done | bytes 65568 | tf_op jit(solution)/shard_map/all_to_all | solution.py:465
  52.7 0.0 copy-start.4
  52.7 0.0 collective-permute-done.2.refs_3_
  52.7 0.0 copy-start.5
  52.7 0.0 copy-done.7
  52.7 0.6 copy-done.4
  53.4 0.0 copy-done.5
  53.4 11.1 %forces_moving.1 = (f32[64,8,256]{2,1,0:T(8,128)}, bf16[104,16,256]{2,1,0:T(8,128)(2,1)}, bf16[104,32,256]{2,1,0:T(8,128)(2,1)}) custom-call(s32[32]{0:T(128)} %refs_0_.9, s32[3,32]{1,0:T(4,128)} %bitcast.3, s32[512]{0:T(512)} %get-tuple-element.33.refs_2_, f32[64,1,256]{2,1,0:T(1,128)} %copy-done.5, f32[32,1,256]{2,1,0:T(1,128)} %get-tuple-element.36.refs_4_.refs_8_, ...), custom_call_target="tpu_custom_call" | custom-call | tf_op jit(solution)/shard_map/forces_moving/pallas_call | solution.py:74
  64.4 7.0 %all-to-all-start.2 = ((f32[64,8,256]{2,1,0:T(8,128)}), f32[64,8,256]{2,1,0:T(8,128)S(1)}, u32[]{:S(2)}, u32[]{:S(2)}) async-start(f32[64,8,256]{2,1,0:T(8,128)} %get-tuple-element.43), calls=%async_computation.2 | async-start | bytes 1048576 | tf_op jit(solution)/shard_map/all_to_all | solution.py:465
  71.4 0.0 copy-start.1
  71.4 11.0 %forces_staying.1.refs_1_ = f32[16,8,256]{2,1,0:T(8,128)} custom-call(s32[32]{0:T(128)} %refs_0_.9, s32[3,32]{1,0:T(4,128)} %bitcast.4, s32[512]{0:T(512)} %get-tuple-element.33.refs_2_, bf16[104,48,256]{2,1,0:T(8,128)(2,1)} %get-tuple-element.34.refs_10_.refs_3_, bf16[32,48,256]{2,1,0:T(8,128)(2,1)} %get-tuple-element.29.refs_8_.refs_11_.refs_4_, ...), custom_call_target="tpu_custom_call" | custom-call | tf_op jit(solution)/shard_map/forces_staying/pallas_call | solution.py:74
  82.5 0.6 all-to-all-done.2.refs_2_
  83.0 0.0 copy-done.1
  83.0 0.0 copy-start
  83.0 0.9 %copy-done = f32[16,8,256]{2,1,0:T(8,128)S(1)} copy-done((f32[16,8,256]{2,1,0:T(8,128)S(1)}, f32[16,8,256]{2,1,0:T(8,128)}, u32[]{:S(2)}) %copy-start) | copy-done | bytes 131096
  83.9 1.7 %settle.1 = (f32[6,32,256]{2,1,0:T(8,128)}, f32[32,256]{1,0:T(8,128)}) custom-call(s32[8,128]{1,0:T(8,128)S(1)} %copy-done.1, f32[16,8,256]{2,1,0:T(8,128)S(1)} %copy-done, f32[64,8,256]{2,1,0:T(8,128)S(1)} %all-to-all-done.2.refs_2_), custom_call_target="tpu_custom_call" | custom-call | tf_op jit(solution)/shard_map/settle/pallas_call | solution.py:74
Async XLA Ops:
  3.1 24.5 %collective-permute-start = (f32[64,8,256]{2,1,0:T(8,128)}, f32[64,8,256]{2,1,0:T(8,128)S(1)}, u32[]{:S(2)}, u32[]{:S(2)}) collective-permute-start(f32[64,8,256]{2,1,0:T(8,128)} %get-tuple-element.26), channel_id=1, source_target_pairs={{0,32},{32,64},{64,96},{96,128},{128,160},{160,192},{192,224},{224... | collective-permute-start | bytes 1572872 | tf_op jit(solution)/shard_map/ppermute | solution.py:483
  7.8 19.7 %all-to-all-start = ((f32[64,8,256]{2,1,0:T(8,128)}), f32[64,8,256]{2,1,0:T(8,128)S(1)}, u32[]{:S(2)}, u32[]{:S(2)}) async-start(f32[64,8,256]{2,1,0:T(8,128)} %get-tuple-element.28), calls=%async_computation | async-start | bytes 1048576 | tf_op jit(solution)/shard_map/all_to_all | solution.py:465
  15.9 9.3 %collective-permute-start.1 = (f32[4,8,256]{2,1,0:T(8,128)}, f32[4,8,256]{2,1,0:T(8,128)S(1)}, u32[]{:S(2)}, u32[]{:S(2)}) collective-permute-start(f32[4,8,256]{2,1,0:T(8,128)} %get-tuple-element.27), channel_id=1, source_target_pairs={{32,0},{64,32},{96,64},{128,96},{160,128},{192,160},{224,192},{256... | collective-permute-start | bytes 98312 | tf_op jit(solution)/shard_map/ppermute | solution.py:485
  25.2 2.3 %copy-start.6 = (f32[4,8,256]{2,1,0:T(8,128)}, f32[4,8,256]{2,1,0:T(8,128)S(1)}, u32[]{:S(2)}) copy-start(f32[4,8,256]{2,1,0:T(8,128)S(1)} %collective-permute-done.1.refs_6_) | copy-start | bytes 98308
  27.5 0.8 copy-start.2
  27.5 1.0 %copy-start.3 = (f32[64,8,256]{2,1,0:T(8,128)}, f32[64,8,256]{2,1,0:T(8,128)S(1)}, u32[]{:S(2)}) copy-start(f32[64,8,256]{2,1,0:T(8,128)S(1)} %collective-permute-done.refs_5_) | copy-start | bytes 1572868
  34.6 18.2 %collective-permute-start.2 = (f32[64,1,256]{2,1,0:T(1,128)}, f32[64,1,256]{2,1,0:T(1,128)S(1)}, u32[]{:S(2)}, u32[]{:S(2)}) collective-permute-start(f32[64,1,256]{2,1,0:T(1,128)} %get-tuple-element.35), channel_id=1, source_target_pairs={{0,32},{32,64},{64,96},{96,128},{128,160},{160,192},{192,224},{224... | collective-permute-start | bytes 196616 | tf_op jit(solution)/shard_map/ppermute | solution.py:520
  38.6 14.1 %all-to-all-start.1 = ((f32[64,1,256]{2,1,0:T(1,128)}), f32[64,1,256]{2,1,0:T(1,128)S(1)}, u32[]{:S(2)}, u32[]{:S(2)}) async-start(f32[64,1,256]{2,1,0:T(1,128)} %get-tuple-element.37), calls=%async_computation.1 | async-start | bytes 131072 | tf_op jit(solution)/shard_map/all_to_all | solution.py:465
  45.4 6.1 %collective-permute-start.3 = (f32[4,1,256]{2,1,0:T(1,128)}, f32[4,1,256]{2,1,0:T(1,128)S(1)}, u32[]{:S(2)}, u32[]{:S(2)}) collective-permute-start(f32[4,1,256]{2,1,0:T(1,128)} %get-tuple-element.31.refs_2_), channel_id=1, source_target_pairs={{32,0},{64,32},{96,64},{128,96},{160,128},{192,160},{224,192},{256... | collective-permute-start | bytes 12296 | tf_op jit(solution)/shard_map/ppermute | solution.py:522
  51.4 1.3 %copy-start.7 = (f32[4,1,256]{2,1,0:T(1,128)}, f32[4,1,256]{2,1,0:T(1,128)S(1)}, u32[]{:S(2)}) copy-start(f32[4,1,256]{2,1,0:T(1,128)S(1)} %collective-permute-done.3.refs_5_) | copy-start | bytes 12292
  52.7 0.6 copy-start.4
  52.7 0.6 copy-start.5
  64.4 18.6 %all-to-all-start.2 = ((f32[64,8,256]{2,1,0:T(8,128)}), f32[64,8,256]{2,1,0:T(8,128)S(1)}, u32[]{:S(2)}, u32[]{:S(2)}) async-start(f32[64,8,256]{2,1,0:T(8,128)} %get-tuple-element.43), calls=%async_computation.2 | async-start | bytes 1048576 | tf_op jit(solution)/shard_map/all_to_all | solution.py:465
  71.4 11.6 %copy-start.1 = (s32[8,128]{1,0:T(8,128)S(1)}, s32[8,128]{1,0:T(8,128)}, u32[]{:S(2)}) copy-start(s32[8,128]{1,0:T(8,128)} %get-tuple-element.32.refs_0_) | copy-start | bytes 12292
  83.0 0.9 %copy-start = (f32[16,8,256]{2,1,0:T(8,128)S(1)}, f32[16,8,256]{2,1,0:T(8,128)}, u32[]{:S(2)}) copy-start(f32[16,8,256]{2,1,0:T(8,128)} %forces_staying.1.refs_1_) | copy-start | bytes 393220

commit v7 on v6

--- a/solution.py
+++ b/solution.py
@@ -1,5 +1,3 @@
-import functools
-
 import jax
 import jax.numpy as jnp
 from jax import lax
@@ -11,6 +9,7 @@
 SLOTS = 2
 MOVERS = 16
 STEP = 8
+WIDE = 512
 JOB_ROW, JOB_CELL, JOB_COUNT, MOVING, STAYING, OUTS, PLAN = 0, 128, 256, 272, 304, 336, 512
 STIFFNESS = 2.0
 REST_DENSITY = 0.8
@@ -63,7 +62,10 @@
         in_sems, out_sems, rest = refs[0], refs[1], refs[2:]
         moves = Moves(
             [pltpu.make_async_copy(a, b, in_sems.at[i]) for i, (a, b) in enumerate(zip(sources, inner))],
-            [pltpu.make_async_copy(a, b, out_sems.at[i]) for i, (a, b) in enumerate(zip(results, targets))],
+            [
+                pltpu.make_async_copy(a, b.at[pl.ds(0, a.shape[0])], out_sems.at[i])
+                for i, (a, b) in enumerate(zip(results, targets))
+            ],
         )
         kernel(moves, *inner, *close, *results, *rest)
         moves.need(*range(n_in))
@@ -73,16 +75,16 @@
 
     return pl.pallas_call(
         body,
-        out_shape=[jax.ShapeDtypeStruct(*o) for o in outs],
+        out_shape=[jax.ShapeDtypeStruct((*o[2:], *o[0][len(o) - 2 :]), o[1]) for o in outs],
         in_specs=[HBM] * n_in + [VMEM] * n_near,
         out_specs=[HBM] * n_out,
         scratch_shapes=[pltpu.SMEM(x.shape, x.dtype) for x in ints]
         + [pltpu.VMEM(x.shape, x.dtype) for x in held[len(into) :]]
-        + [(pltpu.SMEM if len(o[0]) == 1 else pltpu.VMEM)(*o) for o in outs]
+        + [(pltpu.SMEM if len(o[0]) == 1 else pltpu.VMEM)(*o[:2]) for o in outs]
         + [pltpu.SemaphoreType.DMA((n_in,)), pltpu.SemaphoreType.DMA((n_out,))]
         + list(scratch),
         compiler_params=pltpu.CompilerParams(vmem_limit_bytes=(64 << 20) - (room << 10)),
-        name=getattr(kernel, "func", kernel).__name__,
+        name=kernel.__name__,
     )(*ints, *held, *near)
 
 
@@ -121,6 +123,7 @@
     head[...] = own[0:RIM]
     tail[...] = jnp.zeros(tail.shape, F32)
     tail[0:RIM] = own[cells - RIM : cells]
+    moves.save(0, 2, 3, 4)
     for t in range(send.shape[0] // SLOTS):
         for k in range(SLOTS):
             cell = sends[0, 0, k, t]
@@ -214,7 +217,22 @@
     moves.save(0)
 
 
-def routing(moves, owners, owners_v, after, plan, landing, seen, *, cells):
+def routing(moves, owners, owners_v, tiles, q, plan, landing, feat1, feat2_own, seen):
+    cells, _, width = feat2_own.shape
+    sub, _ = rows_and_lanes(width)
+    moves.need(2, 3)
+
+    def first(i, carry):
+        feat1[i] = first_features(tiles[i], sub)
+        return carry
+
+    def second(i, carry):
+        feat2_own[i] = second_features(tiles[RIM + i], q[i], sub)
+        return carry
+
+    lax.fori_loop(0, tiles.shape[0], first, 0, unroll=8)
+    lax.fori_loop(0, cells, second, 0, unroll=8)
+    moves.save(2, 3)
     me = lax.axis_index("dev")
     moves.need(0, 1)
     for d in range(seen.shape[0]):
@@ -251,12 +269,12 @@
 
 
 def densities(
-    moves, counts, plan, sends, tab_own, tiles_own, below, above, rest, mine, sums,
+    moves, counts, plan, sends, below, above, rest, tab_own, tiles_own, mine, sums,
     rho, q, q_head, q_tail, send_q, tab, tiles,
 ):
     cells, _, width = mine.shape
     sub, lane = rows_and_lanes(width)
-    moves.need(5, 6, 7)
+    moves.need(3, 4, 5)
     for start, count in ((0, RIM), (RIM + cells, tab.shape[0] - RIM - cells)):
 
         def source(i, carry, start=start):
@@ -336,10 +354,10 @@
         for k in range(self.near.shape[0] + 1):
             row = self.row(c, k)
             rows = slice(k * width, k * width + width)
+            first = first + contract(self.feat1[row], odd[rows], 1)
             self.make(later, k, 0, next_odd, next_even)
-            first = first + contract(self.feat1[row], odd[rows], 1)
+            second = second + contract(self.feat2[row], even[rows], 1)
             self.make(later, k, 1, next_odd, next_even)
-            second = second + contract(self.feat2[row], even[rows], 1)
         first = first[0:8] + first[8:16]
         first = jnp.where(sub < 4, first[:, :width], first[:, width:])
         second = second[:, :width] + second[:, width:]
@@ -351,14 +369,16 @@
     pairs.fill(order[start], *a)
     moves.need(*range(len(moves.ins)))
 
-    def two(t, carry):
-        for i, now, then in ((2 * t, a, b), (2 * t + 1, b, a)):
+    def some(t, carry):
+        for k in range(STEP):
+            i = STEP * t + k
+            now, then = (a, b) if k % 2 == 0 else (b, a)
             c = order[start + i]
             later = order[start + jnp.minimum(i + 1, count - 1)]
             finish(i, c, *pairs.step(c, *now, later, *then, sub))
         return carry
 
-    lax.fori_loop(0, count // 2, two, 0)
+    lax.fori_loop(0, count // STEP, some, 0)
 
 
 def advance(first, second, tile, row_q, row_rho, row_fluid, active, sub):
@@ -386,21 +406,22 @@
 
 
 def forces_moving(
-    moves, counts, near, plan, q_below, q_own, q_above, q_rest, tiles, rho, fluid, tab, mine,
-    outbox, feat1, feat2, q, moved, *buffers,
+    moves, counts, near, plan, q_below, q_own, q_above, q_rest, feat2_own, tiles, rho, fluid, tab, mine, feat1,
+    outbox, feat2, q, moved, *buffers,
 ):
+    cells = rho.shape[0]
     sub, lane = rows_and_lanes(tiles.shape[2])
-    moves.need(3, 4, 5, 6, 7)
+    moves.need(3, 5, 6, 8)
 
     def source(i, carry):
-        tile = tiles[i]
-        feat1[i] = first_features(tile, sub)
-        feat2[i] = second_features(tile, q[i], sub)
+        feat2[i] = second_features(tiles[i], q[i], sub)
         return carry
 
-    lax.fori_loop(0, tiles.shape[0], source, 0, unroll=8)
-    moves.save(1, 2)
-    moves.need(*range(12))
+    lax.fori_loop(0, RIM, source, 0, unroll=4)
+    lax.fori_loop(RIM + cells, tiles.shape[0], source, 0, unroll=8)
+    moves.need(4, 7)
+    moves.save(1)
+    moves.need(*range(14))
 
     def finish(i, c, first, second):
         row = pl.ds(c, 1)
@@ -433,7 +454,7 @@
     )
 
 
-def settle(moves, landing, stayed, inbox, state, density):
+def settle(moves, landing, stayed, inbox, state, density, _):
     cells = state.shape[1]
     me = lax.axis_index("dev")
     moves.need(0, 1)
@@ -498,7 +519,7 @@
         densities,
         4096,
         [counts, jobs, sends],
-        [tab_own, own, below, above, rest, mine, sums],
+        [below, above, rest, tab_own, own, mine, sums],
         [],
         [
             ((cells, width), F32),
@@ -510,44 +531,46 @@
             ((total, 8, width), F32),
         ],
         into=[
-            (5, RIM, cells),
-            (6, RIM, cells),
             (6, 0, RIM),
             (6, RIM + cells, RIM),
             (6, 2 * RIM + cells, SLOTS * peers),
+            (5, RIM, cells),
+            (6, RIM, cells),
         ],
     )
     q_below = lax.ppermute(q_tail, "group", up)
     q_rest = exchange(send_q)
     q_above = lax.ppermute(q_head, "group", down)
-    plan, landing = call(
-        functools.partial(routing, cells=cells),
+    plan, landing, feat1, feat2_own = call(
+        routing,
         4096,
         [owners],
-        [owners, q_head],
+        [owners, tiles, q],
         [],
-        [((PLAN,), jnp.int32), ((8, 128), jnp.int32)],
+        [
+            ((PLAN,), jnp.int32),
+            ((8, 128), jnp.int32),
+            ((total, 16, width), BF16),
+            ((cells, 32, width), BF16),
+        ],
         [pltpu.SMEM((peers,), jnp.int32)],
     )
     partners = neighbours.shape[1] + 1
     buffers = [pltpu.VMEM((partners * width, 2 * width), BF16)] * 4
-    outbox, feat1, feat2 = call(
+    outbox, feat2 = call(
         forces_moving,
         4096,
         [counts, near, plan],
-        [q_below, q, q_above, q_rest, tiles, rho, fluid, tab, mine],
+        [q_below, q, q_above, q_rest, feat2_own, tiles, rho, fluid, tab, mine, feat1],
         [],
-        [
-            ((SLOTS * peers, 8, width), F32),
-            ((total, 16, width), BF16),
-            ((total, 32, width), BF16),
-        ],
+        [((SLOTS * peers, 8, width), F32), ((total, 32, width), BF16)],
         [pltpu.VMEM((total, 1, width), F32), pltpu.VMEM((MOVERS, 8, width), F32)] + buffers,
         into=[
-            (3, 0, RIM),
-            (3, RIM, cells),
-            (3, RIM + cells, RIM),
-            (3, 2 * RIM + cells, SLOTS * peers),
+            (2, 0, RIM),
+            (2, RIM, cells),
+            (2, RIM + cells, RIM),
+            (2, 2 * RIM + cells, SLOTS * peers),
+            (1, RIM, cells),
         ],
     )
     inbox = exchange(outbox)
@@ -557,7 +580,7 @@
         [counts, near, plan],
         [tab, mine, feat1, feat2, tiles, q, rho, fluid],
         [],
-        [((cells - MOVERS, 8, width), F32)],
+        [((cells - MOVERS, 8, width), F32, WIDE)],
         buffers,
     )
     return call(
@@ -567,6 +590,8 @@
         [stayed],
         [inbox],
         [((6, cells, width), F32), ((cells, width), F32)],
+        [pltpu.VMEM((cells - MOVERS, 8, width), F32)],
+        into=[(2, 0, cells - MOVERS)],
     )
 
 

time: 86.2 us -> 84.8 us (0.984)
  the two profiles are of different devices: /device:TPU:97 before, /device:TPU:225 now
where the time goes in v7:
time: 84.8 us; the launch traced here: 84.3 us
  Pallas kernels  41.5 us (49%)
  starting transfers between devices  33.4 us (39%)
  waiting for transfers between devices  6.89 us (8%)
  local copies, waits for them, and re-layouts  1.62 us (2%)
  between operations  0.93 us (1%)
    pallas_call x7, Pallas kernels, call(): pl.pallas_call(body, out_shape=[jax.ShapeDtypeStruct((*o[2:], *o[0][len(o...  41.5 us
    all_to_all x3, starting transfers between devices, exchange(): return lax.all_to_all(x, 'dev', split_axis=0, concat_axis=0, tiled=True)  22.1 us
    all_to_all x3, waiting for transfers between devices, exchange(): return lax.all_to_all(x, 'dev', split_axis=0, concat_axis=0, tiled=True)  5.52 us
    ppermute x1, starting transfers between devices, shards(): below = lax.ppermute(tail, 'group', up)  4.76 us
    ppermute x1, starting transfers between devices, shards(): q_below = lax.ppermute(q_tail, 'group', up)  2.65 us
    ppermute x1, starting transfers between devices, shards(): above = lax.ppermute(head, 'group', down)  1.92 us
    ppermute x1, starting transfers between devices, shards(): q_above = lax.ppermute(q_head, 'group', down)  1.92 us
  transfers between devices with their start and end apart: 7, of which 4 were waited for; matrix products, arithmetic and copies ran while one was open for 0% of the time, Pallas kernels for 23%

profile of v7, /device:TPU:225, one launch (start us, length us, event | category | flops | bytes accessed | tf_op | source)
XLA Modules:
  0.0 84.3 jit_solution(6902653669607467291)
XLA Ops:
  0.6 2.4 %prepare.1 = (f32[32,8,256]{2,1,0:T(8,128)}, f32[64,8,256]{2,1,0:T(8,128)}, f32[4,8,256]{2,1,0:T(8,128)}, f32[64,8,256]{2,1,0:T(8,128)}, f32[32,256]{1,0:T(8,128)}) custom-call(s32[32]{0:T(128)} %refs_0_.9, s32[1,1,2,32]{3,2,1,0:T(2,128)} %bitcast.5, f32[3,32,256]{2,1,0:T(8,128)} %refs_2_.1, f32[3,32,256]{2,1,0:T(8,128)} %refs_3_.1, f32[32,256]{1,0:T(8,128)} %refs_4_.1, ...), custom_call_target="tpu_custom_call" | custom-call | tf_op jit(solution)/shard_map/prepare/pallas_call | solution.py:76
  3.0 4.8 %collective-permute-start = (f32[64,8,256]{2,1,0:T(8,128)}, f32[64,8,256]{2,1,0:T(8,128)S(1)}, u32[]{:S(2)}, u32[]{:S(2)}) collective-permute-start(f32[64,8,256]{2,1,0:T(8,128)} %get-tuple-element.26), channel_id=1, source_target_pairs={{0,32},{32,64},{64,96},{96,128},{128,160},{160,192},{192,224},{224... | collective-permute-start | bytes 1572872 | tf_op jit(solution)/shard_map/ppermute | solution.py:504
  7.8 8.1 %all-to-all-start = ((f32[64,8,256]{2,1,0:T(8,128)}), f32[64,8,256]{2,1,0:T(8,128)S(1)}, u32[]{:S(2)}, u32[]{:S(2)}) async-start(f32[64,8,256]{2,1,0:T(8,128)} %get-tuple-element.28), calls=%async_computation | async-start | bytes 1048576 | tf_op jit(solution)/shard_map/all_to_all | solution.py:486
  15.8 1.9 %collective-permute-start.1 = (f32[4,8,256]{2,1,0:T(8,128)}, f32[4,8,256]{2,1,0:T(8,128)S(1)}, u32[]{:S(2)}, u32[]{:S(2)}) collective-permute-start(f32[4,8,256]{2,1,0:T(8,128)} %get-tuple-element.27), channel_id=1, source_target_pairs={{32,0},{64,32},{96,64},{128,96},{160,128},{192,160},{224,192},{256... | collective-permute-start | bytes 98312 | tf_op jit(solution)/shard_map/ppermute | solution.py:506
  17.8 6.9 %home.1 = (f32[33,8,256]{2,1,0:T(8,128)}, bf16[32,48,256]{2,1,0:T(8,128)(2,1)}, bf16[32,48,256]{2,1,0:T(8,128)(2,1)}, s32[512]{0:T(512)}) custom-call(s32[3,32]{1,0:T(4,128)} %bitcast.2, f32[32,8,256]{2,1,0:T(8,128)} %get-tuple-element.24.refs_1_.refs_7_), custom_call_target="tpu_custom_call" | custom-call | tf_op jit(solution)/shard_map/home/pallas_call | solution.py:76
  24.7 0.0 collective-permute-done.1.refs_4_
  24.7 0.0 copy-start.5
  24.7 2.8 %all-to-all-done.refs_5_ = f32[64,8,256]{2,1,0:T(8,128)S(1)} async-done(((f32[64,8,256]{2,1,0:T(8,128)}), f32[64,8,256]{2,1,0:T(8,128)S(1)}, u32[]{:S(2)}, u32[]{:S(2)}) %all-to-all-start) | async-done | bytes 524320 | tf_op jit(solution)/shard_map/all_to_all | solution.py:486
  27.5 0.0 copy-start.1
  27.5 0.0 collective-permute-done.refs_3_
  27.5 0.0 copy-start.2
  27.5 0.0 copy-done.5
  27.5 0.8 copy-done.1
  28.3 0.2 copy-done.2
  28.4 6.7 %densities.1 = (f32[32,256]{1,0:T(8,128)}, f32[32,1,256]{2,1,0:T(1,128)}, f32[4,1,256]{2,1,0:T(1,128)}, f32[64,1,256]{2,1,0:T(1,128)}, f32[64,1,256]{2,1,0:T(1,1...) custom-call(s32[32]{0:T(128)} %refs_0_.9, s32[512]{0:T(512)} %get-tuple-element.25.refs_1_, ...), custom_call_target="tpu_custom_call" | custom-call | tf_op jit(solution)/shard_map/densities/pallas_call | solution.py:76
  35.2 2.6 %collective-permute-start.2 = (f32[64,1,256]{2,1,0:T(1,128)}, f32[64,1,256]{2,1,0:T(1,128)S(1)}, u32[]{:S(2)}, u32[]{:S(2)}) collective-permute-start(f32[64,1,256]{2,1,0:T(1,128)} %get-tuple-element.38), channel_id=1, source_target_pairs={{0,32},{32,64},{64,96},{96,128},{128,160},{160,192},{192,224},{224... | collective-permute-start | bytes 196616 | tf_op jit(solution)/shard_map/ppermute | solution.py:541
  37.8 7.1 %all-to-all-start.1 = ((f32[64,1,256]{2,1,0:T(1,128)}), f32[64,1,256]{2,1,0:T(1,128)S(1)}, u32[]{:S(2)}, u32[]{:S(2)}) async-start(f32[64,1,256]{2,1,0:T(1,128)} %get-tuple-element.40), calls=%async_computation.1 | async-start | bytes 131072 | tf_op jit(solution)/shard_map/all_to_all | solution.py:486
  45.0 1.9 %collective-permute-start.3 = (f32[4,1,256]{2,1,0:T(1,128)}, f32[4,1,256]{2,1,0:T(1,128)S(1)}, u32[]{:S(2)}, u32[]{:S(2)}) collective-permute-start(f32[4,1,256]{2,1,0:T(1,128)} %get-tuple-element.39), channel_id=1, source_target_pairs={{32,0},{64,32},{96,64},{128,96},{160,128},{192,160},{224,192},{256... | collective-permute-start | bytes 12296 | tf_op jit(solution)/shard_map/ppermute | solution.py:543
  46.9 2.8 %routing.1 = (s32[512]{0:T(512)}, s32[8,128]{1,0:T(8,128)}, bf16[104,16,256]{2,1,0:T(8,128)(2,1)}, bf16[32,32,256]{2,1,0:T(8,128)(2,1)}) custom-call(s32[1,1024]{1,0:T(1,128)} %refs_1_.1, s32[1,1024]{1,0:T(1,128)} %refs_1_.1, f32[104,8,256]{2,1,0:T(8,128)} %get-tuple-element.32.refs_2_.refs_8_.refs_7_, f32[32,1,256]{2,1,0:T(1,128)} %get-tuple-element.33.refs_3_.refs_4_.refs_8_), custom_call_target="tpu_custom_call" | custom-call | tf_op jit(solution)/shard_map/routing/pallas_call | solution.py:76
  49.7 1.4 %collective-permute-done.3.refs_5_ = f32[4,1,256]{2,1,0:T(1,128)S(1)} collective-permute-done((f32[4,1,256]{2,1,0:T(1,128)}, f32[4,1,256]{2,1,0:T(1,128)S(1)}, u32[]{:S(2)}, u32[]{:S(2)}) %collective-permute-start.3) | collective-permute-done | bytes 4128 | tf_op jit(solution)/shard_map/ppermute | solution.py:543
  51.0 0.0 copy-start.6
  51.0 1.3 %all-to-all-done.1.refs_6_ = f32[64,1,256]{2,1,0:T(1,128)S(1)} async-done(((f32[64,1,256]{2,1,0:T(1,128)}), f32[64,1,256]{2,1,0:T(1,128)S(1)}, u32[]{:S(2)}, u32[]{:S(2)}) %all-to-all-start.1) | async-done | bytes 65568 | tf_op jit(solution)/shard_map/all_to_all | solution.py:486
  52.3 0.0 copy-start.3
  52.3 0.0 collective-permute-done.2.refs_3_
  52.3 0.0 copy-start.4
  52.3 0.0 copy-done.6
  52.3 0.6 copy-done.3
  52.9 0.0 copy-done.4
  53.0 10.6 %forces_moving.1 = (f32[64,8,256]{2,1,0:T(8,128)}, bf16[104,32,256]{2,1,0:T(8,128)(2,1)}) custom-call(s32[32]{0:T(128)} %refs_0_.9, s32[3,32]{1,0:T(4,128)} %bitcast.3, s32[512]{0:T(512)} %get-tuple-element.35.refs_2_, f32[64,1,256]{2,1,0:T(1,128)} %copy-done.4, f32[32,1,256]{2,1,0:T(1,128)} %get-tuple-element.33.refs_3_.refs_4_.refs_8_, ...), custom_call_target="tpu_custom_call" | custom-call | tf_op jit(solution)/shard_map/forces_moving/pallas_call | solution.py:76
  63.6 7.0 %all-to-all-start.2 = ((f32[64,8,256]{2,1,0:T(8,128)}), f32[64,8,256]{2,1,0:T(8,128)S(1)}, u32[]{:S(2)}, u32[]{:S(2)}) async-start(f32[64,8,256]{2,1,0:T(8,128)} %get-tuple-element.45), calls=%async_computation.2 | async-start | bytes 1048576 | tf_op jit(solution)/shard_map/all_to_all | solution.py:486
  70.5 0.0 copy-start
  70.5 10.1 %forces_staying.1.refs_1_ = f32[512,8,256]{2,1,0:T(8,128)} custom-call(s32[32]{0:T(128)} %refs_0_.9, s32[3,32]{1,0:T(4,128)} %bitcast.4, s32[512]{0:T(512)} %get-tuple-element.35.refs_2_, bf16[104,48,256]{2,1,0:T(8,128)(2,1)} %get-tuple-element.36.refs_11_.refs_3_, bf16[32,48,256]{2,1,0:T(8,128)(2,1)} %get-tuple-element.30.refs_8_.refs_12_.refs_4_, ...), custom_call_target="tpu_custom_call" | custom-call | tf_op jit(solution)/shard_map/forces_staying/pallas_call | solution.py:76
  80.7 1.5 %all-to-all-done.2.refs_2_ = f32[64,8,256]{2,1,0:T(8,128)S(1)} async-done(((f32[64,8,256]{2,1,0:T(8,128)}), f32[64,8,256]{2,1,0:T(8,128)S(1)}, u32[]{:S(2)}, u32[]{:S(2)}) %all-to-all-start.2) | async-done | bytes 524320 | tf_op jit(solution)/shard_map/all_to_all | solution.py:486
  82.1 0.0 copy-done
  82.1 2.0 %settle.1 = (f32[6,32,256]{2,1,0:T(8,128)}, f32[32,256]{1,0:T(8,128)}) custom-call(s32[8,128]{1,0:T(8,128)S(1)} %copy-done, f32[512,8,256]{2,1,0:T(8,128)} %forces_staying.1.refs_1_, f32[64,8,256]{2,1,0:T(8,128)S(1)} %all-to-all-done.2.refs_2_), custom_call_target="tpu_custom_call" | custom-call | tf_op jit(solution)/shard_map/settle/pallas_call | solution.py:76
Async XLA Ops:
  3.0 24.5 %collective-permute-start = (f32[64,8,256]{2,1,0:T(8,128)}, f32[64,8,256]{2,1,0:T(8,128)S(1)}, u32[]{:S(2)}, u32[]{:S(2)}) collective-permute-start(f32[64,8,256]{2,1,0:T(8,128)} %get-tuple-element.26), channel_id=1, source_target_pairs={{0,32},{32,64},{64,96},{96,128},{128,160},{160,192},{192,224},{224... | collective-permute-start | bytes 1572872 | tf_op jit(solution)/shard_map/ppermute | solution.py:504
  7.8 19.7 %all-to-all-start = ((f32[64,8,256]{2,1,0:T(8,128)}), f32[64,8,256]{2,1,0:T(8,128)S(1)}, u32[]{:S(2)}, u32[]{:S(2)}) async-start(f32[64,8,256]{2,1,0:T(8,128)} %get-tuple-element.28), calls=%async_computation | async-start | bytes 1048576 | tf_op jit(solution)/shard_map/all_to_all | solution.py:486
  15.8 8.8 %collective-permute-start.1 = (f32[4,8,256]{2,1,0:T(8,128)}, f32[4,8,256]{2,1,0:T(8,128)S(1)}, u32[]{:S(2)}, u32[]{:S(2)}) collective-permute-start(f32[4,8,256]{2,1,0:T(8,128)} %get-tuple-element.27), channel_id=1, source_target_pairs={{32,0},{64,32},{96,64},{128,96},{160,128},{192,160},{224,192},{256... | collective-permute-start | bytes 98312 | tf_op jit(solution)/shard_map/ppermute | solution.py:506
  24.7 2.8 %copy-start.5 = (f32[4,8,256]{2,1,0:T(8,128)}, f32[4,8,256]{2,1,0:T(8,128)S(1)}, u32[]{:S(2)}) copy-start(f32[4,8,256]{2,1,0:T(8,128)S(1)} %collective-permute-done.1.refs_4_) | copy-start | bytes 98308
  27.5 0.8 copy-start.1
  27.5 1.0 %copy-start.2 = (f32[64,8,256]{2,1,0:T(8,128)}, f32[64,8,256]{2,1,0:T(8,128)S(1)}, u32[]{:S(2)}) copy-start(f32[64,8,256]{2,1,0:T(8,128)S(1)} %collective-permute-done.refs_3_) | copy-start | bytes 1572868
  35.2 17.1 %collective-permute-start.2 = (f32[64,1,256]{2,1,0:T(1,128)}, f32[64,1,256]{2,1,0:T(1,128)S(1)}, u32[]{:S(2)}, u32[]{:S(2)}) collective-permute-start(f32[64,1,256]{2,1,0:T(1,128)} %get-tuple-element.38), channel_id=1, source_target_pairs={{0,32},{32,64},{64,96},{96,128},{128,160},{160,192},{192,224},{224... | collective-permute-start | bytes 196616 | tf_op jit(solution)/shard_map/ppermute | solution.py:541
  37.8 14.5 %all-to-all-start.1 = ((f32[64,1,256]{2,1,0:T(1,128)}), f32[64,1,256]{2,1,0:T(1,128)S(1)}, u32[]{:S(2)}, u32[]{:S(2)}) async-start(f32[64,1,256]{2,1,0:T(1,128)} %get-tuple-element.40), calls=%async_computation.1 | async-start | bytes 131072 | tf_op jit(solution)/shard_map/all_to_all | solution.py:486
  45.0 6.1 %collective-permute-start.3 = (f32[4,1,256]{2,1,0:T(1,128)}, f32[4,1,256]{2,1,0:T(1,128)S(1)}, u32[]{:S(2)}, u32[]{:S(2)}) collective-permute-start(f32[4,1,256]{2,1,0:T(1,128)} %get-tuple-element.39), channel_id=1, source_target_pairs={{32,0},{64,32},{96,64},{128,96},{160,128},{192,160},{224,192},{256... | collective-permute-start | bytes 12296 | tf_op jit(solution)/shard_map/ppermute | solution.py:543
  51.0 1.3 %copy-start.6 = (f32[4,1,256]{2,1,0:T(1,128)}, f32[4,1,256]{2,1,0:T(1,128)S(1)}, u32[]{:S(2)}) copy-start(f32[4,1,256]{2,1,0:T(1,128)S(1)} %collective-permute-done.3.refs_5_) | copy-start | bytes 12292
  52.3 0.6 copy-start.3
  52.3 0.6 copy-start.4
  63.6 18.6 %all-to-all-start.2 = ((f32[64,8,256]{2,1,0:T(8,128)}), f32[64,8,256]{2,1,0:T(8,128)S(1)}, u32[]{:S(2)}, u32[]{:S(2)}) async-start(f32[64,8,256]{2,1,0:T(8,128)} %get-tuple-element.45), calls=%async_computation.2 | async-start | bytes 1048576 | tf_op jit(solution)/shard_map/all_to_all | solution.py:486
  70.5 11.6 %copy-start = (s32[8,128]{1,0:T(8,128)S(1)}, s32[8,128]{1,0:T(8,128)}, u32[]{:S(2)}) copy-start(s32[8,128]{1,0:T(8,128)} %get-tuple-element.34.refs_0_) | copy-start | bytes 12292

commit v8 on v7

--- a/solution.py
+++ b/solution.py
@@ -121,8 +121,7 @@
         own[c, 7:8, :] = jnp.where(active, bond[row], 0.0)
         fluid[row, :] = jnp.where(active, free[row], 0.0)
     head[...] = own[0:RIM]
-    tail[...] = jnp.zeros(tail.shape, F32)
-    tail[0:RIM] = own[cells - RIM : cells]
+    tail[...] = own[cells - RIM : cells]
     moves.save(0, 2, 3, 4)
     for t in range(send.shape[0] // SLOTS):
         for k in range(SLOTS):
@@ -185,28 +184,28 @@
         mine[i] = target_rows(tiles[i], sub)
         return carry
 
-    lax.fori_loop(0, cells, build, 0, unroll=4)
+    lax.fori_loop(0, cells, build, 0, unroll=8)
     moves.save(1, 2)
 
+    sums[cells] = jnp.zeros((8, width), F32)
+
     def alone(t, carry):
+        local, away = carry
         for k in range(STEP):
             c = t * STEP + k
             sums[c] = cubes(tab[c], mine[c])
-        return carry
-
-    lax.fori_loop(0, cells // STEP, alone, 0)
-    sums[cells] = jnp.zeros((8, width), F32)
-    local, away = jnp.int32(0), jnp.int32(0)
-    for k in range(near.shape[0]):
-        for c in range(cells):
-            row = near[k, c]
-            inside = (row >= RIM) & (row < RIM + cells)
-            jobs[local] = row
-            jobs[128 + local] = c
-            plan[JOB_ROW + away] = row
-            plan[JOB_CELL + away] = c
-            local = local + inside.astype(jnp.int32)
-            away = away + 1 - inside.astype(jnp.int32)
+            for n in range(near.shape[0]):
+                row = near[n, c]
+                inside = (row >= RIM) & (row < RIM + cells)
+                jobs[local] = row
+                jobs[128 + local] = c
+                plan[JOB_ROW + away] = row
+                plan[JOB_CELL + away] = c
+                local = local + inside.astype(jnp.int32)
+                away = away + 1 - inside.astype(jnp.int32)
+        return local, away
+
+    local, away = lax.fori_loop(0, cells // STEP, alone, (jnp.int32(0), jnp.int32(0)))
     for k in range(STEP):
         jobs[local + k] = RIM
         jobs[128 + local + k] = cells
@@ -497,12 +496,12 @@
             ((cells, 8, width), F32),
             ((SLOTS * peers, 8, width), F32),
             ((RIM, 8, width), F32),
-            ((SLOTS * peers, 8, width), F32),
+            ((RIM, 8, width), F32),
             ((cells, width), F32),
         ],
     )
+    rest = exchange(send)
     below = lax.ppermute(tail, "group", up)
-    rest = exchange(send)
     above = lax.ppermute(head, "group", down)
     row_type, small = ((RIM, 1, width), F32), ((SLOTS * peers, 1, width), F32)
     pair_type, own_type = ((total, 48, width), BF16), ((cells, 48, width), BF16)

time: 84.8 us -> 84 us (level)
  the two profiles are of different devices: /device:TPU:225 before, /device:TPU:97 now
where the time goes in v8:
time: 84 us; the launch traced here: 83.5 us
  Pallas kernels  40.5 us (48%)
  starting transfers between devices  36.6 us (44%)
  waiting for transfers between devices  4.14 us (5%)
  local copies, waits for them, and re-layouts  1.43 us (2%)
    pallas_call x7, Pallas kernels, call(): pl.pallas_call(body, out_shape=[jax.ShapeDtypeStruct((*o[2:], *o[0][len(o...  40.5 us
    all_to_all x3, starting transfers between devices, exchange(): return lax.all_to_all(x, 'dev', split_axis=0, concat_axis=0, tiled=True)  23 us
    ppermute x1, starting transfers between devices, shards(): q_below = lax.ppermute(q_tail, 'group', up)  5.06 us
    ppermute x1, starting transfers between devices, shards(): below = lax.ppermute(tail, 'group', up)  4.76 us
    all_to_all x3, waiting for transfers between devices, exchange(): return lax.all_to_all(x, 'dev', split_axis=0, concat_axis=0, tiled=True)  2.77 us
    ppermute x1, starting transfers between devices, shards(): above = lax.ppermute(head, 'group', down)  1.92 us
    ppermute x1, starting transfers between devices, shards(): q_above = lax.ppermute(q_head, 'group', down)  1.92 us
  transfers between devices with their start and end apart: 7, of which 3 were waited for; matrix products, arithmetic and copies ran while one was open for 0% of the time, Pallas kernels for 24%

profile of v8, /device:TPU:97, one launch (start us, length us, event | category | flops | bytes accessed | tf_op | source)
XLA Modules:
  0.0 83.5 jit_solution(6969344171435737152)
XLA Ops:
  0.6 2.2 %prepare.1 = (f32[32,8,256]{2,1,0:T(8,128)}, f32[64,8,256]{2,1,0:T(8,128)}, f32[4,8,256]{2,1,0:T(8,128)}, f32[4,8,256]{2,1,0:T(8,128)}, f32[32,256]{1,0:T(8,128)}) custom-call(s32[32]{0:T(128)} %refs_0_.9, s32[1,1,2,32]{3,2,1,0:T(2,128)} %bitcast.5, f32[3,32,256]{2,1,0:T(8,128)} %refs_2_.1, f32[3,32,256]{2,1,0:T(8,128)} %refs_3_.1, f32[32,256]{1,0:T(8,128)} %refs_4_.1, ...), custom_call_target="tpu_custom_call" | custom-call | tf_op jit(solution)/shard_map/prepare/pallas_call | solution.py:76
  2.8 7.8 %all-to-all-start = ((f32[64,8,256]{2,1,0:T(8,128)}), f32[64,8,256]{2,1,0:T(8,128)S(1)}, u32[]{:S(2)}, u32[]{:S(2)}) async-start(f32[64,8,256]{2,1,0:T(8,128)} %get-tuple-element.28), calls=%async_computation | async-start | bytes 1048576 | tf_op jit(solution)/shard_map/all_to_all | solution.py:485
  10.6 4.8 %collective-permute-start = (f32[4,8,256]{2,1,0:T(8,128)}, f32[4,8,256]{2,1,0:T(8,128)S(1)}, u32[]{:S(2)}, u32[]{:S(2)}) collective-permute-start(f32[4,8,256]{2,1,0:T(8,128)} %get-tuple-element.26), channel_id=1, source_target_pairs={{0,32},{32,64},{64,96},{96,128},{128,160},{160,192},{192,224},{224... | collective-permute-start | bytes 98312 | tf_op jit(solution)/shard_map/ppermute | solution.py:504
  15.3 1.9 %collective-permute-start.1 = (f32[4,8,256]{2,1,0:T(8,128)}, f32[4,8,256]{2,1,0:T(8,128)S(1)}, u32[]{:S(2)}, u32[]{:S(2)}) collective-permute-start(f32[4,8,256]{2,1,0:T(8,128)} %get-tuple-element.27), channel_id=1, source_target_pairs={{32,0},{64,32},{96,64},{128,96},{160,128},{192,160},{224,192},{256... | collective-permute-start | bytes 98312 | tf_op jit(solution)/shard_map/ppermute | solution.py:505
  17.3 7.1 %home.1 = (f32[33,8,256]{2,1,0:T(8,128)}, bf16[32,48,256]{2,1,0:T(8,128)(2,1)}, bf16[32,48,256]{2,1,0:T(8,128)(2,1)}, s32[512]{0:T(512)}) custom-call(s32[3,32]{1,0:T(4,128)} %bitcast.2, f32[32,8,256]{2,1,0:T(8,128)} %get-tuple-element.24.refs_1_.refs_7_), custom_call_target="tpu_custom_call" | custom-call | tf_op jit(solution)/shard_map/home/pallas_call | solution.py:76
  24.4 0.0 collective-permute-done.refs_3_
  24.4 0.0 copy-start.4
  24.4 0.0 collective-permute-done.1.refs_4_
  24.4 0.0 copy-start.5
  24.4 0.0 all-to-all-done.refs_5_
  24.4 0.0 copy-start.1
  24.4 0.6 copy-done.4
  25.0 0.0 copy-done.5
  25.0 0.2 copy-done.1
  25.2 5.8 %densities.1 = (f32[32,256]{1,0:T(8,128)}, f32[32,1,256]{2,1,0:T(1,128)}, f32[4,1,256]{2,1,0:T(1,128)}, f32[64,1,256]{2,1,0:T(1,128)}, f32[64,1,256]{2,1,0:T(1,1...) custom-call(s32[32]{0:T(128)} %refs_0_.9, s32[512]{0:T(512)} %get-tuple-element.25.refs_1_, ...), custom_call_target="tpu_custom_call" | custom-call | tf_op jit(solution)/shard_map/densities/pallas_call | solution.py:76
  31.0 5.1 %collective-permute-start.2 = (f32[64,1,256]{2,1,0:T(1,128)}, f32[64,1,256]{2,1,0:T(1,128)S(1)}, u32[]{:S(2)}, u32[]{:S(2)}) collective-permute-start(f32[64,1,256]{2,1,0:T(1,128)} %get-tuple-element.38), channel_id=1, source_target_pairs={{0,32},{32,64},{64,96},{96,128},{128,160},{160,192},{192,224},{224... | collective-permute-start | bytes 196616 | tf_op jit(solution)/shard_map/ppermute | solution.py:540
  36.1 8.2 %all-to-all-start.1 = ((f32[64,1,256]{2,1,0:T(1,128)}), f32[64,1,256]{2,1,0:T(1,128)S(1)}, u32[]{:S(2)}, u32[]{:S(2)}) async-start(f32[64,1,256]{2,1,0:T(1,128)} %get-tuple-element.40), calls=%async_computation.1 | async-start | bytes 131072 | tf_op jit(solution)/shard_map/all_to_all | solution.py:485
  44.3 1.9 %collective-permute-start.3 = (f32[4,1,256]{2,1,0:T(1,128)}, f32[4,1,256]{2,1,0:T(1,128)S(1)}, u32[]{:S(2)}, u32[]{:S(2)}) collective-permute-start(f32[4,1,256]{2,1,0:T(1,128)} %get-tuple-element.39), channel_id=1, source_target_pairs={{32,0},{64,32},{96,64},{128,96},{160,128},{192,160},{224,192},{256... | collective-permute-start | bytes 12296 | tf_op jit(solution)/shard_map/ppermute | solution.py:542
  46.2 2.8 %routing.1 = (s32[512]{0:T(512)}, s32[8,128]{1,0:T(8,128)}, bf16[104,16,256]{2,1,0:T(8,128)(2,1)}, bf16[32,32,256]{2,1,0:T(8,128)(2,1)}) custom-call(s32[1,1024]{1,0:T(1,128)} %refs_1_.1, s32[1,1024]{1,0:T(1,128)} %refs_1_.1, f32[104,8,256]{2,1,0:T(8,128)} %get-tuple-element.32.refs_2_.refs_8_.refs_7_, f32[32,1,256]{2,1,0:T(1,128)} %get-tuple-element.33.refs_3_.refs_4_.refs_8_), custom_call_target="tpu_custom_call" | custom-call | tf_op jit(solution)/shard_map/routing/pallas_call | solution.py:76
  49.0 1.4 %collective-permute-done.3.refs_5_ = f32[4,1,256]{2,1,0:T(1,128)S(1)} collective-permute-done((f32[4,1,256]{2,1,0:T(1,128)}, f32[4,1,256]{2,1,0:T(1,128)S(1)}, u32[]{:S(2)}, u32[]{:S(2)}) %collective-permute-start.3) | collective-permute-done | bytes 4128 | tf_op jit(solution)/shard_map/ppermute | solution.py:542
  50.4 0.0 copy-start.6
  50.4 1.3 %all-to-all-done.1.refs_6_ = f32[64,1,256]{2,1,0:T(1,128)S(1)} async-done(((f32[64,1,256]{2,1,0:T(1,128)}), f32[64,1,256]{2,1,0:T(1,128)S(1)}, u32[]{:S(2)}, u32[]{:S(2)}) %all-to-all-start.1) | async-done | bytes 65568 | tf_op jit(solution)/shard_map/all_to_all | solution.py:485
  51.7 0.0 copy-start.2
  51.7 0.0 collective-permute-done.2.refs_3_
  51.7 0.0 copy-start.3
  51.7 0.0 copy-done.6
  51.7 0.6 copy-done.2
  52.3 0.0 copy-done.3
  52.3 10.6 %forces_moving.1 = (f32[64,8,256]{2,1,0:T(8,128)}, bf16[104,32,256]{2,1,0:T(8,128)(2,1)}) custom-call(s32[32]{0:T(128)} %refs_0_.9, s32[3,32]{1,0:T(4,128)} %bitcast.3, s32[512]{0:T(512)} %get-tuple-element.35.refs_2_, f32[64,1,256]{2,1,0:T(1,128)} %copy-done.3, f32[32,1,256]{2,1,0:T(1,128)} %get-tuple-element.33.refs_3_.refs_4_.refs_8_, ...), custom_call_target="tpu_custom_call" | custom-call | tf_op jit(solution)/shard_map/forces_moving/pallas_call | solution.py:76
  62.9 7.0 %all-to-all-start.2 = ((f32[64,8,256]{2,1,0:T(8,128)}), f32[64,8,256]{2,1,0:T(8,128)S(1)}, u32[]{:S(2)}, u32[]{:S(2)}) async-start(f32[64,8,256]{2,1,0:T(8,128)} %get-tuple-element.45), calls=%async_computation.2 | async-start | bytes 1048576 | tf_op jit(solution)/shard_map/all_to_all | solution.py:485
  69.9 0.0 copy-start
  69.9 10.1 %forces_staying.1.refs_1_ = f32[512,8,256]{2,1,0:T(8,128)} custom-call(s32[32]{0:T(128)} %refs_0_.9, s32[3,32]{1,0:T(4,128)} %bitcast.4, s32[512]{0:T(512)} %get-tuple-element.35.refs_2_, bf16[104,48,256]{2,1,0:T(8,128)(2,1)} %get-tuple-element.36.refs_11_.refs_3_, bf16[32,48,256]{2,1,0:T(8,128)(2,1)} %get-tuple-element.30.refs_8_.refs_12_.refs_4_, ...), custom_call_target="tpu_custom_call" | custom-call | tf_op jit(solution)/shard_map/forces_staying/pallas_call | solution.py:76
  80.0 1.5 %all-to-all-done.2.refs_2_ = f32[64,8,256]{2,1,0:T(8,128)S(1)} async-done(((f32[64,8,256]{2,1,0:T(8,128)}), f32[64,8,256]{2,1,0:T(8,128)S(1)}, u32[]{:S(2)}, u32[]{:S(2)}) %all-to-all-start.2) | async-done | bytes 524320 | tf_op jit(solution)/shard_map/all_to_all | solution.py:485
  81.5 0.0 copy-done
  81.5 2.0 %settle.1 = (f32[6,32,256]{2,1,0:T(8,128)}, f32[32,256]{1,0:T(8,128)}) custom-call(s32[8,128]{1,0:T(8,128)S(1)} %copy-done, f32[512,8,256]{2,1,0:T(8,128)} %forces_staying.1.refs_1_, f32[64,8,256]{2,1,0:T(8,128)S(1)} %all-to-all-done.2.refs_2_), custom_call_target="tpu_custom_call" | custom-call | tf_op jit(solution)/shard_map/settle/pallas_call | solution.py:76
Async XLA Ops:
  2.8 21.6 %all-to-all-start = ((f32[64,8,256]{2,1,0:T(8,128)}), f32[64,8,256]{2,1,0:T(8,128)S(1)}, u32[]{:S(2)}, u32[]{:S(2)}) async-start(f32[64,8,256]{2,1,0:T(8,128)} %get-tuple-element.28), calls=%async_computation | async-start | bytes 1048576 | tf_op jit(solution)/shard_map/all_to_all | solution.py:485
  10.6 13.8 %collective-permute-start = (f32[4,8,256]{2,1,0:T(8,128)}, f32[4,8,256]{2,1,0:T(8,128)S(1)}, u32[]{:S(2)}, u32[]{:S(2)}) collective-permute-start(f32[4,8,256]{2,1,0:T(8,128)} %get-tuple-element.26), channel_id=1, source_target_pairs={{0,32},{32,64},{64,96},{96,128},{128,160},{160,192},{192,224},{224... | collective-permute-start | bytes 98312 | tf_op jit(solution)/shard_map/ppermute | solution.py:504
  15.3 9.1 %collective-permute-start.1 = (f32[4,8,256]{2,1,0:T(8,128)}, f32[4,8,256]{2,1,0:T(8,128)S(1)}, u32[]{:S(2)}, u32[]{:S(2)}) collective-permute-start(f32[4,8,256]{2,1,0:T(8,128)} %get-tuple-element.27), channel_id=1, source_target_pairs={{32,0},{64,32},{96,64},{128,96},{160,128},{192,160},{224,192},{256... | collective-permute-start | bytes 98312 | tf_op jit(solution)/shard_map/ppermute | solution.py:505
  24.4 0.6 copy-start.4
  24.4 0.6 copy-start.5
  24.4 0.8 copy-start.1
  31.0 20.7 %collective-permute-start.2 = (f32[64,1,256]{2,1,0:T(1,128)}, f32[64,1,256]{2,1,0:T(1,128)S(1)}, u32[]{:S(2)}, u32[]{:S(2)}) collective-permute-start(f32[64,1,256]{2,1,0:T(1,128)} %get-tuple-element.38), channel_id=1, source_target_pairs={{0,32},{32,64},{64,96},{96,128},{128,160},{160,192},{192,224},{224... | collective-permute-start | bytes 196616 | tf_op jit(solution)/shard_map/ppermute | solution.py:540
  36.1 15.6 %all-to-all-start.1 = ((f32[64,1,256]{2,1,0:T(1,128)}), f32[64,1,256]{2,1,0:T(1,128)S(1)}, u32[]{:S(2)}, u32[]{:S(2)}) async-start(f32[64,1,256]{2,1,0:T(1,128)} %get-tuple-element.40), calls=%async_computation.1 | async-start | bytes 131072 | tf_op jit(solution)/shard_map/all_to_all | solution.py:485
  44.3 6.1 %collective-permute-start.3 = (f32[4,1,256]{2,1,0:T(1,128)}, f32[4,1,256]{2,1,0:T(1,128)S(1)}, u32[]{:S(2)}, u32[]{:S(2)}) collective-permute-start(f32[4,1,256]{2,1,0:T(1,128)} %get-tuple-element.39), channel_id=1, source_target_pairs={{32,0},{64,32},{96,64},{128,96},{160,128},{192,160},{224,192},{256... | collective-permute-start | bytes 12296 | tf_op jit(solution)/shard_map/ppermute | solution.py:542
  50.4 1.3 %copy-start.6 = (f32[4,1,256]{2,1,0:T(1,128)}, f32[4,1,256]{2,1,0:T(1,128)S(1)}, u32[]{:S(2)}) copy-start(f32[4,1,256]{2,1,0:T(1,128)S(1)} %collective-permute-done.3.refs_5_) | copy-start | bytes 12292
  51.7 0.6 copy-start.2
  51.7 0.6 copy-start.3
  62.9 18.6 %all-to-all-start.2 = ((f32[64,8,256]{2,1,0:T(8,128)}), f32[64,8,256]{2,1,0:T(8,128)S(1)}, u32[]{:S(2)}, u32[]{:S(2)}) async-start(f32[64,8,256]{2,1,0:T(8,128)} %get-tuple-element.45), calls=%async_computation.2 | async-start | bytes 1048576 | tf_op jit(solution)/shard_map/all_to_all | solution.py:485
  69.9 11.6 %copy-start = (s32[8,128]{1,0:T(8,128)S(1)}, s32[8,128]{1,0:T(8,128)}, u32[]{:S(2)}) copy-start(s32[8,128]{1,0:T(8,128)} %get-tuple-element.34.refs_0_) | copy-start | bytes 12292

commit v9 on v8

--- a/solution.py
+++ b/solution.py
@@ -7,10 +7,13 @@
 
 RIM = 4
 SLOTS = 2
+PARTNERS = 4
 MOVERS = 16
 STEP = 8
 WIDE = 512
-JOB_ROW, JOB_CELL, JOB_COUNT, MOVING, STAYING, OUTS, PLAN = 0, 128, 256, 272, 304, 336, 512
+JOB_ROW, JOB_CELL, JOB_COUNT, MOVING, STAYING, OUTS = 0, 128, 256, 272, 304, 336
+COUNTS, SENDS, NEAR, PLAN = 512, 544, 640, 1024
+WIDE_ROWS, WIDE_LIST = 4096, 1 << 20
 STIFFNESS = 2.0
 REST_DENSITY = 0.8
 VISCOSITY = 0.5
@@ -46,6 +49,8 @@
 
 
 def call(kernel, room, ints, held, near, outs, scratch=(), into=()):
+    used = [h[1] if isinstance(h, tuple) else h.shape[0] for h in held]
+    held = [h[0] if isinstance(h, tuple) else h for h in held]
     n_in, n_near, n_out = len(ints) + len(held), len(near), len(outs)
 
     def body(*refs):
@@ -54,7 +59,9 @@
         targets, refs = refs[:n_out], refs[n_out:]
         inner, refs = list(refs[: n_in - len(into)]), refs[n_in - len(into) :]
         results, refs = refs[:n_out], refs[n_out:]
-        sources = list(sources)
+        sources = [r.at[pl.ds(0, PLAN)] if r.shape == (WIDE_LIST,) else r for r in sources]
+        for i, count in enumerate(used):
+            sources[len(ints) + i] = sources[len(ints) + i].at[pl.ds(0, count)]
         for i, (out, start, count) in enumerate(into):
             target = (*results, *refs[2:])[out]
             inner.insert(len(ints) + i, target.at[pl.ds(start, count)])
@@ -78,8 +85,13 @@
         out_shape=[jax.ShapeDtypeStruct((*o[2:], *o[0][len(o) - 2 :]), o[1]) for o in outs],
         in_specs=[HBM] * n_in + [VMEM] * n_near,
         out_specs=[HBM] * n_out,
-        scratch_shapes=[pltpu.SMEM(x.shape, x.dtype) for x in ints]
-        + [pltpu.VMEM(x.shape, x.dtype) for x in held[len(into) :]]
+        scratch_shapes=[
+            pltpu.SMEM((PLAN,) if x.shape == (WIDE_LIST,) else x.shape, x.dtype) for x in ints
+        ]
+        + [
+            pltpu.VMEM((n, *x.shape[1:]), x.dtype)
+            for n, x in zip(used[len(into) :], held[len(into) :])
+        ]
         + [(pltpu.SMEM if len(o[0]) == 1 else pltpu.VMEM)(*o[:2]) for o in outs]
         + [pltpu.SemaphoreType.DMA((n_in,)), pltpu.SemaphoreType.DMA((n_out,))]
         + list(scratch),
@@ -174,10 +186,10 @@
     lax.fori_loop(0, lax.div(count + (STEP - 1), STEP), some, 0)
 
 
-def home(moves, near, tiles, sums, tab, mine, plan, jobs):
+def home(moves, near, counts, sends, tiles, sums, tab, mine, plan, jobs):
     cells, _, width = tiles.shape
     sub, _ = rows_and_lanes(width)
-    moves.need(0, 1)
+    moves.need(*range(4))
 
     def build(i, carry):
         tab[i] = source_rows(tiles[i], sub)
@@ -194,6 +206,7 @@
         for k in range(STEP):
             c = t * STEP + k
             sums[c] = cubes(tab[c], mine[c])
+            plan[COUNTS + c] = counts[c]
             for n in range(near.shape[0]):
                 row = near[n, c]
                 inside = (row >= RIM) & (row < RIM + cells)
@@ -206,6 +219,9 @@
         return local, away
 
     local, away = lax.fori_loop(0, cells // STEP, alone, (jnp.int32(0), jnp.int32(0)))
+    for t in range(sends.shape[3]):
+        for k in range(SLOTS):
+            plan[SENDS + t * SLOTS + k] = jnp.maximum(sends[0, 0, k, t], 0)
     for k in range(STEP):
         jobs[local + k] = RIM
         jobs[128 + local + k] = cells
@@ -216,10 +232,10 @@
     moves.save(0)
 
 
-def routing(moves, owners, owners_v, tiles, q, plan, landing, feat1, feat2_own, seen):
+def routing(moves, owners, near, counts, owners_v, tiles, q, plan, landing, feat1, feat2_own, seen):
     cells, _, width = feat2_own.shape
     sub, _ = rows_and_lanes(width)
-    moves.need(2, 3)
+    moves.need(4, 5)
 
     def first(i, carry):
         feat1[i] = first_features(tiles[i], sub)
@@ -233,7 +249,7 @@
     lax.fori_loop(0, cells, second, 0, unroll=8)
     moves.save(2, 3)
     me = lax.axis_index("dev")
-    moves.need(0, 1)
+    moves.need(*range(4))
     for d in range(seen.shape[0]):
         seen[d] = 0
     for i in range(seen.shape[0] * SLOTS):
@@ -242,6 +258,9 @@
     for c in range(cells):
         to = owners[0, me * cells + c]
         leaves = (to != me).astype(jnp.int32)
+        plan[COUNTS + c] = counts[c]
+        for k in range(near.shape[0]):
+            plan[NEAR + k * cells + c] = near[k, c]
         plan[MOVING + moving] = c
         plan[STAYING + staying] = c
         spot = jnp.where(to != me, to * SLOTS + seen[to], seen.shape[0] * SLOTS)
@@ -268,12 +287,12 @@
 
 
 def densities(
-    moves, counts, plan, sends, below, above, rest, tab_own, tiles_own, mine, sums,
+    moves, plan, below, above, rest, tab_own, tiles_own, mine, sums,
     rho, q, q_head, q_tail, send_q, tab, tiles,
 ):
     cells, _, width = mine.shape
     sub, lane = rows_and_lanes(width)
-    moves.need(3, 4, 5)
+    moves.need(1, 2, 3)
     for start, count in ((0, RIM), (RIM + cells, tab.shape[0] - RIM - cells)):
 
         def source(i, carry, start=start):
@@ -282,14 +301,14 @@
 
         lax.fori_loop(0, count, source, 0, unroll=4)
 
-    moves.need(*range(10))
+    moves.need(*range(8))
     moves.save(5, 6)
     run_jobs(
         lambda i: plan[JOB_ROW + i], lambda i: plan[JOB_CELL + i], plan[JOB_COUNT], tab, 0, mine, sums
     )
     for c in range(cells):
         row = jnp.sum(sums[c], axis=0, keepdims=True)
-        active = lane < counts[c]
+        active = lane < plan[COUNTS + c]
         safe = jnp.where(active, row, 1.0)
         value = STIFFNESS * (row - REST_DENSITY) / (safe * safe)
         q[c] = jnp.where(active, value, 0.0)
@@ -300,8 +319,7 @@
         q_tail[r] = q[cells - RIM + r]
     for t in range(send_q.shape[0] // SLOTS):
         for k in range(SLOTS):
-            pick = jnp.maximum(sends[0, 0, k, t], 0)
-            send_q[t * SLOTS + k] = q[pick]
+            send_q[t * SLOTS + k] = q[plan[SENDS + t * SLOTS + k]]
 
 
 def first_features(tile, sub):
@@ -323,11 +341,12 @@
 
 
 class Pairs:
-    def __init__(self, near, tab, mine, feat1, feat2):
-        self.near, self.tab, self.mine, self.feat1, self.feat2 = near, tab, mine, feat1, feat2
+    def __init__(self, plan, tab, mine, feat1, feat2, partners):
+        self.plan, self.tab, self.mine, self.feat1, self.feat2 = plan, tab, mine, feat1, feat2
+        self.partners = partners
 
     def row(self, c, k):
-        return RIM + c if k == 0 else self.near[k - 1, c]
+        return RIM + c if k == 0 else self.plan[NEAR + (k - 1) * self.mine.shape[0] + c]
 
     def make(self, c, k, part, odd, even):
         width = odd.shape[1] // 2
@@ -343,14 +362,14 @@
         even[rows, width:] = (square - high.astype(F32)).astype(BF16)
 
     def fill(self, c, odd, even):
-        for k in range(self.near.shape[0] + 1):
+        for k in range(self.partners):
             self.make(c, k, 0, odd, even)
             self.make(c, k, 1, odd, even)
 
     def step(self, c, odd, even, later, next_odd, next_even, sub):
         width = odd.shape[1] // 2
         first = second = 0.0
-        for k in range(self.near.shape[0] + 1):
+        for k in range(self.partners):
             row = self.row(c, k)
             rows = slice(k * width, k * width + width)
             first = first + contract(self.feat1[row], odd[rows], 1)
@@ -405,12 +424,12 @@
 
 
 def forces_moving(
-    moves, counts, near, plan, q_below, q_own, q_above, q_rest, feat2_own, tiles, rho, fluid, tab, mine, feat1,
+    moves, plan, q_below, q_own, q_above, q_rest, feat2_own, tiles, rho, fluid, tab, mine, feat1,
     outbox, feat2, q, moved, *buffers,
 ):
     cells = rho.shape[0]
     sub, lane = rows_and_lanes(tiles.shape[2])
-    moves.need(3, 5, 6, 8)
+    moves.need(1, 3, 4, 6)
 
     def source(i, carry):
         feat2[i] = second_features(tiles[i], q[i], sub)
@@ -418,18 +437,18 @@
 
     lax.fori_loop(0, RIM, source, 0, unroll=4)
     lax.fori_loop(RIM + cells, tiles.shape[0], source, 0, unroll=8)
-    moves.need(4, 7)
+    moves.need(2, 5)
     moves.save(1)
-    moves.need(*range(14))
+    moves.need(*range(12))
 
     def finish(i, c, first, second):
         row = pl.ds(c, 1)
         moved[i] = advance(
-            first, second, tiles[RIM + c], q[RIM + c], rho[row, :], fluid[row, :], lane < counts[c], sub
+            first, second, tiles[RIM + c], q[RIM + c], rho[row, :], fluid[row, :], lane < plan[COUNTS + c], sub
         )
 
     sweep(
-        Pairs(near, tab, mine, feat1, feat2), plan, MOVING, MOVERS, buffers, finish, sub, moves
+        Pairs(plan, tab, mine, feat1, feat2, PARTNERS), plan, MOVING, MOVERS, buffers, finish, sub, moves
     )
     for t in range(outbox.shape[0] // SLOTS):
         for k in range(SLOTS):
@@ -437,19 +456,19 @@
 
 
 def forces_staying(
-    moves, counts, near, plan, tab, mine, feat1, feat2, tiles, q, rho, fluid, stayed, *buffers
+    moves, plan, tab, mine, feat1, feat2, tiles, q, rho, fluid, stayed, *buffers
 ):
     sub, lane = rows_and_lanes(tiles.shape[2])
-    moves.need(1, 2, 3, 4)
+    moves.need(0, 1, 2)
 
     def finish(i, c, first, second):
         row = pl.ds(c, 1)
         stayed[i] = advance(
-            first, second, tiles[RIM + c], q[c], rho[row, :], fluid[row, :], lane < counts[c], sub
+            first, second, tiles[RIM + c], q[c], rho[row, :], fluid[row, :], lane < plan[COUNTS + c], sub
         )
 
     sweep(
-        Pairs(near, tab, mine, feat1, feat2), plan, STAYING, stayed.shape[0], buffers, finish, sub, moves
+        Pairs(plan, tab, mine, feat1, feat2, PARTNERS), plan, STAYING, stayed.shape[0], buffers, finish, sub, moves
     )
 
 
@@ -493,36 +512,37 @@
         [positions, velocities, masses, walls],
         [],
         [
-            ((cells, 8, width), F32),
+            ((cells, 8, width), F32, WIDE),
             ((SLOTS * peers, 8, width), F32),
             ((RIM, 8, width), F32),
             ((RIM, 8, width), F32),
-            ((cells, width), F32),
+            ((cells, width), F32, WIDE_ROWS),
         ],
     )
     rest = exchange(send)
     below = lax.ppermute(tail, "group", up)
     above = lax.ppermute(head, "group", down)
     row_type, small = ((RIM, 1, width), F32), ((SLOTS * peers, 1, width), F32)
+    plan_type = ((PLAN,), jnp.int32, WIDE_LIST)
     pair_type, own_type = ((total, 48, width), BF16), ((cells, 48, width), BF16)
     sums, tab_own, mine, jobs = call(
         home,
         4096,
-        [near],
-        [own],
+        [near, counts, sends],
+        [(own, cells)],
         [],
-        [((cells + 1, 8, width), F32), own_type, own_type, ((PLAN,), jnp.int32)],
+        [((cells + 1, 8, width), F32, WIDE), own_type, own_type, plan_type],
         [pltpu.SMEM((256,), jnp.int32)],
     )
     rho, q, q_head, q_tail, send_q, tab, tiles = call(
         densities,
-        4096,
-        [counts, jobs, sends],
-        [below, above, rest, tab_own, own, mine, sums],
+        11400,
+        [jobs],
+        [below, above, rest, tab_own, (own, cells), mine, (sums, cells + 1)],
         [],
         [
-            ((cells, width), F32),
-            ((cells, 1, width), F32),
+            ((cells, width), F32, WIDE_ROWS),
+            ((cells, 1, width), F32, WIDE_ROWS),
             row_type,
             small,
             small,
@@ -543,11 +563,11 @@
     plan, landing, feat1, feat2_own = call(
         routing,
         4096,
-        [owners],
-        [owners, tiles, q],
+        [owners, near, counts],
+        [owners, tiles, (q, cells)],
         [],
         [
-            ((PLAN,), jnp.int32),
+            plan_type,
             ((8, 128), jnp.int32),
             ((total, 16, width), BF16),
             ((cells, 32, width), BF16),
@@ -558,9 +578,21 @@
     buffers = [pltpu.VMEM((partners * width, 2 * width), BF16)] * 4
     outbox, feat2 = call(
         forces_moving,
-        4096,
-        [counts, near, plan],
-        [q_below, q, q_above, q_rest, feat2_own, tiles, rho, fluid, tab, mine, feat1],
+        10700,
+        [plan],
+        [
+            q_below,
+            (q, cells),
+            q_above,
+            q_rest,
+            feat2_own,
+            tiles,
+            (rho, cells),
+            (fluid, cells),
+            tab,
+            mine,
+            feat1,
+        ],
         [],
         [((SLOTS * peers, 8, width), F32), ((total, 32, width), BF16)],
         [pltpu.VMEM((total, 1, width), F32), pltpu.VMEM((MOVERS, 8, width), F32)] + buffers,
@@ -576,8 +608,8 @@
     [stayed] = call(
         forces_staying,
         4096,
-        [counts, near, plan],
-        [tab, mine, feat1, feat2, tiles, q, rho, fluid],
+        [plan],
+        [tab, mine, feat1, feat2, tiles, (q, cells), (rho, cells), (fluid, cells)],
         [],
         [((cells - MOVERS, 8, width), F32, WIDE)],
         buffers,

time: 84 us -> 82.4 us (0.981)
  local copies, waits for them, and re-layouts: 1.43 us -> 0.01 us
    unnamed x14 -> x2, local copies, waits for them, and re-layouts: 1.43 us -> 0.01 us
  transfers between devices with their start and end apart: 7 -> 7, of which waited for: 3 -> 3; matrix products, arithmetic and copies ran while one was open for 0% -> 0% of each run, Pallas kernels for 24% -> 25%
where the time goes in v9:
time: 82.4 us; the launch traced here: 81.8 us
  Pallas kernels  41 us (50%)
  starting transfers between devices  35.9 us (44%)
  waiting for transfers between devices  4.17 us (5%)
    pallas_call x7, Pallas kernels, call(): pl.pallas_call(body, out_shape=[jax.ShapeDtypeStruct((*o[2:], *o[0][len(o...  41 us
    all_to_all x3, starting transfers between devices, exchange(): return lax.all_to_all(x, 'dev', split_axis=0, concat_axis=0, tiled=True)  22.8 us
    ppermute x1, starting transfers between devices, shards(): below = lax.ppermute(tail, 'group', up)  4.76 us
    ppermute x1, starting transfers between devices, shards(): q_below = lax.ppermute(q_tail, 'group', up)  4.56 us
    all_to_all x3, waiting for transfers between devices, exchange(): return lax.all_to_all(x, 'dev', split_axis=0, concat_axis=0, tiled=True)  3 us
    ppermute x1, starting transfers between devices, shards(): q_above = lax.ppermute(q_head, 'group', down)  1.92 us
    ppermute x1, starting transfers between devices, shards(): above = lax.ppermute(head, 'group', down)  1.92 us
  transfers between devices with their start and end apart: 7, of which 3 were waited for; matrix products, arithmetic and copies ran while one was open for 0% of the time, Pallas kernels for 25%

profile of v9, /device:TPU:97, one launch (start us, length us, event | category | flops | bytes accessed | tf_op | source)
XLA Modules:
  0.0 81.8 jit_solution(943610130247991258)
XLA Ops:
  0.6 2.2 %prepare.1 = (f32[512,8,256]{2,1,0:T(8,128)}, f32[64,8,256]{2,1,0:T(8,128)}, f32[4,8,256]{2,1,0:T(8,128)}, f32[4,8,256]{2,1,0:T(8,128)}, f32[4096,256]{1,0:T(8,128)}) custom-call(s32[32]{0:T(128)} %refs_2_.3, s32[1,1,2,32]{3,2,1,0:T(2,128)} %bitcast.4, f32[3,32,256]{2,1,0:T(8,128)} %refs_2_.2, f32[3,32,256]{2,1,0:T(8,128)} %refs_3_.2, f32[32,256]{1,0:T(8,128)} %refs_4_.1, ...), custom_call_target="tpu_custom_call" | custom-call | tf_op jit(solution)/shard_map/prepare/pallas_call | solution.py:83
  2.8 7.8 %all-to-all-start = ((f32[64,8,256]{2,1,0:T(8,128)}), f32[64,8,256]{2,1,0:T(8,128)S(1)}, u32[]{:S(2)}, u32[]{:S(2)}) async-start(f32[64,8,256]{2,1,0:T(8,128)} %get-tuple-element.28), calls=%async_computation | async-start | bytes 1048576 | tf_op jit(solution)/shard_map/all_to_all | solution.py:504
  10.6 4.8 %collective-permute-start = (f32[4,8,256]{2,1,0:T(8,128)}, f32[4,8,256]{2,1,0:T(8,128)S(1)}, u32[]{:S(2)}, u32[]{:S(2)}) collective-permute-start(f32[4,8,256]{2,1,0:T(8,128)} %get-tuple-element.26), channel_id=1, source_target_pairs={{0,32},{32,64},{64,96},{96,128},{128,160},{160,192},{192,224},{224... | collective-permute-start | bytes 98312 | tf_op jit(solution)/shard_map/ppermute | solution.py:523
  15.4 1.9 %collective-permute-start.1 = (f32[4,8,256]{2,1,0:T(8,128)}, f32[4,8,256]{2,1,0:T(8,128)S(1)}, u32[]{:S(2)}, u32[]{:S(2)}) collective-permute-start(f32[4,8,256]{2,1,0:T(8,128)} %get-tuple-element.27), channel_id=1, source_target_pairs={{32,0},{64,32},{96,64},{128,96},{160,128},{192,160},{224,192},{256... | collective-permute-start | bytes 98312 | tf_op jit(solution)/shard_map/ppermute | solution.py:524
  17.3 7.2 %home.1 = (f32[512,8,256]{2,1,0:T(8,128)}, bf16[32,48,256]{2,1,0:T(8,128)(2,1)}, bf16[32,48,256]{2,1,0:T(8,128)(2,1)}, s32[1048576]{0:T(1024)}) custom-call(s32[3,32]{1,0:T(4,128)} %bitcast.2, s32[32]{0:T(128)} %refs_2_.3, s32[1,1,2,32]{3,2,1,0:T(2,128)} %bitcast.5, f32[512,8,256]{2,1,0:T(8,128)} %get-tuple-element.24.refs_3_.refs_5_), custom_call_target="tpu_custom_call" | custom-call | tf_op jit(solution)/shard_map/home/pallas_call | solution.py:83
  24.5 0.0 collective-permute-done.refs_1_
  24.5 0.0 collective-permute-done.1.refs_2_
  24.5 0.0 all-to-all-done.refs_3_
  24.5 6.1 %densities.1 = (f32[4096,256]{1,0:T(8,128)}, f32[4096,1,256]{2,1,0:T(1,128)}, f32[4,1,256]{2,1,0:T(1,128)S(1)}, f32[64,1,256]{2,1,0:T(1,128)S(1)}, f32[64,1,256]...) custom-call(s32[1048576]{0:T(1024)} %get-tuple-element.25.refs_0_, ...), custom_call_target="tpu_custom_call" | custom-call | tf_op jit(solution)/shard_map/densities/pallas_call | solution.py:83
  30.7 4.6 %collective-permute-start.2 = (f32[64,1,256]{2,1,0:T(1,128)S(1)}, f32[64,1,256]{2,1,0:T(1,128)S(1)}, u32[]{:S(2)}, u32[]{:S(2)}) collective-permute-start(f32[64,1,256]{2,1,0:T(1,128)S(1)} %get-tuple-element.38), channel_id=1, source_target_pairs={{0,32},{32,64},{64,96},{96,128},{128,160},{160,192},{192,224},{224... | collective-permute-start | bytes 196616 | tf_op jit(solution)/shard_map/ppermute | solution.py:560
  35.2 8.2 %all-to-all-start.1 = ((f32[64,1,256]{2,1,0:T(1,128)}), f32[64,1,256]{2,1,0:T(1,128)S(1)}, u32[]{:S(2)}, u32[]{:S(2)}) async-start(f32[64,1,256]{2,1,0:T(1,128)} %get-tuple-element.40), calls=%async_computation.1 | async-start | bytes 131072 | tf_op jit(solution)/shard_map/all_to_all | solution.py:504
  43.5 1.9 %collective-permute-start.3 = (f32[4,1,256]{2,1,0:T(1,128)S(1)}, f32[4,1,256]{2,1,0:T(1,128)S(1)}, u32[]{:S(2)}, u32[]{:S(2)}) collective-permute-start(f32[4,1,256]{2,1,0:T(1,128)S(1)} %get-tuple-element.39), channel_id=1, source_target_pairs={{32,0},{64,32},{96,64},{128,96},{160,128},{192,160},{224,192},{256... | collective-permute-start | bytes 12296 | tf_op jit(solution)/shard_map/ppermute | solution.py:562
  45.4 2.8 %routing.1 = (s32[1048576]{0:T(1024)}, s32[8,128]{1,0:T(8,128)}, bf16[104,16,256]{2,1,0:T(8,128)(2,1)}, bf16[32,32,256]{2,1,0:T(8,128)(2,1)}) custom-call(s32[1,1024]{1,0:T(1,128)} %refs_3_.3, s32[3,32]{1,0:T(4,128)} %bitcast.3, s32[32]{0:T(128)} %refs_2_.3, s32[1,1024]{1,0:T(1,128)} %refs_3_.3, f32[104,8,256]{2,1,0:T(8,128)} %get-tuple-element.32.refs_4_.refs_6_.refs_5_, ...), custom_call_target="tpu_custom_call" | custom-call | tf_op jit(solution)/shard_map/routing/pallas_call | solution.py:83
  48.2 1.2 %collective-permute-done.3.refs_3_ = f32[4,1,256]{2,1,0:T(1,128)S(1)} collective-permute-done((f32[4,1,256]{2,1,0:T(1,128)S(1)}, f32[4,1,256]{2,1,0:T(1,128)S(1)}, u32[]{:S(2)}, u32[]{:S(2)}) %collective-permute-start.3) | collective-permute-done | bytes 4128 | tf_op jit(solution)/shard_map/ppermute | solution.py:562
  49.4 1.5 %all-to-all-done.1.refs_4_ = f32[64,1,256]{2,1,0:T(1,128)S(1)} async-done(((f32[64,1,256]{2,1,0:T(1,128)}), f32[64,1,256]{2,1,0:T(1,128)S(1)}, u32[]{:S(2)}, u32[]{:S(2)}) %all-to-all-start.1) | async-done | bytes 65568 | tf_op jit(solution)/shard_map/all_to_all | solution.py:504
  50.9 0.0 collective-permute-done.2.refs_1_
  50.9 10.6 %forces_moving.1 = (f32[64,8,256]{2,1,0:T(8,128)}, bf16[104,32,256]{2,1,0:T(8,128)(2,1)}) custom-call(s32[1048576]{0:T(1024)} %get-tuple-element.35.refs_0_, f32[64,1,256]{2,1,0:T(1,128)S(1)} %collective-permute-done.2.refs_1_, f32[4096,1,256]{2,1,0:T(1,128)} %get-tuple-element.33.refs_5_.refs_2_.refs_6_, f32[4,1,256]{2,1,0:T(1,128)S(1)} %collective-permute-done.3.refs_3_, ...), custom_call_target="tpu_custom_call" | custom-call | tf_op jit(solution)/shard_map/forces_moving/pallas_call | solution.py:83
  61.4 6.7 %all-to-all-start.2 = ((f32[64,8,256]{2,1,0:T(8,128)}), f32[64,8,256]{2,1,0:T(8,128)S(1)}, u32[]{:S(2)}, u32[]{:S(2)}) async-start(f32[64,8,256]{2,1,0:T(8,128)} %get-tuple-element.45), calls=%async_computation.2 | async-start | bytes 1048576 | tf_op jit(solution)/shard_map/all_to_all | solution.py:504
  68.2 0.0 copy-start
  68.2 10.1 %forces_staying.1.refs_1_ = f32[512,8,256]{2,1,0:T(8,128)} custom-call(s32[1048576]{0:T(1024)} %get-tuple-element.35.refs_0_, bf16[104,48,256]{2,1,0:T(8,128)(2,1)} %get-tuple-element.36.refs_9_.refs_1_, bf16[32,48,256]{2,1,0:T(8,128)(2,1)} %get-tuple-element.30.refs_6_.refs_10_.refs_2_, bf16[104,16,256]{2,1,0:T(8,128)(2,1)} %get-tuple-element.37.refs_11_.refs_3_, ...), custom_call_target="tpu_custom_call" | custom-call | tf_op jit(solution)/shard_map/forces_staying/pallas_call | solution.py:83
  78.3 1.5 %all-to-all-done.2.refs_2_ = f32[64,8,256]{2,1,0:T(8,128)S(1)} async-done(((f32[64,8,256]{2,1,0:T(8,128)}), f32[64,8,256]{2,1,0:T(8,128)S(1)}, u32[]{:S(2)}, u32[]{:S(2)}) %all-to-all-start.2) | async-done | bytes 524320 | tf_op jit(solution)/shard_map/all_to_all | solution.py:504
  79.8 0.0 copy-done
  79.8 2.0 %settle.1 = (f32[6,32,256]{2,1,0:T(8,128)}, f32[32,256]{1,0:T(8,128)}) custom-call(s32[8,128]{1,0:T(8,128)S(1)} %copy-done, f32[512,8,256]{2,1,0:T(8,128)} %forces_staying.1.refs_1_, f32[64,8,256]{2,1,0:T(8,128)S(1)} %all-to-all-done.2.refs_2_), custom_call_target="tpu_custom_call" | custom-call | tf_op jit(solution)/shard_map/settle/pallas_call | solution.py:83
Async XLA Ops:
  2.8 21.7 %all-to-all-start = ((f32[64,8,256]{2,1,0:T(8,128)}), f32[64,8,256]{2,1,0:T(8,128)S(1)}, u32[]{:S(2)}, u32[]{:S(2)}) async-start(f32[64,8,256]{2,1,0:T(8,128)} %get-tuple-element.28), calls=%async_computation | async-start | bytes 1048576 | tf_op jit(solution)/shard_map/all_to_all | solution.py:504
  10.6 13.9 %collective-permute-start = (f32[4,8,256]{2,1,0:T(8,128)}, f32[4,8,256]{2,1,0:T(8,128)S(1)}, u32[]{:S(2)}, u32[]{:S(2)}) collective-permute-start(f32[4,8,256]{2,1,0:T(8,128)} %get-tuple-element.26), channel_id=1, source_target_pairs={{0,32},{32,64},{64,96},{96,128},{128,160},{160,192},{192,224},{224... | collective-permute-start | bytes 98312 | tf_op jit(solution)/shard_map/ppermute | solution.py:523
  15.4 9.2 %collective-permute-start.1 = (f32[4,8,256]{2,1,0:T(8,128)}, f32[4,8,256]{2,1,0:T(8,128)S(1)}, u32[]{:S(2)}, u32[]{:S(2)}) collective-permute-start(f32[4,8,256]{2,1,0:T(8,128)} %get-tuple-element.27), channel_id=1, source_target_pairs={{32,0},{64,32},{96,64},{128,96},{160,128},{192,160},{224,192},{256... | collective-permute-start | bytes 98312 | tf_op jit(solution)/shard_map/ppermute | solution.py:524
  30.7 20.2 %collective-permute-start.2 = (f32[64,1,256]{2,1,0:T(1,128)S(1)}, f32[64,1,256]{2,1,0:T(1,128)S(1)}, u32[]{:S(2)}, u32[]{:S(2)}) collective-permute-start(f32[64,1,256]{2,1,0:T(1,128)S(1)} %get-tuple-element.38), channel_id=1, source_target_pairs={{0,32},{32,64},{64,96},{96,128},{128,160},{160,192},{192,224},{224... | collective-permute-start | bytes 196616 | tf_op jit(solution)/shard_map/ppermute | solution.py:560
  35.2 15.6 %all-to-all-start.1 = ((f32[64,1,256]{2,1,0:T(1,128)}), f32[64,1,256]{2,1,0:T(1,128)S(1)}, u32[]{:S(2)}, u32[]{:S(2)}) async-start(f32[64,1,256]{2,1,0:T(1,128)} %get-tuple-element.40), calls=%async_computation.1 | async-start | bytes 131072 | tf_op jit(solution)/shard_map/all_to_all | solution.py:504
  43.5 5.9 %collective-permute-start.3 = (f32[4,1,256]{2,1,0:T(1,128)S(1)}, f32[4,1,256]{2,1,0:T(1,128)S(1)}, u32[]{:S(2)}, u32[]{:S(2)}) collective-permute-start(f32[4,1,256]{2,1,0:T(1,128)S(1)} %get-tuple-element.39), channel_id=1, source_target_pairs={{32,0},{64,32},{96,64},{128,96},{160,128},{192,160},{224,192},{256... | collective-permute-start | bytes 12296 | tf_op jit(solution)/shard_map/ppermute | solution.py:562
  61.4 18.4 %all-to-all-start.2 = ((f32[64,8,256]{2,1,0:T(8,128)}), f32[64,8,256]{2,1,0:T(8,128)S(1)}, u32[]{:S(2)}, u32[]{:S(2)}) async-start(f32[64,8,256]{2,1,0:T(8,128)} %get-tuple-element.45), calls=%async_computation.2 | async-start | bytes 1048576 | tf_op jit(solution)/shard_map/all_to_all | solution.py:504
  68.2 11.6 %copy-start = (s32[8,128]{1,0:T(8,128)S(1)}, s32[8,128]{1,0:T(8,128)}, u32[]{:S(2)}) copy-start(s32[8,128]{1,0:T(8,128)} %get-tuple-element.34.refs_0_) | copy-start | bytes 12292

commit v10 on v9

--- a/solution.py
+++ b/solution.py
@@ -313,7 +313,6 @@
         value = STIFFNESS * (row - REST_DENSITY) / (safe * safe)
         q[c] = jnp.where(active, value, 0.0)
         rho[c : c + 1, :] = jnp.where(active, row, 0.0)
-    q_tail[...] = jnp.zeros(q_tail.shape, F32)
     for r in range(RIM):
         q_head[r] = q[r]
         q_tail[r] = q[cells - RIM + r]
@@ -544,7 +543,7 @@
             ((cells, width), F32, WIDE_ROWS),
             ((cells, 1, width), F32, WIDE_ROWS),
             row_type,
-            small,
+            row_type,
             small,
             pair_type,
             ((total, 8, width), F32),
@@ -557,8 +556,8 @@
             (6, RIM, cells),
         ],
     )
+    q_rest = exchange(send_q)
     q_below = lax.ppermute(q_tail, "group", up)
-    q_rest = exchange(send_q)
     q_above = lax.ppermute(q_head, "group", down)
     plan, landing, feat1, feat2_own = call(
         routing,

time: 82.4 us -> 82.1 us (level)
  waiting for transfers between devices: 4.17 us -> 2.35 us
  starting transfers between devices: 35.9 us -> 37.7 us
    all_to_all x3, waiting for transfers between devices: 3 us -> 1.49 us  [exchange(): return lax.all_to_all(x, 'dev', split_axis=0, concat_axis=0, tiled=True)]
    all_to_all x3, starting transfers between devices: 22.8 us -> 24.3 us  [exchange(): return lax.all_to_all(x, 'dev', split_axis=0, concat_axis=0, tiled=True)]
  transfers between devices with their start and end apart: 7 -> 7, of which waited for: 3 -> 2; matrix products, arithmetic and copies ran while one was open for 0% -> 0% of each run, Pallas kernels for 25% -> 25%
where the time goes in v10:
time: 82.1 us; the launch traced here: 81.7 us
  Pallas kernels  40.8 us (50%)
  starting transfers between devices  37.7 us (46%)
  waiting for transfers between devices  2.35 us (3%)
    pallas_call x7, Pallas kernels, call(): pl.pallas_call(body, out_shape=[jax.ShapeDtypeStruct((*o[2:], *o[0][len(o...  40.8 us
    all_to_all x3, starting transfers between devices, exchange(): return lax.all_to_all(x, 'dev', split_axis=0, concat_axis=0, tiled=True)  24.3 us
    ppermute x1, starting transfers between devices, shards(): q_below = lax.ppermute(q_tail, 'group', up)  4.86 us
    ppermute x1, starting transfers between devices, shards(): below = lax.ppermute(tail, 'group', up)  4.76 us
    ppermute x1, starting transfers between devices, shards(): q_above = lax.ppermute(q_head, 'group', down)  1.92 us
    ppermute x1, starting transfers between devices, shards(): above = lax.ppermute(head, 'group', down)  1.92 us
  transfers between devices with their start and end apart: 7, of which 2 were waited for; matrix products, arithmetic and copies ran while one was open for 0% of the time, Pallas kernels for 25%

profile of v10, /device:TPU:97, one launch (start us, length us, event | category | flops | bytes accessed | tf_op | source)
XLA Modules:
  0.0 81.7 jit_solution(18029678360285210688)
XLA Ops:
  0.6 2.2 %prepare.1 = (f32[512,8,256]{2,1,0:T(8,128)}, f32[64,8,256]{2,1,0:T(8,128)}, f32[4,8,256]{2,1,0:T(8,128)}, f32[4,8,256]{2,1,0:T(8,128)}, f32[4096,256]{1,0:T(8,128)}) custom-call(s32[32]{0:T(128)} %refs_2_.3, s32[1,1,2,32]{3,2,1,0:T(2,128)} %bitcast.4, f32[3,32,256]{2,1,0:T(8,128)} %refs_2_.2, f32[3,32,256]{2,1,0:T(8,128)} %refs_3_.2, f32[32,256]{1,0:T(8,128)} %refs_4_.1, ...), custom_call_target="tpu_custom_call" | custom-call | tf_op jit(solution)/shard_map/prepare/pallas_call | solution.py:83
  2.8 7.8 %all-to-all-start = ((f32[64,8,256]{2,1,0:T(8,128)}), f32[64,8,256]{2,1,0:T(8,128)S(1)}, u32[]{:S(2)}, u32[]{:S(2)}) async-start(f32[64,8,256]{2,1,0:T(8,128)} %get-tuple-element.28), calls=%async_computation | async-start | bytes 1048576 | tf_op jit(solution)/shard_map/all_to_all | solution.py:503
  10.6 4.8 %collective-permute-start = (f32[4,8,256]{2,1,0:T(8,128)}, f32[4,8,256]{2,1,0:T(8,128)S(1)}, u32[]{:S(2)}, u32[]{:S(2)}) collective-permute-start(f32[4,8,256]{2,1,0:T(8,128)} %get-tuple-element.26), channel_id=1, source_target_pairs={{0,32},{32,64},{64,96},{96,128},{128,160},{160,192},{192,224},{224... | collective-permute-start | bytes 98312 | tf_op jit(solution)/shard_map/ppermute | solution.py:522
  15.4 1.9 %collective-permute-start.1 = (f32[4,8,256]{2,1,0:T(8,128)}, f32[4,8,256]{2,1,0:T(8,128)S(1)}, u32[]{:S(2)}, u32[]{:S(2)}) collective-permute-start(f32[4,8,256]{2,1,0:T(8,128)} %get-tuple-element.27), channel_id=1, source_target_pairs={{32,0},{64,32},{96,64},{128,96},{160,128},{192,160},{224,192},{256... | collective-permute-start | bytes 98312 | tf_op jit(solution)/shard_map/ppermute | solution.py:523
  17.3 7.2 %home.1 = (f32[512,8,256]{2,1,0:T(8,128)}, bf16[32,48,256]{2,1,0:T(8,128)(2,1)}, bf16[32,48,256]{2,1,0:T(8,128)(2,1)}, s32[1048576]{0:T(1024)}) custom-call(s32[3,32]{1,0:T(4,128)} %bitcast.2, s32[32]{0:T(128)} %refs_2_.3, s32[1,1,2,32]{3,2,1,0:T(2,128)} %bitcast.5, f32[512,8,256]{2,1,0:T(8,128)} %get-tuple-element.24.refs_3_.refs_5_), custom_call_target="tpu_custom_call" | custom-call | tf_op jit(solution)/shard_map/home/pallas_call | solution.py:83
  24.5 0.0 collective-permute-done.refs_1_
  24.5 0.0 collective-permute-done.1.refs_2_
  24.5 0.0 all-to-all-done.refs_3_
  24.5 6.0 %densities.1 = (f32[4096,256]{1,0:T(8,128)}, f32[4096,1,256]{2,1,0:T(1,128)}, f32[4,1,256]{2,1,0:T(1,128)S(1)}, f32[4,1,256]{2,1,0:T(1,128)S(1)}, f32[64,1,256]{...) custom-call(s32[1048576]{0:T(1024)} %get-tuple-element.25.refs_0_, ...), custom_call_target="tpu_custom_call" | custom-call | tf_op jit(solution)/shard_map/densities/pallas_call | solution.py:83
  30.6 7.7 %all-to-all-start.1 = ((f32[64,1,256]{2,1,0:T(1,128)}), f32[64,1,256]{2,1,0:T(1,128)S(1)}, u32[]{:S(2)}, u32[]{:S(2)}) async-start(f32[64,1,256]{2,1,0:T(1,128)} %get-tuple-element.40), calls=%async_computation.1 | async-start | bytes 131072 | tf_op jit(solution)/shard_map/all_to_all | solution.py:503
  38.3 4.9 %collective-permute-start.2 = (f32[4,1,256]{2,1,0:T(1,128)S(1)}, f32[4,1,256]{2,1,0:T(1,128)S(1)}, u32[]{:S(2)}, u32[]{:S(2)}) collective-permute-start(f32[4,1,256]{2,1,0:T(1,128)S(1)} %get-tuple-element.38), channel_id=1, source_target_pairs={{0,32},{32,64},{64,96},{96,128},{128,160},{160,192},{192,224},{224... | collective-permute-start | bytes 12296 | tf_op jit(solution)/shard_map/ppermute | solution.py:560
  43.1 1.9 %collective-permute-start.3 = (f32[4,1,256]{2,1,0:T(1,128)S(1)}, f32[4,1,256]{2,1,0:T(1,128)S(1)}, u32[]{:S(2)}, u32[]{:S(2)}) collective-permute-start(f32[4,1,256]{2,1,0:T(1,128)S(1)} %get-tuple-element.39), channel_id=1, source_target_pairs={{32,0},{64,32},{96,64},{128,96},{160,128},{192,160},{224,192},{256... | collective-permute-start | bytes 12296 | tf_op jit(solution)/shard_map/ppermute | solution.py:561
  45.1 2.8 %routing.1 = (s32[1048576]{0:T(1024)}, s32[8,128]{1,0:T(8,128)}, bf16[104,16,256]{2,1,0:T(8,128)(2,1)}, bf16[32,32,256]{2,1,0:T(8,128)(2,1)}) custom-call(s32[1,1024]{1,0:T(1,128)} %refs_3_.3, s32[3,32]{1,0:T(4,128)} %bitcast.3, s32[32]{0:T(128)} %refs_2_.3, s32[1,1024]{1,0:T(1,128)} %refs_3_.3, f32[104,8,256]{2,1,0:T(8,128)} %get-tuple-element.32.refs_4_.refs_6_.refs_5_, ...), custom_call_target="tpu_custom_call" | custom-call | tf_op jit(solution)/shard_map/routing/pallas_call | solution.py:83
  47.8 0.0 collective-permute-done.2.refs_1_
  47.8 0.9 %collective-permute-done.3.refs_3_ = f32[4,1,256]{2,1,0:T(1,128)S(1)} collective-permute-done((f32[4,1,256]{2,1,0:T(1,128)S(1)}, f32[4,1,256]{2,1,0:T(1,128)S(1)}, u32[]{:S(2)}, u32[]{:S(2)}) %collective-permute-start.3) | collective-permute-done | bytes 4128 | tf_op jit(solution)/shard_map/ppermute | solution.py:561
  48.7 0.0 all-to-all-done.1.refs_4_
  48.7 10.5 %forces_moving.1 = (f32[64,8,256]{2,1,0:T(8,128)}, bf16[104,32,256]{2,1,0:T(8,128)(2,1)}) custom-call(s32[1048576]{0:T(1024)} %get-tuple-element.35.refs_0_, f32[4,1,256]{2,1,0:T(1,128)S(1)} %collective-permute-done.2.refs_1_, f32[4096,1,256]{2,1,0:T(1,128)} %get-tuple-element.33.refs_5_.refs_2_.refs_6_, f32[4,1,256]{2,1,0:T(1,128)S(1)} %collective-permute-done.3.refs_3_, ...), custom_call_target="tpu_custom_call" | custom-call | tf_op jit(solution)/shard_map/forces_moving/pallas_call | solution.py:83
  59.3 8.8 %all-to-all-start.2 = ((f32[64,8,256]{2,1,0:T(8,128)}), f32[64,8,256]{2,1,0:T(8,128)S(1)}, u32[]{:S(2)}, u32[]{:S(2)}) async-start(f32[64,8,256]{2,1,0:T(8,128)} %get-tuple-element.45), calls=%async_computation.2 | async-start | bytes 1048576 | tf_op jit(solution)/shard_map/all_to_all | solution.py:503
  68.1 0.0 copy-start
  68.1 10.1 %forces_staying.1.refs_1_ = f32[512,8,256]{2,1,0:T(8,128)} custom-call(s32[1048576]{0:T(1024)} %get-tuple-element.35.refs_0_, bf16[104,48,256]{2,1,0:T(8,128)(2,1)} %get-tuple-element.36.refs_9_.refs_1_, bf16[32,48,256]{2,1,0:T(8,128)(2,1)} %get-tuple-element.30.refs_6_.refs_10_.refs_2_, bf16[104,16,256]{2,1,0:T(8,128)(2,1)} %get-tuple-element.37.refs_11_.refs_3_, ...), custom_call_target="tpu_custom_call" | custom-call | tf_op jit(solution)/shard_map/forces_staying/pallas_call | solution.py:83
  78.2 1.5 %all-to-all-done.2.refs_2_ = f32[64,8,256]{2,1,0:T(8,128)S(1)} async-done(((f32[64,8,256]{2,1,0:T(8,128)}), f32[64,8,256]{2,1,0:T(8,128)S(1)}, u32[]{:S(2)}, u32[]{:S(2)}) %all-to-all-start.2) | async-done | bytes 524320 | tf_op jit(solution)/shard_map/all_to_all | solution.py:503
  79.7 0.0 copy-done
  79.7 2.0 %settle.1 = (f32[6,32,256]{2,1,0:T(8,128)}, f32[32,256]{1,0:T(8,128)}) custom-call(s32[8,128]{1,0:T(8,128)S(1)} %copy-done, f32[512,8,256]{2,1,0:T(8,128)} %forces_staying.1.refs_1_, f32[64,8,256]{2,1,0:T(8,128)S(1)} %all-to-all-done.2.refs_2_), custom_call_target="tpu_custom_call" | custom-call | tf_op jit(solution)/shard_map/settle/pallas_call | solution.py:83
Async XLA Ops:
  2.8 21.7 %all-to-all-start = ((f32[64,8,256]{2,1,0:T(8,128)}), f32[64,8,256]{2,1,0:T(8,128)S(1)}, u32[]{:S(2)}, u32[]{:S(2)}) async-start(f32[64,8,256]{2,1,0:T(8,128)} %get-tuple-element.28), calls=%async_computation | async-start | bytes 1048576 | tf_op jit(solution)/shard_map/all_to_all | solution.py:503
  10.6 13.9 %collective-permute-start = (f32[4,8,256]{2,1,0:T(8,128)}, f32[4,8,256]{2,1,0:T(8,128)S(1)}, u32[]{:S(2)}, u32[]{:S(2)}) collective-permute-start(f32[4,8,256]{2,1,0:T(8,128)} %get-tuple-element.26), channel_id=1, source_target_pairs={{0,32},{32,64},{64,96},{96,128},{128,160},{160,192},{192,224},{224... | collective-permute-start | bytes 98312 | tf_op jit(solution)/shard_map/ppermute | solution.py:522
  15.4 9.2 %collective-permute-start.1 = (f32[4,8,256]{2,1,0:T(8,128)}, f32[4,8,256]{2,1,0:T(8,128)S(1)}, u32[]{:S(2)}, u32[]{:S(2)}) collective-permute-start(f32[4,8,256]{2,1,0:T(8,128)} %get-tuple-element.27), channel_id=1, source_target_pairs={{32,0},{64,32},{96,64},{128,96},{160,128},{192,160},{224,192},{256... | collective-permute-start | bytes 98312 | tf_op jit(solution)/shard_map/ppermute | solution.py:523
  30.6 18.1 %all-to-all-start.1 = ((f32[64,1,256]{2,1,0:T(1,128)}), f32[64,1,256]{2,1,0:T(1,128)S(1)}, u32[]{:S(2)}, u32[]{:S(2)}) async-start(f32[64,1,256]{2,1,0:T(1,128)} %get-tuple-element.40), calls=%async_computation.1 | async-start | bytes 131072 | tf_op jit(solution)/shard_map/all_to_all | solution.py:503
  38.3 9.6 %collective-permute-start.2 = (f32[4,1,256]{2,1,0:T(1,128)S(1)}, f32[4,1,256]{2,1,0:T(1,128)S(1)}, u32[]{:S(2)}, u32[]{:S(2)}) collective-permute-start(f32[4,1,256]{2,1,0:T(1,128)S(1)} %get-tuple-element.38), channel_id=1, source_target_pairs={{0,32},{32,64},{64,96},{96,128},{128,160},{160,192},{192,224},{224... | collective-permute-start | bytes 12296 | tf_op jit(solution)/shard_map/ppermute | solution.py:560
  43.1 5.6 %collective-permute-start.3 = (f32[4,1,256]{2,1,0:T(1,128)S(1)}, f32[4,1,256]{2,1,0:T(1,128)S(1)}, u32[]{:S(2)}, u32[]{:S(2)}) collective-permute-start(f32[4,1,256]{2,1,0:T(1,128)S(1)} %get-tuple-element.39), channel_id=1, source_target_pairs={{32,0},{64,32},{96,64},{128,96},{160,128},{192,160},{224,192},{256... | collective-permute-start | bytes 12296 | tf_op jit(solution)/shard_map/ppermute | solution.py:561
  59.3 20.5 %all-to-all-start.2 = ((f32[64,8,256]{2,1,0:T(8,128)}), f32[64,8,256]{2,1,0:T(8,128)S(1)}, u32[]{:S(2)}, u32[]{:S(2)}) async-start(f32[64,8,256]{2,1,0:T(8,128)} %get-tuple-element.45), calls=%async_computation.2 | async-start | bytes 1048576 | tf_op jit(solution)/shard_map/all_to_all | solution.py:503
  68.1 11.6 %copy-start = (s32[8,128]{1,0:T(8,128)S(1)}, s32[8,128]{1,0:T(8,128)}, u32[]{:S(2)}) copy-start(s32[8,128]{1,0:T(8,128)} %get-tuple-element.34.refs_0_) | copy-start | bytes 12292

commit v11 on v10

--- a/solution.py
+++ b/solution.py
@@ -299,7 +299,7 @@
             tab[start + i] = source_rows(tiles[start + i], sub)
             return carry
 
-        lax.fori_loop(0, count, source, 0, unroll=4)
+        lax.fori_loop(0, count, source, 0, unroll=min(count, 17))
 
     moves.need(*range(8))
     moves.save(5, 6)

time: 82.1 us -> 82.3 us (level)
  no operation moved by 1% of the time
where the time goes in v11:
time: 82.3 us; the launch traced here: 81.7 us
  Pallas kernels  40.8 us (50%)
  starting transfers between devices  37.7 us (46%)
  waiting for transfers between devices  2.36 us (3%)
    pallas_call x7, Pallas kernels, call(): pl.pallas_call(body, out_shape=[jax.ShapeDtypeStruct((*o[2:], *o[0][len(o...  40.8 us
    all_to_all x3, starting transfers between devices, exchange(): return lax.all_to_all(x, 'dev', split_axis=0, concat_axis=0, tiled=True)  24 us
    ppermute x1, starting transfers between devices, shards(): q_below = lax.ppermute(q_tail, 'group', up)  5.1 us
    ppermute x1, starting transfers between devices, shards(): below = lax.ppermute(tail, 'group', up)  4.76 us
    ppermute x1, starting transfers between devices, shards(): q_above = lax.ppermute(q_head, 'group', down)  1.92 us
    ppermute x1, starting transfers between devices, shards(): above = lax.ppermute(head, 'group', down)  1.92 us
  transfers between devices with their start and end apart: 7, of which 2 were waited for; matrix products, arithmetic and copies ran while one was open for 0% of the time, Pallas kernels for 25%

profile of v11, /device:TPU:97, one launch (start us, length us, event | category | flops | bytes accessed | tf_op | source)
XLA Modules:
  0.0 81.7 jit_solution(3057201496334206444)
XLA Ops:
  0.6 2.2 %prepare.1 = (f32[512,8,256]{2,1,0:T(8,128)}, f32[64,8,256]{2,1,0:T(8,128)}, f32[4,8,256]{2,1,0:T(8,128)}, f32[4,8,256]{2,1,0:T(8,128)}, f32[4096,256]{1,0:T(8,128)}) custom-call(s32[32]{0:T(128)} %refs_2_.3, s32[1,1,2,32]{3,2,1,0:T(2,128)} %bitcast.4, f32[3,32,256]{2,1,0:T(8,128)} %refs_2_.2, f32[3,32,256]{2,1,0:T(8,128)} %refs_3_.2, f32[32,256]{1,0:T(8,128)} %refs_4_.1, ...), custom_call_target="tpu_custom_call" | custom-call | tf_op jit(solution)/shard_map/prepare/pallas_call | solution.py:83
  2.8 7.8 %all-to-all-start = ((f32[64,8,256]{2,1,0:T(8,128)}), f32[64,8,256]{2,1,0:T(8,128)S(1)}, u32[]{:S(2)}, u32[]{:S(2)}) async-start(f32[64,8,256]{2,1,0:T(8,128)} %get-tuple-element.28), calls=%async_computation | async-start | bytes 1048576 | tf_op jit(solution)/shard_map/all_to_all | solution.py:503
  10.6 4.8 %collective-permute-start = (f32[4,8,256]{2,1,0:T(8,128)}, f32[4,8,256]{2,1,0:T(8,128)S(1)}, u32[]{:S(2)}, u32[]{:S(2)}) collective-permute-start(f32[4,8,256]{2,1,0:T(8,128)} %get-tuple-element.26), channel_id=1, source_target_pairs={{0,32},{32,64},{64,96},{96,128},{128,160},{160,192},{192,224},{224... | collective-permute-start | bytes 98312 | tf_op jit(solution)/shard_map/ppermute | solution.py:522
  15.4 1.9 %collective-permute-start.1 = (f32[4,8,256]{2,1,0:T(8,128)}, f32[4,8,256]{2,1,0:T(8,128)S(1)}, u32[]{:S(2)}, u32[]{:S(2)}) collective-permute-start(f32[4,8,256]{2,1,0:T(8,128)} %get-tuple-element.27), channel_id=1, source_target_pairs={{32,0},{64,32},{96,64},{128,96},{160,128},{192,160},{224,192},{256... | collective-permute-start | bytes 98312 | tf_op jit(solution)/shard_map/ppermute | solution.py:523
  17.3 7.2 %home.1 = (f32[512,8,256]{2,1,0:T(8,128)}, bf16[32,48,256]{2,1,0:T(8,128)(2,1)}, bf16[32,48,256]{2,1,0:T(8,128)(2,1)}, s32[1048576]{0:T(1024)}) custom-call(s32[3,32]{1,0:T(4,128)} %bitcast.2, s32[32]{0:T(128)} %refs_2_.3, s32[1,1,2,32]{3,2,1,0:T(2,128)} %bitcast.5, f32[512,8,256]{2,1,0:T(8,128)} %get-tuple-element.24.refs_3_.refs_5_), custom_call_target="tpu_custom_call" | custom-call | tf_op jit(solution)/shard_map/home/pallas_call | solution.py:83
  24.5 0.0 collective-permute-done.refs_1_
  24.5 0.0 collective-permute-done.1.refs_2_
  24.5 0.0 all-to-all-done.refs_3_
  24.5 6.0 %densities.1 = (f32[4096,256]{1,0:T(8,128)}, f32[4096,1,256]{2,1,0:T(1,128)}, f32[4,1,256]{2,1,0:T(1,128)S(1)}, f32[4,1,256]{2,1,0:T(1,128)S(1)}, f32[64,1,256]{...) custom-call(s32[1048576]{0:T(1024)} %get-tuple-element.25.refs_0_, ...), custom_call_target="tpu_custom_call" | custom-call | tf_op jit(solution)/shard_map/densities/pallas_call | solution.py:83
  30.6 7.4 %all-to-all-start.1 = ((f32[64,1,256]{2,1,0:T(1,128)}), f32[64,1,256]{2,1,0:T(1,128)S(1)}, u32[]{:S(2)}, u32[]{:S(2)}) async-start(f32[64,1,256]{2,1,0:T(1,128)} %get-tuple-element.40), calls=%async_computation.1 | async-start | bytes 131072 | tf_op jit(solution)/shard_map/all_to_all | solution.py:503
  38.0 5.1 %collective-permute-start.2 = (f32[4,1,256]{2,1,0:T(1,128)S(1)}, f32[4,1,256]{2,1,0:T(1,128)S(1)}, u32[]{:S(2)}, u32[]{:S(2)}) collective-permute-start(f32[4,1,256]{2,1,0:T(1,128)S(1)} %get-tuple-element.38), channel_id=1, source_target_pairs={{0,32},{32,64},{64,96},{96,128},{128,160},{160,192},{192,224},{224... | collective-permute-start | bytes 12296 | tf_op jit(solution)/shard_map/ppermute | solution.py:560
  43.1 1.9 %collective-permute-start.3 = (f32[4,1,256]{2,1,0:T(1,128)S(1)}, f32[4,1,256]{2,1,0:T(1,128)S(1)}, u32[]{:S(2)}, u32[]{:S(2)}) collective-permute-start(f32[4,1,256]{2,1,0:T(1,128)S(1)} %get-tuple-element.39), channel_id=1, source_target_pairs={{32,0},{64,32},{96,64},{128,96},{160,128},{192,160},{224,192},{256... | collective-permute-start | bytes 12296 | tf_op jit(solution)/shard_map/ppermute | solution.py:561
  45.1 2.8 %routing.1 = (s32[1048576]{0:T(1024)}, s32[8,128]{1,0:T(8,128)}, bf16[104,16,256]{2,1,0:T(8,128)(2,1)}, bf16[32,32,256]{2,1,0:T(8,128)(2,1)}) custom-call(s32[1,1024]{1,0:T(1,128)} %refs_3_.3, s32[3,32]{1,0:T(4,128)} %bitcast.3, s32[32]{0:T(128)} %refs_2_.3, s32[1,1024]{1,0:T(1,128)} %refs_3_.3, f32[104,8,256]{2,1,0:T(8,128)} %get-tuple-element.32.refs_4_.refs_6_.refs_5_, ...), custom_call_target="tpu_custom_call" | custom-call | tf_op jit(solution)/shard_map/routing/pallas_call | solution.py:83
  47.8 0.0 collective-permute-done.2.refs_1_
  47.8 0.9 %collective-permute-done.3.refs_3_ = f32[4,1,256]{2,1,0:T(1,128)S(1)} collective-permute-done((f32[4,1,256]{2,1,0:T(1,128)S(1)}, f32[4,1,256]{2,1,0:T(1,128)S(1)}, u32[]{:S(2)}, u32[]{:S(2)}) %collective-permute-start.3) | collective-permute-done | bytes 4128 | tf_op jit(solution)/shard_map/ppermute | solution.py:561
  48.7 0.0 all-to-all-done.1.refs_4_
  48.7 10.5 %forces_moving.1 = (f32[64,8,256]{2,1,0:T(8,128)}, bf16[104,32,256]{2,1,0:T(8,128)(2,1)}) custom-call(s32[1048576]{0:T(1024)} %get-tuple-element.35.refs_0_, f32[4,1,256]{2,1,0:T(1,128)S(1)} %collective-permute-done.2.refs_1_, f32[4096,1,256]{2,1,0:T(1,128)} %get-tuple-element.33.refs_5_.refs_2_.refs_6_, f32[4,1,256]{2,1,0:T(1,128)S(1)} %collective-permute-done.3.refs_3_, ...), custom_call_target="tpu_custom_call" | custom-call | tf_op jit(solution)/shard_map/forces_moving/pallas_call | solution.py:83
  59.3 8.8 %all-to-all-start.2 = ((f32[64,8,256]{2,1,0:T(8,128)}), f32[64,8,256]{2,1,0:T(8,128)S(1)}, u32[]{:S(2)}, u32[]{:S(2)}) async-start(f32[64,8,256]{2,1,0:T(8,128)} %get-tuple-element.45), calls=%async_computation.2 | async-start | bytes 1048576 | tf_op jit(solution)/shard_map/all_to_all | solution.py:503
  68.1 0.0 copy-start
  68.1 10.1 %forces_staying.1.refs_1_ = f32[512,8,256]{2,1,0:T(8,128)} custom-call(s32[1048576]{0:T(1024)} %get-tuple-element.35.refs_0_, bf16[104,48,256]{2,1,0:T(8,128)(2,1)} %get-tuple-element.36.refs_9_.refs_1_, bf16[32,48,256]{2,1,0:T(8,128)(2,1)} %get-tuple-element.30.refs_6_.refs_10_.refs_2_, bf16[104,16,256]{2,1,0:T(8,128)(2,1)} %get-tuple-element.37.refs_11_.refs_3_, ...), custom_call_target="tpu_custom_call" | custom-call | tf_op jit(solution)/shard_map/forces_staying/pallas_call | solution.py:83
  78.2 1.5 %all-to-all-done.2.refs_2_ = f32[64,8,256]{2,1,0:T(8,128)S(1)} async-done(((f32[64,8,256]{2,1,0:T(8,128)}), f32[64,8,256]{2,1,0:T(8,128)S(1)}, u32[]{:S(2)}, u32[]{:S(2)}) %all-to-all-start.2) | async-done | bytes 524320 | tf_op jit(solution)/shard_map/all_to_all | solution.py:503
  79.7 0.0 copy-done
  79.7 2.0 %settle.1 = (f32[6,32,256]{2,1,0:T(8,128)}, f32[32,256]{1,0:T(8,128)}) custom-call(s32[8,128]{1,0:T(8,128)S(1)} %copy-done, f32[512,8,256]{2,1,0:T(8,128)} %forces_staying.1.refs_1_, f32[64,8,256]{2,1,0:T(8,128)S(1)} %all-to-all-done.2.refs_2_), custom_call_target="tpu_custom_call" | custom-call | tf_op jit(solution)/shard_map/settle/pallas_call | solution.py:83
Async XLA Ops:
  2.8 21.7 %all-to-all-start = ((f32[64,8,256]{2,1,0:T(8,128)}), f32[64,8,256]{2,1,0:T(8,128)S(1)}, u32[]{:S(2)}, u32[]{:S(2)}) async-start(f32[64,8,256]{2,1,0:T(8,128)} %get-tuple-element.28), calls=%async_computation | async-start | bytes 1048576 | tf_op jit(solution)/shard_map/all_to_all | solution.py:503
  10.6 13.9 %collective-permute-start = (f32[4,8,256]{2,1,0:T(8,128)}, f32[4,8,256]{2,1,0:T(8,128)S(1)}, u32[]{:S(2)}, u32[]{:S(2)}) collective-permute-start(f32[4,8,256]{2,1,0:T(8,128)} %get-tuple-element.26), channel_id=1, source_target_pairs={{0,32},{32,64},{64,96},{96,128},{128,160},{160,192},{192,224},{224... | collective-permute-start | bytes 98312 | tf_op jit(solution)/shard_map/ppermute | solution.py:522
  15.4 9.2 %collective-permute-start.1 = (f32[4,8,256]{2,1,0:T(8,128)}, f32[4,8,256]{2,1,0:T(8,128)S(1)}, u32[]{:S(2)}, u32[]{:S(2)}) collective-permute-start(f32[4,8,256]{2,1,0:T(8,128)} %get-tuple-element.27), channel_id=1, source_target_pairs={{32,0},{64,32},{96,64},{128,96},{160,128},{192,160},{224,192},{256... | collective-permute-start | bytes 98312 | tf_op jit(solution)/shard_map/ppermute | solution.py:523
  30.6 18.1 %all-to-all-start.1 = ((f32[64,1,256]{2,1,0:T(1,128)}), f32[64,1,256]{2,1,0:T(1,128)S(1)}, u32[]{:S(2)}, u32[]{:S(2)}) async-start(f32[64,1,256]{2,1,0:T(1,128)} %get-tuple-element.40), calls=%async_computation.1 | async-start | bytes 131072 | tf_op jit(solution)/shard_map/all_to_all | solution.py:503
  38.0 9.8 %collective-permute-start.2 = (f32[4,1,256]{2,1,0:T(1,128)S(1)}, f32[4,1,256]{2,1,0:T(1,128)S(1)}, u32[]{:S(2)}, u32[]{:S(2)}) collective-permute-start(f32[4,1,256]{2,1,0:T(1,128)S(1)} %get-tuple-element.38), channel_id=1, source_target_pairs={{0,32},{32,64},{64,96},{96,128},{128,160},{160,192},{192,224},{224... | collective-permute-start | bytes 12296 | tf_op jit(solution)/shard_map/ppermute | solution.py:560
  43.1 5.6 %collective-permute-start.3 = (f32[4,1,256]{2,1,0:T(1,128)S(1)}, f32[4,1,256]{2,1,0:T(1,128)S(1)}, u32[]{:S(2)}, u32[]{:S(2)}) collective-permute-start(f32[4,1,256]{2,1,0:T(1,128)S(1)} %get-tuple-element.39), channel_id=1, source_target_pairs={{32,0},{64,32},{96,64},{128,96},{160,128},{192,160},{224,192},{256... | collective-permute-start | bytes 12296 | tf_op jit(solution)/shard_map/ppermute | solution.py:561
  59.3 20.5 %all-to-all-start.2 = ((f32[64,8,256]{2,1,0:T(8,128)}), f32[64,8,256]{2,1,0:T(8,128)S(1)}, u32[]{:S(2)}, u32[]{:S(2)}) async-start(f32[64,8,256]{2,1,0:T(8,128)} %get-tuple-element.45), calls=%async_computation.2 | async-start | bytes 1048576 | tf_op jit(solution)/shard_map/all_to_all | solution.py:503
  68.1 11.6 %copy-start = (s32[8,128]{1,0:T(8,128)S(1)}, s32[8,128]{1,0:T(8,128)}, u32[]{:S(2)}) copy-start(s32[8,128]{1,0:T(8,128)} %get-tuple-element.34.refs_0_) | copy-start | bytes 12292
